TPU v7x, 512 devices: a whole 4x8x8 slice. The times are simulated.
512 devices in a mesh: ctx: 64 (over y, z), tp: 8 (over x, core).
Axes of the slice: x: 4, y: 8, z: 8, core: 2. Of those that a mesh axis runs over, the one named last changes fastest.
Arguments:
- queries: bfloat16 [32768, 4096], P('ctx', 'tp'), may hold values from -6 to 6
- key_rows: bfloat16 [32768, 4096], P('ctx', 'tp'), may hold values from -6 to 6
- value_rows: bfloat16 [32768, 4096], P('ctx', 'tp'), may hold values from -6 to 6
- log_decay: float32 [32, 32768], P('tp', 'ctx'), may hold values from -1 to 0
- doc_ids: int32 [32768], P('ctx'), may hold values from 0 to 5, never falling along the last dimension, each value on 1 to 16384 neighbouring positions
- head_gain: float32 [4096], P('tp'), may hold values from 0.1 to 1.9
- out_weight: bfloat16 [4096, 4096], P('ctx', 'tp'), may hold values from -0.09375 to 0.09375
Outputs:
- mixed: bfloat16 [32768, 4096], P('ctx', 'tp')
All inputs are finite; a program needn't handle non-finite values.
Results may differ from a plain program's by a relative error of at most 0.013.
Values may be sent and summed in bfloat16 or wider, within the bound.
No kernel may reach another device: no remote copies, remote signals or barrier semaphores. Data moves between devices by JAX's collectives and lax.ppermute only.
A program may use at most 64 MiB of HBM per device.

v0:
```python
from functools import partial

import jax
import jax.numpy as jnp
from jax import lax
from jax.sharding import PartitionSpec as P

HD = 128
BLOCK = 512


def shifted(value, axis, steps):
    count = lax.axis_size(axis)
    leading, last = (max(0, -steps), min(count, count - steps))
    return lax.ppermute(value, axis, [(source, source + steps) for source in range(leading, last)])


def entering(array, axis, combine, identity):
    length, here = (lax.axis_size(axis), lax.axis_index(axis))
    everything = jax.tree.map(lambda part: lax.all_gather(part, axis), array)
    start = jax.tree.map(
        lambda part, zero: jnp.broadcast_to(jnp.asarray(zero, part.dtype), part.shape),
        array,
        identity,
    )

    def lap(k, before):
        reached = k < here
        new = combine(before, jax.tree.map(lambda part: part[k], everything))
        return jax.tree.map(lambda a, b: jnp.where(reached, a, b), new, before)

    return lax.fori_loop(0, length, lap, start)


def carry_product(query_blk, memory):
    upper_part = memory.astype(jnp.bfloat16)
    lower_part = (memory - upper_part.astype(jnp.float32)).astype(jnp.bfloat16)
    first_term = jnp.einsum(
        "thd,hde->the", query_blk, upper_part, preferred_element_type=jnp.float32
    )
    second_term = jnp.einsum(
        "thd,hde->the", query_blk, lower_part, preferred_element_type=jnp.float32
    )
    return first_term + second_term


def mix_block(with_carry, carry_in, pieces):
    memory, prior_doc = carry_in
    query_blk, key_blk, value_blk, log_block, doc_block = pieces
    cumulative = jnp.cumsum(log_block, axis=1)
    positions = jnp.arange(doc_block.shape[0])
    causal = positions[:, None] >= positions[None, :]
    same_doc = jnp.logical_and(doc_block[:, None] == doc_block[None, :], causal)[None]
    log_gap = cumulative[:, :, None] - cumulative[:, None, :]
    decay_mask = jnp.where(same_doc, jnp.exp(jnp.where(same_doc, log_gap, 0.0)), 0.0)
    scores = jnp.einsum("thd,shd->hts", query_blk, key_blk, preferred_element_type=jnp.float32)
    weighted = (scores * decay_mask).astype(jnp.bfloat16)
    heads_out = jnp.einsum("hts,shd->thd", weighted, value_blk, preferred_element_type=jnp.float32)
    final_log = cumulative[:, -1]
    to_end = (
        jnp.exp(final_log[:, None] - cumulative)
        * (doc_block == doc_block[-1]).astype(jnp.float32)[None, :]
    )
    decayed = (key_blk * to_end.T[:, :, None]).astype(jnp.bfloat16)
    retain = jnp.exp(final_log) * jnp.all(doc_block == prior_doc).astype(jnp.float32)
    update = jnp.einsum("shd,she->hde", decayed, value_blk, preferred_element_type=jnp.float32)
    memory = retain[:, None, None] * memory + update
    return ((memory, doc_block[-1]), heads_out)


def finish(heads_out, head_gain):
    scale = lax.rsqrt(jnp.mean(heads_out * heads_out, axis=-1, keepdims=True) + 1e-06)
    flat = (heads_out * scale).reshape(heads_out.shape[0], -1)
    return (flat * head_gain[None, :]).astype(jnp.bfloat16)


def join_plain(earlier, later):
    retain_early, memory_early = earlier
    retain_late, memory_late = later
    return (retain_early * retain_late, retain_late[:, None, None] * memory_early + memory_late)


def local(queries, key_rows, value_rows, log_decay, doc_ids, head_gain, out_weight):
    row_count = queries.shape[0]
    head_count = queries.shape[1] // HD
    blocks = row_count // BLOCK

    def split(rows_in):
        return rows_in.reshape(blocks, BLOCK, head_count, HD)

    log_blocks = log_decay.reshape(head_count, blocks, BLOCK).transpose(1, 0, 2)
    doc_blocks = doc_ids.reshape(blocks, BLOCK)
    start = (jnp.zeros((head_count, HD, HD), jnp.float32), doc_ids[0])
    block_step = partial(mix_block, blocks > 1)
    (local_memory, _), local_heads = lax.scan(
        block_step,
        start,
        (split(queries), split(key_rows), split(value_rows), log_blocks, doc_blocks),
    )
    local_heads = local_heads.reshape(row_count, head_count, HD)
    cumulative = jnp.cumsum(log_decay, axis=1)
    total_decay = jnp.exp(cumulative[:, -1])
    ones_heads = jnp.ones((head_count,), jnp.float32)
    prior_doc = shifted(doc_ids[-1:], "ctx", 1)[0]
    retain = total_decay * jnp.all(doc_ids == prior_doc).astype(jnp.float32)
    identity = (ones_heads, jnp.zeros_like(local_memory))
    _, incoming = entering((retain, local_memory), "ctx", join_plain, identity)
    linked = (doc_ids == prior_doc).astype(jnp.float32)
    reach_in = jnp.exp(cumulative).T * linked[:, None]
    query_heads = queries.reshape(row_count, head_count, HD)
    carried = carry_product(query_heads, incoming)
    heads_out = local_heads + reach_in[:, :, None] * carried
    normed = finish(heads_out, head_gain)
    weight_all = lax.all_gather(out_weight, "ctx", axis=0, tiled=True)
    product = jnp.dot(
        lax.all_gather(normed, "tp", axis=1, tiled=True),
        weight_all,
        preferred_element_type=jnp.float32,
    )
    return product.astype(jnp.bfloat16)


def solution(mesh):
    return jax.shard_map(
        local,
        mesh=mesh,
        in_specs=(
            P("ctx", "tp"),
            P("ctx", "tp"),
            P("ctx", "tp"),
            P("tp", "ctx"),
            P("ctx"),
            P("tp"),
            P("ctx", "tp"),
        ),
        out_specs=P("ctx", "tp"),
        check_vma=False,
    )
```

profile of v0, /device:TPU:1, one launch (start us, length us, event | category | flops | bytes accessed | tf_op | source)
XLA Modules:
  0.0 309.8 jit_solution(3854732766042310444)
XLA Ops:
  6.5 1.4 fusion.26
  8.0 5.3 %collective-permute-start = (s32[1]{0:T(128)}, s32[1]{0:T(128)}, u32[]{:S(2)}, u32[]{:S(2)}) collective-permute-start(s32[1]{0:T(128)} %get-tuple-element.161), channel_id=1, source_target_pairs={{0,8},{8,16},{16,24},{24,32},{32,40},{40,48},{48,56},{56,64},{64,7... | collective-permute-start | bytes 20 | tf_op jit(solution)/shard_map/ppermute | solution.py:15
  14.0 1.2 reduce-window.12
  15.8 1.3 copy.37
  17.1 1.3 dynamic-slice.2
  19.0 3.2 %fusion.25 = (f32[512]{0:T(512)S(1)}, pred[512]{0:T(512)(128)(4,1)S(1)}, pred[]{:T(512)}, f32[512]{0:T(512)S(1)}) fusion(s32[512]{0:T(512)} %param.13, s32[]{:T(128)} %bitcast.1, s32[]{:T(128)} %bitcast.6, s32[]{:T(128)} %bitcast.7), kind=kLoop, calls=%fused_computation.46 | loop fusion | flops 3071 | bytes 6669 | tf_op jit(solution)/shard_map/convert_element_type | solution.py:108
  24.4 2.0 convolution_add_fusion.1
  28.2 3.1 fusion.2
  31.3 120.7 %all-reduce = f32[256]{0:T(256)S(1)} all-reduce(f32[256]{0:T(256)S(1)} %get-tuple-element.164), channel_id=2, replica_groups=mesh['ctx'=64,'tp'=8] {'ctx'}, use_global_device_ids=true, to_apply=%add | all-reduce | flops 256 | bytes 2048
  152.1 19.8 %all-gather.10.cloned.1.call-done = f32[256,128,128]{2,1,0:T(8,128)} async-done(((f32[4,128,128]{2,1,0:T(8,128)}), f32[256,128,128]{2,1,0:T(8,128)}) %all-gather.10.cloned.1.call-update) | async-done | bytes 16777232 | tf_op jit(solution)/shard_map/all_gather | solution.py:20
  171.9 70.0 %while.9 = (s32[]{:T(128)}, f32[4,128,128]{2,1,0:T(8,128)S(1)}, s32[]{:T(128)}, f32[64,4]{1,0:T(8,128)S(1)}, f32[64,4,128,128]{3,2,1,0:T(8,128)}, /*index=5*/s32[]{:T(128)}, s32[]{:T(128)}) while((s32[]{:T(128)}, f32[4,128,128]{2,1,0:T(8,128)S(1)}, s32[]{:T(128)}, f32[64,4]{1,0:T(8,128)S(1)}, f32[64,4,128,128]{3,2,1,0:T(8,128)}, ...), condition=%wide.region_5.6_spmd.clone, body=%wide.region_4.5_spmd.clone.sunk | while | flops 262148 | bytes 786585 | solution.py:32
  187.2 1.1 fusion.36
  188.3 1.1 fusion.36
  193.8 1.1 fusion.36
  200.3 1.1 fusion.36
  202.5 1.1 fusion.36
  205.8 1.1 fusion.36
  208.0 1.1 fusion.36
  226.6 1.1 fusion.36
  234.3 1.1 fusion.36
  239.8 1.1 fusion.36
  243.9 12.2 %all-gather.8.cloned.1.call-done = bf16[4096,512]{1,0:T(8,128)(2,1)} async-done(((bf16[64,512]{1,0:T(8,128)(2,1)}), bf16[4096,512]{1,0:T(8,128)(2,1)}) %all-gather.8.cloned.1.call-update) | async-done | bytes 4194320 | tf_op jit(solution)/shard_map/all_gather | solution.py:114
  256.0 40.6 %all-gather.6.cloned.1.call-done = bf16[512,4096]{0,1:T(8,128)(2,1)} async-done(((bf16[512,512]{0,1:T(8,128)(2,1)}), bf16[512,4096]{0,1:T(8,128)(2,1)}) %all-gather.6.cloned.1.call-update) | async-done | bytes 4194320 | tf_op jit(solution)/shard_map/all_gather | solution.py:116
  296.7 6.6 %convolution_convert_fusion = bf16[512,512]{1,0:T(8,128)(2,1)} fusion(bf16[512,4096]{0,1:T(8,128)(2,1)} %all-gather.6.cloned.1.call-done, bf16[4096,512]{1,0:T(8,128)(2,1)} %all-gather.8.cloned.1.call-done), kind=kOutput, calls=%fused_computation.10 | convolution fusion | flops 2147745792 | bytes 8912896 | tf_op jit(solution)/shard_map/dot_general | solution.py:115
  (148 shorter events, 63.3 us)
Async XLA Ops:
  6.5 21.7 %copy-start = (bf16[512,512]{1,0:T(8,128)(2,1)S(1)}, bf16[512,512]{1,0:T(8,128)(2,1)}, u32[]{:S(2)}) copy-start(bf16[512,512]{1,0:T(8,128)(2,1)} %param.9) | copy-start | bytes 1572868
  6.5 165.3 %all-gather.10.cloned.1.call-start = ((), (), s32[]{:S(2)}) async-start(), calls=%async_computation.2 | async-start | bytes 17039360 | tf_op jit(solution)/shard_map/all_gather | solution.py:20
  8.0 11.1 %collective-permute-start = (s32[1]{0:T(128)}, s32[1]{0:T(128)}, u32[]{:S(2)}, u32[]{:S(2)}) collective-permute-start(s32[1]{0:T(128)} %get-tuple-element.161), channel_id=1, source_target_pairs={{0,8},{8,16},{16,24},{24,32},{32,40},{40,48},{48,56},{56,64},{64,7... | collective-permute-start | bytes 20 | tf_op jit(solution)/shard_map/ppermute | solution.py:15
  26.5 229.6 %all-gather.8.cloned.1.call-start = ((), (), s32[]{:S(2)}) async-start(), calls=%async_computation.1 | async-start | bytes 4259840 | tf_op jit(solution)/shard_map/all_gather | solution.py:114
  27.2 269.5 %all-gather.6.cloned.1.call-start = ((), (), s32[]{:S(2)}) async-start(), calls=%async_computation | async-start | bytes 4718592 | tf_op jit(solution)/shard_map/all_gather | solution.py:116
  241.9 1.0 copy-start.1
Sparse Core Ops, SparseCore 0:
  26.6 145.2 all-gather.9
  174.9 81.1 all-gather.7
  258.2 38.4 all-gather.5
where the time goes:
time: 312 us; the launch traced here: 310 us
  blocking collectives  121 us (39%)
  other arithmetic  75 us (24%)
  waiting for transfers between devices  73.3 us (23%)
  between operations  15.2 us (5%)
  matrix products  12.5 us (4%)
  local copies, waits for them, and re-layouts  5.77 us (2%)
  starting transfers between devices  5.4 us (2%)
    unnamed x1, blocking collectives  121 us
    select_n x64, other arithmetic, lap(): return jax.tree.map(lambda a, b: jnp.where(reached, a, b), new, before)  67.4 us
    all_gather x1, waiting for transfers between devices, local(): lax.all_gather(normed, 'tp', axis=1, tiled=True)  40.6 us
    all_gather x1, waiting for transfers between devices, entering(): everything = jax.tree.map(lambda part: lax.all_gather(part, axis), array)  19.8 us
    all_gather x1, waiting for transfers between devices, local(): weight_all = lax.all_gather(out_weight, 'ctx', axis=0, tiled=True)  12.2 us
    dot_general x1, matrix products, local(): jnp.dot(lax.all_gather(normed, 'tp', axis=1, tiled=True), weight_all, pre...  6.61 us
  transfers between devices with their start and end apart: 4, of which 3 were waited for; matrix products, arithmetic and copies ran while one was open for 26% of the time, Pallas kernels for 0%

commit v1 on v0

v1 whole, which is shorter than its diff:
```python
import jax
import jax.numpy as jnp
from jax import lax
from jax.experimental import pallas as pl
from jax.experimental.pallas import tpu as pltpu
from jax.sharding import Mesh, PartitionSpec as P

HD = 128
BLOCK = 512
HEADS = 4
RING = 8
SLICE = HEADS * HD // RING
ROWS = SLICE + 16
ALL = ("y", "z", "x", "c")
NT = (((1,), (1,)), ((), ()))
TN = (((0,), (0,)), ((), ()))
VMEM = pl.BlockSpec(memory_space=pltpu.VMEM)
SMEM = pl.BlockSpec(memory_space=pltpu.SMEM)


def flat_pairs(sizes, move):
    ny, nz, nx, nc = sizes
    index = lambda y, z, x, c: (((y % ny) * nz + z % nz) * nx + x % nx) * nc + c % nc
    return [
        (index(y, z, x, c), index(*move(y, z, x, c)))
        for y in range(ny)
        for z in range(nz)
        for x in range(nx)
        for c in range(nc)
    ]


def parts_of(value):
    high = value.astype(jnp.bfloat16)
    rest = value - high.astype(jnp.float32)
    middle = rest.astype(jnp.bfloat16)
    low = (rest - middle.astype(jnp.float32)).astype(jnp.bfloat16)
    return high, middle, low


def dot(a, b, dims=(((1,), (0,)), ((), ()))):
    return lax.dot_general(a, b, dims, preferred_element_type=jnp.float32)


def running(log_ref, doc_ref, stage):
    docs = doc_ref[...].astype(jnp.float32)
    lane = lax.broadcasted_iota(jnp.int32, docs.shape, 1)
    stage[...] = jnp.zeros_like(stage)
    stage[0:HEADS, :] = log_ref[...]
    stage[HEADS : HEADS + 1, :] = docs - jnp.where(lane == 0, 0.0, pltpu.roll(docs, 1, 1))
    parts = parts_of(stage[...])
    row = lax.broadcasted_iota(jnp.int32, (BLOCK, BLOCK), 0)
    column = lax.broadcasted_iota(jnp.int32, (BLOCK, BLOCK), 1)
    lower = jnp.where(row >= column, 1.0, 0.0).astype(jnp.bfloat16)
    down = sum(dot(lower, part, NT) for part in parts)
    return parts, lower, down


def state_kernel(key_ref, value_ref, log_ref, doc_ref, out_ref, stage):
    _, _, down = running(log_ref, doc_ref, stage)
    final = down[BLOCK - 1 : BLOCK, :]
    kept = down[:, HEADS : HEADS + 1] == final[:, HEADS : HEADS + 1]
    to_end = jnp.where(kept, jnp.exp(final - down), 0.0)
    meta_row = lax.broadcasted_iota(jnp.int32, (16, HD), 0)
    for h in range(HEADS):
        span = slice(h * HD, (h + 1) * HD)
        decayed = (key_ref[:, span].astype(jnp.float32) * to_end[:, h : h + 1]).astype(jnp.bfloat16)
        state = dot(decayed, value_ref[:, span], TN).astype(jnp.bfloat16)
        high, middle, low = [part.astype(jnp.float32) for part in parts_of(final[:, h : h + 1])]
        meta = jnp.where(meta_row == 0, high, jnp.where(meta_row == 1, middle, jnp.where(meta_row == 2, low, 0.0)))
        meta = jnp.where(meta_row == 3, final[:, HEADS : HEADS + 1], meta).astype(jnp.bfloat16)
        for half in range(2):
            out_ref[2 * h + half, 0:SLICE, :] = state[half * SLICE : (half + 1) * SLICE]
            out_ref[2 * h + half, SLICE:ROWS, :] = meta


def read_meta(ref, k):
    meta = ref[k, SLICE:ROWS, :].astype(jnp.float32)
    return meta[0:1] + meta[1:2] + meta[2:3], meta[3:4]


def row_kernel(states_ref, out_ref):
    total = jnp.zeros((SLICE, HD), jnp.float32)
    logs = jnp.zeros((1, HD), jnp.float32)
    prior = None
    for k in range(RING):
        log, last = read_meta(states_ref, k)
        if k:
            total = total * jnp.where(last == prior, jnp.exp(log), 0.0)
        total = total + states_ref[k, 0:SLICE, :].astype(jnp.float32)
        logs = logs + log
        prior = last
    meta_row = lax.broadcasted_iota(jnp.int32, (16, HD), 0)
    high, middle, low = [part.astype(jnp.float32) for part in parts_of(logs)]
    meta = jnp.where(meta_row == 0, high, jnp.where(meta_row == 1, middle, jnp.where(meta_row == 2, low, 0.0)))
    meta = jnp.where(meta_row == 3, prior, meta).astype(jnp.bfloat16)
    total = total.astype(jnp.bfloat16)
    for k in range(RING):
        out_ref[k, 0:SLICE, :] = total
        out_ref[k, SLICE:ROWS, :] = meta


def enter_kernel(place_ref, states_ref, rows_ref, out_ref):
    here = place_ref[0]
    running_state = jnp.zeros((SLICE, HD), jnp.float32)
    memory = running_state
    prior = jnp.zeros((1, HD), jnp.float32)
    prior_row = prior
    for k in range(RING):
        log, last = read_meta(rows_ref, k)
        memory = jnp.where(here == k, running_state, memory)
        prior = jnp.where(here == k, prior_row, prior)
        running_state = running_state * jnp.where(last == prior_row, jnp.exp(log), 0.0)
        running_state = running_state + rows_ref[k, 0:SLICE, :].astype(jnp.float32)
        prior_row = last
    for k in range(RING):
        out_ref[k, 0:SLICE, :] = memory.astype(jnp.bfloat16)
        out_ref[k, SLICE:ROWS, :] = jnp.broadcast_to(prior, (16, HD)).astype(jnp.bfloat16)
        log, last = read_meta(states_ref, k)
        memory = memory * jnp.where(last == prior, jnp.exp(log), 0.0)
        memory = memory + states_ref[k, 0:SLICE, :].astype(jnp.float32)
        prior = last


def attend_kernel(query_ref, key_ref, value_ref, log_ref, doc_ref, memory_ref, gain_ref, out_ref, stage, mask):
    parts, lower, down = running(log_ref, doc_ref, stage)
    across = sum(dot(part, lower, NT) for part in parts)
    doc_down = down[:, HEADS : HEADS + 1]
    mask[...] = jnp.where(doc_down == across[HEADS : HEADS + 1, :], 0.0, -1e30)
    row = lax.broadcasted_iota(jnp.int32, (BLOCK, BLOCK), 0)
    column = lax.broadcasted_iota(jnp.int32, (BLOCK, BLOCK), 1)
    mask[...] = jnp.where(row >= column, mask[...], -1e30)
    prior = memory_ref[0, SLICE : SLICE + 16, :].astype(jnp.float32)[0:1, 0:1]
    reach = jnp.where(doc_down == prior, jnp.exp(down), 0.0)
    part_rows = BLOCK // 2
    for h in range(HEADS):
        span = slice(h * HD, (h + 1) * HD)
        memory = jnp.concatenate([memory_ref[2 * h, 0:SLICE, :], memory_ref[2 * h + 1, 0:SLICE, :]], axis=0)
        for i in range(2):
            rows = slice(i * part_rows, (i + 1) * part_rows)
            seen = slice(0, (i + 1) * part_rows)
            query = query_ref[rows, span]
            scores = dot(query, key_ref[seen, span], NT)
            gap = down[rows, h : h + 1] - across[h : h + 1, seen] + mask[rows, seen]
            weighted = (scores * jnp.exp(gap)).astype(jnp.bfloat16)
            heads = dot(weighted, value_ref[seen, span])
            heads = heads + reach[rows, h : h + 1] * dot(query, memory)
            scale = lax.rsqrt(jnp.mean(heads * heads, axis=-1, keepdims=True) + 1e-06)
            out_ref[rows, span] = (heads * scale * gain_ref[:, span]).astype(jnp.bfloat16)


def project_kernel(places_ref, own_ref, before_ref, after_ref, far_one_ref, far_two_ref, weight_ref, out_ref):
    step = pl.program_id(0)
    half = BLOCK // 2

    @pl.when(step == 0)
    def _():
        out_ref[...] = dot(own_ref[...], weight_ref[0])

    @pl.when(step == 1)
    def _():
        out_ref[...] += dot(before_ref[...], weight_ref[0])

    @pl.when(step == 2)
    def _():
        out_ref[...] += dot(after_ref[...], weight_ref[0])

    @pl.when(step == 3)
    def _():
        out_ref[0:half, :] += dot(far_one_ref[...], weight_ref[0])
        out_ref[half:BLOCK, :] += dot(far_two_ref[...], weight_ref[0])


def project(places, blocks, weight):
    columns = weight.shape[-1]
    whole = lambda array: pl.BlockSpec(array.shape, lambda k, places: (0, 0))
    return pl.pallas_call(
        project_kernel,
        out_shape=jax.ShapeDtypeStruct((BLOCK, columns), jnp.float32),
        grid_spec=pltpu.PrefetchScalarGridSpec(
            num_scalar_prefetch=1,
            grid=(4,),
            in_specs=[whole(block) for block in blocks]
            + [pl.BlockSpec((1, BLOCK, columns), lambda k, places: (places[k], 0, 0))],
            out_specs=pl.BlockSpec((BLOCK, columns), lambda k, places: (0, 0)),
        ),
        compiler_params=pltpu.CompilerParams(vmem_limit_bytes=32 * 2**20),
        cost_estimate=pl.CostEstimate(
            flops=2 * BLOCK * 4 * BLOCK * columns, bytes_accessed=6 * 2**20, transcendentals=0
        ),
    )(places, *blocks, weight)


def call(kernel, out_shape, args, specs, scratch=(), flops=0, transcendentals=0):
    return pl.pallas_call(
        kernel,
        out_shape=out_shape,
        in_specs=specs,
        out_specs=VMEM,
        scratch_shapes=list(scratch),
        compiler_params=pltpu.CompilerParams(vmem_limit_bytes=32 * 2**20),
        cost_estimate=pl.CostEstimate(flops=flops, bytes_accessed=2**20, transcendentals=transcendentals),
    )(*args)


def local(sizes, queries, key_rows, value_rows, log_decay, doc_ids, head_gain, out_weight):
    nx = sizes[2]
    y, x, c = (lax.axis_index(name) for name in ("y", "x", "c"))
    slices = jax.ShapeDtypeStruct((RING, ROWS, HD), jnp.bfloat16)
    docs = doc_ids.reshape(1, BLOCK)
    stage = pltpu.VMEM((8, BLOCK), jnp.float32)

    swap = flat_pairs(
        sizes, lambda y, z, x, c: (y, z, x, c) if y % 2 == c else (y + 1 if c else y - 1, z, x, 1 - c)
    )
    weight = lax.all_gather(lax.ppermute(out_weight, ALL, swap), ("y", "z"), axis=0, tiled=True)
    weight = weight.reshape(8, BLOCK, -1)

    states = call(
        state_kernel, slices, (key_rows, value_rows, log_decay, docs), [VMEM] * 4, [stage], 10**8, 4096
    )
    states = lax.all_to_all(states, "z", 0, 0, tiled=True)
    rows = call(row_kernel, slices, (states,), [VMEM])
    rows = lax.all_to_all(rows, "y", 0, 0, tiled=True)
    entering = call(enter_kernel, slices, (y.reshape(1), states, rows), [SMEM, VMEM, VMEM])
    entering = lax.all_to_all(entering, "z", 0, 0, tiled=True)
    normed = call(
        attend_kernel,
        jax.ShapeDtypeStruct(queries.shape, jnp.bfloat16),
        (queries, key_rows, value_rows, log_decay, docs, entering, head_gain.reshape(1, -1)),
        [VMEM] * 7,
        [stage, pltpu.VMEM((BLOCK, BLOCK), jnp.float32)],
        10**9,
        2**20,
    )

    right = [(i, (i + 1) % nx) for i in range(nx)]
    left = [(i, (i - 1) % nx) for i in range(nx)]
    before = lax.ppermute(normed, "x", right)
    after = lax.ppermute(normed, "x", left)
    half = BLOCK // 2
    far_one = lax.ppermute(before[:half], "x", right)
    far_two = lax.ppermute(after[half:], "x", left)
    blocks = (normed, before, after, far_one, far_two)
    order = jnp.stack([x, (x + nx - 1) % nx, (x + 1) % nx, (x + 2) % nx])
    other = project(2 * order + 1 - c, blocks, weight)
    other = lax.ppermute(other, "c", [(0, 1), (1, 0)])
    own = project(2 * order + c, blocks, weight)
    return (own + other).astype(jnp.bfloat16)


def solution(mesh):
    sizes = (8, 8, 4, 2)
    split = Mesh(mesh.devices.reshape(sizes), ALL)
    ctx, tp = ("y", "z"), ("x", "c")
    return jax.shard_map(
        lambda *args: local(sizes, *args),
        mesh=split,
        in_specs=(P(ctx, tp), P(ctx, tp), P(ctx, tp), P(tp, ctx), P(ctx), P(tp), P(ctx, tp)),
        out_specs=P(ctx, tp),
        check_vma=False,
    )
```

time: 312 us -> 124 us (0.40)
  blocking collectives: 121 us -> 28.9 us
  other arithmetic: 75 us -> 1.04 us
  waiting for transfers between devices: 73.3 us -> 26.9 us
  starting transfers between devices: 5.4 us -> 31.7 us
  matrix products: 12.5 us -> 0 us
  Pallas kernels: 0 us -> 9.8 us
  local copies, waits for them, and re-layouts: 5.77 us -> 11.5 us
    unnamed x1 -> x0, blocking collectives: 121 us -> none
    select_n x64 -> x0, other arithmetic: 67.4 us -> none  [lap(): return jax.tree.map(lambda a, b: jnp.where(reached, a, b), new, before)]
    all_gather x3 -> x1, waiting for transfers between devices: 72.6 us -> 5.23 us  [local(): lax.all_gather(lax.ppermute(out_weight, ALL, swap), ('y', 'z'), axis=0, t...]
    all_to_all x0 -> x2, blocking collectives: none -> 28.9 us  [the longest x1 18.1 us: local(): states = lax.all_to_all(states, 'z', 0, 0, tiled=True)]
    ppermute x1 -> x6, starting transfers between devices: 5.32 us -> 25 us  [the longest x1 6.47 us: local(): other = lax.ppermute(other, 'c', [(0, 1), (1, 0)])]
    ppermute x1 -> x6, waiting for transfers between devices: 0.01 us -> 13.9 us  [the longest x1 5.47 us: local(): far_one = lax.ppermute(before[:half], 'x', right)]
    dot_general x5 -> x0, matrix products: 12.5 us -> none  [the longest x1 6.61 us: local(): jnp.dot(lax.all_gather(normed, 'tp', axis=1, tiled=True), weight_all, pre...]
    unnamed x8 -> x26, local copies, waits for them, and re-layouts: 1.45 us -> 11.5 us
  transfers between devices with their start and end apart: 4 -> 8, of which waited for: 3 -> 6; matrix products, arithmetic and copies ran while one was open for 26% -> 0% of each run, Pallas kernels for 0% -> 6%
where the time goes in v1:
time: 124 us; the launch traced here: 123 us
  starting transfers between devices  31.7 us (26%)
  blocking collectives  28.9 us (23%)
  waiting for transfers between devices  26.9 us (22%)
  between operations  13.6 us (11%)
  local copies, waits for them, and re-layouts  11.5 us (9%)
  Pallas kernels  9.8 us (8%)
    all_to_all x1, blocking collectives, local(): states = lax.all_to_all(states, 'z', 0, 0, tiled=True)  18.1 us
    unnamed x26, local copies, waits for them, and re-layouts  11.5 us
    all_to_all x1, blocking collectives, local(): entering = lax.all_to_all(entering, 'z', 0, 0, tiled=True)  10.8 us
    all_to_all x1, waiting for transfers between devices, local(): rows = lax.all_to_all(rows, 'y', 0, 0, tiled=True)  7.84 us
    all_to_all x1, starting transfers between devices, local(): rows = lax.all_to_all(rows, 'y', 0, 0, tiled=True)  6.7 us
    ppermute x1, starting transfers between devices, local(): other = lax.ppermute(other, 'c', [(0, 1), (1, 0)])  6.47 us
    ppermute x1, waiting for transfers between devices, local(): far_one = lax.ppermute(before[:half], 'x', right)  5.47 us
    ppermute x1, starting transfers between devices, local(): far_two = lax.ppermute(after[half:], 'x', left)  5.42 us
  transfers between devices with their start and end apart: 8, of which 6 were waited for; matrix products, arithmetic and copies ran while one was open for 0% of the time, Pallas kernels for 6%

profile of v1, /device:TPU:1, one launch (start us, length us, event | category | flops | bytes accessed | tf_op | source)
XLA Modules:
  0.0 123.4 jit_solution(6334252564717081064)
XLA Ops:
  6.5 4.6 %collective-permute-start.4 = (bf16[64,512]{1,0:T(8,128)(2,1)}, bf16[64,512]{1,0:T(8,128)(2,1)S(1)}, u32[]{:S(2)}, u32[]{:S(2)}) collective-permute-start(bf16[64,512]{1,0:T(8,128)(2,1)} %param.13), channel_id=1, source_target_pairs={{0,0},{1,64},{2,2},{3,66},{4,4},{5,68},{6,6},{7,70},{8,8},{9,72},{... | collective-permute-start | bytes 196616 | tf_op jit(solution)/shard_map/ppermute | solution.py:216
  11.1 2.1 %collective-permute-done.4 = bf16[64,512]{1,0:T(8,128)(2,1)S(1)} collective-permute-done((bf16[64,512]{1,0:T(8,128)(2,1)}, bf16[64,512]{1,0:T(8,128)(2,1)S(1)}, u32[]{:S(2)}, u32[]{:S(2)}) %collective-permute-start.4) | collective-permute-done | bytes 65568 | tf_op jit(solution)/shard_map/ppermute | solution.py:216
  15.0 1.0 copy-done.4
  17.4 1.6 %shard_map.73 = bf16[8,80,128]{2,1,0:T(8,128)(2,1)S(1)} custom-call(bf16[512,512]{1,0:T(8,128)(2,1)S(1)} %copy-done.2, bf16[512,512]{1,0:T(8,128)(2,1)S(1)} %copy-done.4, f32[4,512]{1,0:T(4,128)S(1)} %copy-done.6, s32[1,512]{1,0:T(1,128)S(1)} %bitcast.10), custom_call_target="tpu_custom_call" | custom-call | flops 100000000 | bytes 1048576 | tf_op jit(solution)/shard_map/pallas_call | solution.py:195
  19.0 18.1 %all_to_all.15.states_ref = bf16[8,80,128]{2,1,0:T(8,128)(2,1)S(1)} all-to-all(bf16[8,80,128]{2,1,0:T(8,128)(2,1)S(1)} %shard_map.73), channel_id=1, replica_groups=mesh['y'=8,'z'=8,'x'=4,'c'=2] {'z'}, dimensions={0} | all-to-all | bytes 327680 | tf_op jit(solution)/shard_map/all_to_all | solution.py:222
  37.8 6.7 %all-to-all-start.1 = ((bf16[8,80,128]{2,1,0:T(8,128)(2,1)}), bf16[8,80,128]{2,1,0:T(8,128)(2,1)S(1)}, u32[]{:S(2)}, u32[]{:S(2)}) async-start(bf16[8,80,128]{2,1,0:T(8,128)(2,1)} %shard_map.74), calls=%async_computation.1 | async-start | bytes 327680 | tf_op jit(solution)/shard_map/all_to_all | solution.py:224
  44.5 7.8 %all-to-all-done.1.rows_ref = bf16[8,80,128]{2,1,0:T(8,128)(2,1)S(1)} async-done(((bf16[8,80,128]{2,1,0:T(8,128)(2,1)}), bf16[8,80,128]{2,1,0:T(8,128)(2,1)S(1)}, u32[]{:S(2)}, u32[]{:S(2)}) %all-to-all-start.1) | async-done | bytes 163872 | tf_op jit(solution)/shard_map/all_to_all | solution.py:224
  52.5 10.8 %all_to_all.16.memory_ref = bf16[8,80,128]{2,1,0:T(8,128)(2,1)S(1)} all-to-all(bf16[8,80,128]{2,1,0:T(8,128)(2,1)S(1)} %shard_map.75), channel_id=1, replica_groups=mesh['y'=8,'z'=8,'x'=4,'c'=2] {'z'}, dimensions={0} | all-to-all | bytes 327680 | tf_op jit(solution)/shard_map/all_to_all | solution.py:226
  63.2 1.0 copy-done.3
  64.3 1.0 copy-done.5
  66.7 1.0 copy-done.10
  68.4 2.6 %shard_map.76.own_ref = bf16[512,512]{1,0:T(8,128)(2,1)S(1)} custom-call(bf16[512,512]{1,0:T(8,128)(2,1)S(1)} %copy-done.10, bf16[512,512]{1,0:T(8,128)(2,1)S(1)} %copy-done.3, bf16[512,512]{1,0:T(8,128)(2,1)S(1)} %copy-done.5, f32[4,512]{1,0:T(4,128)S(1)} %copy-done.7, s32[1,512]{1,0:T(1,128)S(1)} %bitcast.11, ...), custom_call_target="tpu_custom_call" | custom-call | flops 1000000000 | bytes 1048576 | tf_op jit(solution)/shard_map/pallas_call | solution.py:195
  71.0 4.7 %collective-permute-start.1 = (bf16[512,512]{1,0:T(8,128)(2,1)S(1)}, bf16[512,512]{1,0:T(8,128)(2,1)S(1)}, u32[]{:S(2)}, u32[]{:S(2)}) collective-permute-start(bf16[512,512]{1,0:T(8,128)(2,1)S(1)} %shard_map.76.own_ref), channel_id=1, source_target_pairs={{0,6},{2,0},{4,2},{6,4},{1,7},{3,1},{5,3},{7,5},{8,14},{10,8},{12,... | collective-permute-start | bytes 1572872 | tf_op jit(solution)/shard_map/ppermute | solution.py:240
  75.7 1.9 %collective-permute-start = (bf16[512,512]{1,0:T(8,128)(2,1)S(1)}, bf16[512,512]{1,0:T(8,128)(2,1)S(1)}, u32[]{:S(2)}, u32[]{:S(2)}) collective-permute-start(bf16[512,512]{1,0:T(8,128)(2,1)S(1)} %shard_map.76.own_ref), channel_id=1, source_target_pairs={{0,2},{2,4},{4,6},{6,0},{1,3},{3,5},{5,7},{7,1},{8,10},{10,12},{12... | collective-permute-start | bytes 1572872 | tf_op jit(solution)/shard_map/ppermute | solution.py:239
  77.7 5.0 %collective-permute-done.1.after_ref = bf16[512,512]{1,0:T(8,128)(2,1)S(1)} collective-permute-done((bf16[512,512]{1,0:T(8,128)(2,1)S(1)}, bf16[512,512]{1,0:T(8,128)(2,1)S(1)}, u32[]{:S(2)}, u32[]{:S(2)}) %collective-permute-start.1) | collective-permute-done | bytes 524320 | tf_op jit(solution)/shard_map/ppermute | solution.py:240
  82.7 5.4 %collective-permute-start.3 = (bf16[256,512]{1,0:T(8,128)(2,1)S(1)}, bf16[256,512]{1,0:T(8,128)(2,1)S(1)}, u32[]{:S(2)}, u32[]{:S(2)}) collective-permute-start(bf16[256,512]{1,0:T(8,128)(2,1)S(1)} %slice.9), channel_id=1, source_target_pairs={{0,6},{2,0},{4,2},{6,4},{1,7},{3,1},{5,3},{7,5},{8,14},{10,8},{12,... | collective-permute-start | bytes 786440 | tf_op jit(solution)/shard_map/ppermute | solution.py:243
  88.2 1.9 %collective-permute-start.2 = (bf16[256,512]{1,0:T(8,128)(2,1)S(1)}, bf16[256,512]{1,0:T(8,128)(2,1)S(1)}, u32[]{:S(2)}, u32[]{:S(2)}) collective-permute-start(bf16[256,512]{1,0:T(8,128)(2,1)S(1)} %slice.8), channel_id=1, source_target_pairs={{0,2},{2,4},{4,6},{6,0},{1,3},{3,5},{5,7},{7,1},{8,10},{10,12},{12... | collective-permute-start | bytes 786440 | tf_op jit(solution)/shard_map/ppermute | solution.py:242
  90.2 1.2 collective-permute-done.3.far_two_ref
  91.4 5.5 %collective-permute-done.2.far_one_ref = bf16[256,512]{1,0:T(8,128)(2,1)S(1)} collective-permute-done((bf16[256,512]{1,0:T(8,128)(2,1)S(1)}, bf16[256,512]{1,0:T(8,128)(2,1)S(1)}, u32[]{:S(2)}, u32[]{:S(2)}) %collective-permute-start.2) | collective-permute-done | bytes 262176 | tf_op jit(solution)/shard_map/ppermute | solution.py:242
  96.9 5.2 %all-gather.2.cloned.1.call-done = bf16[4096,512]{1,0:T(8,128)(2,1)} async-done(((bf16[64,512]{1,0:T(8,128)(2,1)}), bf16[4096,512]{1,0:T(8,128)(2,1)}) %all-gather.2.cloned.1.call-update) | async-done | bytes 4194320 | tf_op jit(solution)/shard_map/all_gather | solution.py:216
  102.1 2.2 %copy-done = bf16[4096,512]{1,0:T(8,128)(2,1)S(1)} copy-done((bf16[4096,512]{1,0:T(8,128)(2,1)S(1)}, bf16[4096,512]{1,0:T(8,128)(2,1)}, u32[]{:S(2)}) %copy-start) | copy-done | bytes 4194328
  104.3 2.4 %shard_map.78 = f32[512,512]{1,0:T(8,128)S(1)} custom-call(s32[4]{0:T(128)S(1)} %get-tuple-element.5.places_ref, bf16[512,512]{1,0:T(8,128)(2,1)S(1)} %shard_map.76.own_ref, bf16[512,512]{1,0:T(8,128)(2,1)S(1)} %collective-permute-done.before_ref, bf16[512,512]{1,0:T(8,128)(2,1)S(1)} %collective-permute-done.1.after_ref, ...), custom_call_target="tpu_custom_call" | custom-call | flops 1073741824 | bytes 6291456 | tf_op jit(solution)/shard_map/pallas_call | solution.py:177
  106.7 6.5 %collective-permute-start.5 = (f32[512,512]{1,0:T(8,128)S(1)}, f32[512,512]{1,0:T(8,128)S(1)}, u32[]{:S(2)}, u32[]{:S(2)}) collective-permute-start(f32[512,512]{1,0:T(8,128)S(1)} %shard_map.78), channel_id=1, source_target_pairs={{0,1},{1,0},{2,3},{3,2},{4,5},{5,4},{6,7},{7,6},{8,9},{9,8},{10,11... | collective-permute-start | bytes 3145736 | tf_op jit(solution)/shard_map/ppermute | solution.py:247
  113.2 2.4 %shard_map.77 = f32[512,512]{1,0:T(8,128)S(1)} custom-call(s32[4]{0:T(128)S(1)} %broadcast_add_fusion.places_ref, bf16[512,512]{1,0:T(8,128)(2,1)S(1)} %shard_map.76.own_ref, bf16[512,512]{1,0:T(8,128)(2,1)S(1)} %collective-permute-done.before_ref, bf16[512,512]{1,0:T(8,128)(2,1)S(1)} %collective-permute-done.1.after_ref, ...), custom_call_target="tpu_custom_call" | custom-call | flops 1073741824 | bytes 6291456 | tf_op jit(solution)/shard_map/pallas_call | solution.py:177
  (32 shorter events, 7.0 us)
Async XLA Ops:
  6.5 95.6 %all-gather.2.cloned.1.call-start = ((), (), s32[]{:S(2)}) async-start(), calls=%async_computation.3 | async-start | bytes 4259840 | tf_op jit(solution)/shard_map/all_gather | solution.py:216
  6.5 6.7 %collective-permute-start.4 = (bf16[64,512]{1,0:T(8,128)(2,1)}, bf16[64,512]{1,0:T(8,128)(2,1)S(1)}, u32[]{:S(2)}, u32[]{:S(2)}) collective-permute-start(bf16[64,512]{1,0:T(8,128)(2,1)} %param.13), channel_id=1, source_target_pairs={{0,0},{1,64},{2,2},{3,66},{4,4},{5,68},{6,6},{7,70},{8,8},{9,72},{... | collective-permute-start | bytes 196616 | tf_op jit(solution)/shard_map/ppermute | solution.py:216
  13.3 0.6 copy-start.12
  13.9 1.0 copy-start.2
  15.0 1.0 copy-start.4
  16.0 0.7 copy-start.6
  16.7 0.7 copy-start.8
  37.8 14.5 %all-to-all-start.1 = ((bf16[8,80,128]{2,1,0:T(8,128)(2,1)}), bf16[8,80,128]{2,1,0:T(8,128)(2,1)S(1)}, u32[]{:S(2)}, u32[]{:S(2)}) async-start(bf16[8,80,128]{2,1,0:T(8,128)(2,1)} %shard_map.74), calls=%async_computation.1 | async-start | bytes 327680 | tf_op jit(solution)/shard_map/all_to_all | solution.py:224
  63.2 1.0 copy-start.3
  64.3 1.0 copy-start.5
  65.3 0.7 copy-start.7
  66.0 0.7 copy-start.9
  66.7 1.0 copy-start.10
  67.7 0.7 copy-start.11
  71.0 11.7 %collective-permute-start.1 = (bf16[512,512]{1,0:T(8,128)(2,1)S(1)}, bf16[512,512]{1,0:T(8,128)(2,1)S(1)}, u32[]{:S(2)}, u32[]{:S(2)}) collective-permute-start(bf16[512,512]{1,0:T(8,128)(2,1)S(1)} %shard_map.76.own_ref), channel_id=1, source_target_pairs={{0,6},{2,0},{4,2},{6,4},{1,7},{3,1},{5,3},{7,5},{8,14},{10,8},{12,... | collective-permute-start | bytes 1572872 | tf_op jit(solution)/shard_map/ppermute | solution.py:240
  75.7 12.4 %collective-permute-start = (bf16[512,512]{1,0:T(8,128)(2,1)S(1)}, bf16[512,512]{1,0:T(8,128)(2,1)S(1)}, u32[]{:S(2)}, u32[]{:S(2)}) collective-permute-start(bf16[512,512]{1,0:T(8,128)(2,1)S(1)} %shard_map.76.own_ref), channel_id=1, source_target_pairs={{0,2},{2,4},{4,6},{6,0},{1,3},{3,5},{5,7},{7,1},{8,10},{10,12},{12... | collective-permute-start | bytes 1572872 | tf_op jit(solution)/shard_map/ppermute | solution.py:239
  82.7 8.7 %collective-permute-start.3 = (bf16[256,512]{1,0:T(8,128)(2,1)S(1)}, bf16[256,512]{1,0:T(8,128)(2,1)S(1)}, u32[]{:S(2)}, u32[]{:S(2)}) collective-permute-start(bf16[256,512]{1,0:T(8,128)(2,1)S(1)} %slice.9), channel_id=1, source_target_pairs={{0,6},{2,0},{4,2},{6,4},{1,7},{3,1},{5,3},{7,5},{8,14},{10,8},{12,... | collective-permute-start | bytes 786440 | tf_op jit(solution)/shard_map/ppermute | solution.py:243
  88.2 8.7 %collective-permute-start.2 = (bf16[256,512]{1,0:T(8,128)(2,1)S(1)}, bf16[256,512]{1,0:T(8,128)(2,1)S(1)}, u32[]{:S(2)}, u32[]{:S(2)}) collective-permute-start(bf16[256,512]{1,0:T(8,128)(2,1)S(1)} %slice.8), channel_id=1, source_target_pairs={{0,2},{2,4},{4,6},{6,0},{1,3},{3,5},{5,7},{7,1},{8,10},{10,12},{12... | collective-permute-start | bytes 786440 | tf_op jit(solution)/shard_map/ppermute | solution.py:242
  102.1 2.2 %copy-start = (bf16[4096,512]{1,0:T(8,128)(2,1)S(1)}, bf16[4096,512]{1,0:T(8,128)(2,1)}, u32[]{:S(2)}) copy-start(bf16[4096,512]{1,0:T(8,128)(2,1)} %all-gather.2.cloned.1.call-done) | copy-start | bytes 12582916
  104.3 8.9 %copy-start.1 = (bf16[4096,512]{1,0:T(8,128)(2,1)S(1)}, bf16[4096,512]{1,0:T(8,128)(2,1)}, u32[]{:S(2)}) copy-start(bf16[4096,512]{1,0:T(8,128)(2,1)} %all-gather.2.cloned.1.call-done) | copy-start | bytes 12582916
  106.7 8.9 %collective-permute-start.5 = (f32[512,512]{1,0:T(8,128)S(1)}, f32[512,512]{1,0:T(8,128)S(1)}, u32[]{:S(2)}, u32[]{:S(2)}) collective-permute-start(f32[512,512]{1,0:T(8,128)S(1)} %shard_map.78), channel_id=1, source_target_pairs={{0,1},{1,0},{2,3},{3,2},{4,5},{5,4},{6,7},{7,6},{8,9},{9,8},{10,11... | collective-permute-start | bytes 3145736 | tf_op jit(solution)/shard_map/ppermute | solution.py:247
Sparse Core Ops, SparseCore 0:
  14.0 88.0 all-gather.1

commit v2 on v1

v2 whole, which is shorter than its diff:
```python
import jax
import jax.numpy as jnp
from jax import lax
from jax.experimental import pallas as pl
from jax.experimental.pallas import tpu as pltpu
from jax.sharding import Mesh, PartitionSpec as P

HD = 128
BLOCK = 512
HEADS = 4
RING = 8
SLICE = HEADS * HD // RING
ROWS = SLICE + 16
FULL = ROWS + 4 * 64
ALL = ("y", "z", "x", "c")
NT = (((1,), (1,)), ((), ()))
TN = (((0,), (0,)), ((), ()))
VMEM = pl.BlockSpec(memory_space=pltpu.VMEM)
ANY = pl.BlockSpec(memory_space=pl.ANY)
SMEM = pl.BlockSpec(memory_space=pltpu.SMEM)


def flat_pairs(sizes, move):
    ny, nz, nx, nc = sizes
    index = lambda y, z, x, c: (((y % ny) * nz + z % nz) * nx + x % nx) * nc + c % nc
    return [
        (index(y, z, x, c), index(*move(y, z, x, c)))
        for y in range(ny)
        for z in range(nz)
        for x in range(nx)
        for c in range(nc)
    ]


def parts_of(value):
    high = value.astype(jnp.bfloat16)
    rest = value - high.astype(jnp.float32)
    middle = rest.astype(jnp.bfloat16)
    low = (rest - middle.astype(jnp.float32)).astype(jnp.bfloat16)
    return high, middle, low


def dot(a, b, dims=(((1,), (0,)), ((), ()))):
    return lax.dot_general(a, b, dims, preferred_element_type=jnp.float32)


def running(log, doc, stage):
    docs = doc.astype(jnp.float32)
    lane = lax.broadcasted_iota(jnp.int32, docs.shape, 1)
    stage[...] = jnp.zeros_like(stage)
    stage[0:HEADS, :] = log
    stage[HEADS : HEADS + 1, :] = docs - jnp.where(lane == 0, 0.0, pltpu.roll(docs, 1, 1))
    parts = parts_of(stage[...])
    row = lax.broadcasted_iota(jnp.int32, (BLOCK, BLOCK), 0)
    column = lax.broadcasted_iota(jnp.int32, (BLOCK, BLOCK), 1)
    lower = jnp.where(row >= column, 1.0, 0.0).astype(jnp.bfloat16)
    down = sum(dot(lower, part, NT) for part in parts)
    return parts, lower, down


def fetch(sources, targets, sems):
    copies = [pltpu.make_async_copy(s, t, sems.at[i]) for i, (s, t) in enumerate(zip(sources, targets))]
    for copy in copies:
        copy.start()
    return copies


def meta_of(log, last):
    row = lax.broadcasted_iota(jnp.int32, (16, HD), 0)
    high, middle, low = [part.astype(jnp.float32) for part in parts_of(log)]
    meta = jnp.where(row == 0, high, jnp.where(row == 1, middle, jnp.where(row == 2, low, 0.0)))
    return jnp.where(row == 3, last, meta).astype(jnp.bfloat16)


def read_meta(meta):
    meta = meta.astype(jnp.float32)
    return meta[0:1] + meta[1:2] + meta[2:3], meta[3:4]


def state_kernel(log_in, doc_in, key_in, value_in, weight_in, out_ref, log, doc, key, value, weight, stage, sems):
    copies = fetch(
        (log_in, doc_in, key_in, value_in, weight_in), (log, doc, key, value, weight), sems
    )
    copies[0].wait()
    copies[1].wait()
    _, _, down = running(log[...], doc[...], stage)
    final = down[BLOCK - 1 : BLOCK, :]
    kept = down[:, HEADS : HEADS + 1] == final[:, HEADS : HEADS + 1]
    to_end = jnp.where(kept, jnp.exp(final - down), 0.0)
    copies[2].wait()
    copies[3].wait()
    for h in range(HEADS):
        span = slice(h * HD, (h + 1) * HD)
        decayed = (key[:, span].astype(jnp.float32) * to_end[:, h : h + 1]).astype(jnp.bfloat16)
        state = dot(decayed, value[:, span], TN).astype(jnp.bfloat16)
        meta = meta_of(final[:, h : h + 1], final[:, HEADS : HEADS + 1])
        for half in range(2):
            out_ref[2 * h + half, 0:SLICE, :] = state[half * SLICE : (half + 1) * SLICE]
            out_ref[2 * h + half, SLICE:ROWS, :] = meta
    copies[4].wait()
    for k in range(RING):
        for j in range(4):
            out_ref[k, ROWS + 64 * j : ROWS + 64 * (j + 1), :] = weight[:, j * HD : (j + 1) * HD]


def row_kernel(states_ref, out_ref, weight_ref):
    total = jnp.zeros((SLICE, HD), jnp.float32)
    logs = jnp.zeros((1, HD), jnp.float32)
    prior = None
    for k in range(RING):
        log, last = read_meta(states_ref[k, SLICE:ROWS, :])
        if k:
            total = total * jnp.where(last == prior, jnp.exp(log), 0.0)
        total = total + states_ref[k, 0:SLICE, :].astype(jnp.float32)
        logs = logs + log
        prior = last
    out_ref[0:SLICE, :] = total.astype(jnp.bfloat16)
    out_ref[SLICE:ROWS, :] = meta_of(logs, prior)
    weight_ref[...] = states_ref[:, ROWS:FULL, :]


def join_kernel(later_ref, earlier_ref, out_ref):
    log, last = read_meta(later_ref[SLICE:ROWS, :])
    log_before, last_before = read_meta(earlier_ref[SLICE:ROWS, :])
    keep = jnp.where(last == last_before, jnp.exp(log), 0.0)
    total = later_ref[0:SLICE, :].astype(jnp.float32) + keep * earlier_ref[0:SLICE, :].astype(jnp.float32)
    out_ref[0:SLICE, :] = total.astype(jnp.bfloat16)
    out_ref[SLICE:ROWS, :] = meta_of(log + log_before, last)


def enter_kernel(states_ref, rows_ref, out_ref):
    memory = rows_ref[0:SLICE, :].astype(jnp.float32)
    _, prior = read_meta(rows_ref[SLICE:ROWS, :])
    for k in range(RING):
        out_ref[k, 0:SLICE, :] = memory.astype(jnp.bfloat16)
        out_ref[k, SLICE:ROWS, :] = jnp.broadcast_to(prior, (16, HD)).astype(jnp.bfloat16)
        log, last = read_meta(states_ref[k, SLICE:ROWS, :])
        memory = memory * jnp.where(last == prior, jnp.exp(log), 0.0)
        memory = memory + states_ref[k, 0:SLICE, :].astype(jnp.float32)
        prior = last


def attend_kernel(
    log_in, doc_in, query_in, key_in, value_in, gain_in, memory_ref, out_ref,
    log, doc, query_ref, key_ref, value_ref, gain_ref, stage, mask, sems,
):
    copies = fetch(
        (log_in, doc_in, query_in, key_in, value_in, gain_in),
        (log, doc, query_ref, key_ref, value_ref, gain_ref),
        sems,
    )
    copies[0].wait()
    copies[1].wait()
    parts, lower, down = running(log[...], doc[...], stage)
    across = sum(dot(part, lower, NT) for part in parts)
    doc_down = down[:, HEADS : HEADS + 1]
    mask[...] = jnp.where(doc_down == across[HEADS : HEADS + 1, :], 0.0, -1e30)
    row = lax.broadcasted_iota(jnp.int32, (BLOCK, BLOCK), 0)
    column = lax.broadcasted_iota(jnp.int32, (BLOCK, BLOCK), 1)
    mask[...] = jnp.where(row >= column, mask[...], -1e30)
    prior = memory_ref[0, SLICE : SLICE + 16, :].astype(jnp.float32)[0:1, 0:1]
    reach = jnp.where(doc_down == prior, jnp.exp(down), 0.0)
    part_rows = BLOCK // 2
    for copy in copies[2:]:
        copy.wait()
    for h in range(HEADS):
        span = slice(h * HD, (h + 1) * HD)
        memory = jnp.concatenate([memory_ref[2 * h, 0:SLICE, :], memory_ref[2 * h + 1, 0:SLICE, :]], axis=0)
        for i in range(2):
            rows = slice(i * part_rows, (i + 1) * part_rows)
            seen = slice(0, (i + 1) * part_rows)
            query = query_ref[rows, span]
            scores = dot(query, key_ref[seen, span], NT)
            gap = down[rows, h : h + 1] - across[h : h + 1, seen] + mask[rows, seen]
            weighted = (scores * jnp.exp(gap)).astype(jnp.bfloat16)
            heads = dot(weighted, value_ref[seen, span])
            heads = heads + reach[rows, h : h + 1] * dot(query, memory)
            scale = lax.rsqrt(jnp.mean(heads * heads, axis=-1, keepdims=True) + 1e-06)
            out_ref[rows, span] = (heads * scale * gain_ref[:, span]).astype(jnp.bfloat16)


def project_kernel(places_ref, *refs):
    blocks, weights, (out_ref, held, sems) = refs[:5], refs[5:13], refs[13:]
    half = BLOCK // 2
    for s in range(4):
        for d in range(RING):

            @pl.when(places_ref[s] == d)
            def _():
                pltpu.make_async_copy(weights[d], held.at[s], sems.at[s]).start()

    for s in range(4):
        pltpu.make_async_copy(weights[0], held.at[s], sems.at[s]).wait()
        weight = jnp.concatenate(
            [held[s, :, 64 * j : 64 * (j + 1), :].reshape(BLOCK, HD) for j in range(4)], axis=1
        )
        if s == 0:
            out_ref[...] = dot(blocks[0][...], weight)
        elif s < 3:
            out_ref[...] += dot(blocks[s][...], weight)
        else:
            out_ref[0:half, :] += dot(blocks[3][...], weight)
            out_ref[half:BLOCK, :] += dot(blocks[4][...], weight)


def call(kernel, out_shape, args, specs, scratch=(), flops=0, transcendentals=0):
    return pl.pallas_call(
        kernel,
        out_shape=out_shape,
        in_specs=specs,
        out_specs=jax.tree.map(lambda _: VMEM, out_shape),
        scratch_shapes=list(scratch),
        compiler_params=pltpu.CompilerParams(vmem_limit_bytes=24 * 2**20),
        cost_estimate=pl.CostEstimate(flops=flops, bytes_accessed=2**20, transcendentals=transcendentals),
    )(*args)


def local(sizes, queries, key_rows, value_rows, log_decay, doc_ids, head_gain, out_weight):
    ny, _, nx, _ = sizes
    y, x, c = (lax.axis_index(name) for name in ("y", "x", "c"))
    shape = lambda *dims: jax.ShapeDtypeStruct(dims, jnp.bfloat16)
    docs, gains = doc_ids.reshape(1, BLOCK), head_gain.reshape(1, -1)
    wide = pltpu.VMEM(queries.shape, jnp.bfloat16)
    logs_held = pltpu.VMEM(log_decay.shape, jnp.float32)
    docs_held = pltpu.VMEM(docs.shape, jnp.int32)
    stage = pltpu.VMEM((8, BLOCK), jnp.float32)

    swap = flat_pairs(
        sizes, lambda y, z, x, c: (y, z, x, c) if y % 2 == c else (y + 1 if c else y - 1, z, x, 1 - c)
    )
    weight = lax.ppermute(out_weight, ALL, swap)

    states = call(
        state_kernel,
        shape(RING, FULL, HD),
        (log_decay, docs, key_rows, value_rows, weight),
        [ANY] * 5,
        [logs_held, docs_held, wide, wide, pltpu.VMEM(weight.shape, jnp.bfloat16), stage, pltpu.SemaphoreType.DMA((5,))],
        10**8,
        4096,
    )
    states = lax.all_to_all(states, "z", 0, 0, tiled=True)
    rows, weight = call(row_kernel, (shape(ROWS, HD), shape(RING, 256, HD)), (states,), [VMEM])

    up = lambda value, steps: lax.ppermute(value, "y", [(i, i + steps) for i in range(ny - steps)])
    right = [(i, (i + 1) % ny) for i in range(ny)]
    left = [(i, (i - 1) % ny) for i in range(ny)]
    rows = call(join_kernel, shape(ROWS, HD), (rows, up(rows, 1)), [VMEM] * 2)
    rows = call(join_kernel, shape(ROWS, HD), (rows, up(rows, 2)), [VMEM] * 2)
    rows = up(rows, 1)
    weights = {0: weight}
    for step in range(1, 5):
        weights[-step % RING] = lax.ppermute(weights[(1 - step) % RING], "y", right)
        if step < 4:
            weights[step] = lax.ppermute(weights[step - 1], "y", left)

    entering = call(enter_kernel, shape(RING, ROWS, HD), (states, rows), [VMEM] * 2)
    entering = lax.all_to_all(entering, "z", 0, 0, tiled=True)
    normed = call(
        attend_kernel,
        shape(*queries.shape),
        (log_decay, docs, queries, key_rows, value_rows, gains, entering),
        [ANY] * 6 + [VMEM],
        [logs_held, docs_held, wide, wide, wide, pltpu.VMEM(gains.shape, jnp.float32), stage]
        + [pltpu.VMEM((BLOCK, BLOCK), jnp.float32), pltpu.SemaphoreType.DMA((6,))],
        10**9,
        2**20,
    )

    right = [(i, (i + 1) % nx) for i in range(nx)]
    left = [(i, (i - 1) % nx) for i in range(nx)]
    before = lax.ppermute(normed, "x", right)
    after = lax.ppermute(normed, "x", left)
    half = BLOCK // 2
    far_one = lax.ppermute(before[:half], "x", right)
    far_two = lax.ppermute(after[half:], "x", left)
    blocks = [normed, before, after, far_one, far_two]
    order = jnp.stack([x, (x + nx - 1) % nx, (x + 1) % nx, (x + 2) % nx])
    project = lambda core: call(
        project_kernel,
        jax.ShapeDtypeStruct(queries.shape, jnp.float32),
        ((2 * order + core - y) % ny, *blocks, *(weights[d] for d in range(RING))),
        [SMEM] + [VMEM] * 5 + [ANY] * RING,
        [pltpu.VMEM((4, RING, 256, HD), jnp.bfloat16), pltpu.SemaphoreType.DMA((4,))],
        2 * 10**9,
    )
    other = lax.ppermute(project(1 - c), "c", [(0, 1), (1, 0)])
    return (project(c) + other).astype(jnp.bfloat16)


def solution(mesh):
    sizes = (8, 8, 4, 2)
    split = Mesh(mesh.devices.reshape(sizes), ALL)
    ctx, tp = ("y", "z"), ("x", "c")
    return jax.shard_map(
        lambda *args: local(sizes, *args),
        mesh=split,
        in_specs=(P(ctx, tp), P(ctx, tp), P(ctx, tp), P(tp, ctx), P(ctx), P(tp), P(ctx, tp)),
        out_specs=P(ctx, tp),
        check_vma=False,
    )
```

time: 124 us -> 148 us (1.19)
  the two profiles are of different devices: /device:TPU:1 before, /device:TPU:25 now
where the time goes in v2:
time: 148 us; the launch traced here: 147 us
  starting transfers between devices  74.2 us (50%)
  waiting for transfers between devices  25.7 us (17%)
  blocking collectives  24.6 us (17%)
  Pallas kernels  13.5 us (9%)
  local copies, waits for them, and re-layouts  7.86 us (5%)
    ppermute x4, starting transfers between devices, local(): weights[-step % RING] = lax.ppermute(weights[(1 - step) % RING], 'y', right)  27.1 us
    all_to_all x1, blocking collectives, local(): states = lax.all_to_all(states, 'z', 0, 0, tiled=True)  24.6 us
    ppermute x3, starting transfers between devices, local(): lax.ppermute(value, 'y', [(i, i + steps) for i in range(ny - steps)])  14.7 us
    pallas_call x8, Pallas kernels, call(): pl.pallas_call(kernel, out_shape=out_shape, in_specs=specs, out_specs=jax...  13.5 us
    ppermute x3, waiting for transfers between devices, local(): lax.ppermute(value, 'y', [(i, i + steps) for i in range(ny - steps)])  10.3 us
    ppermute x1, starting transfers between devices, local(): other = lax.ppermute(project(1 - c), 'c', [(0, 1), (1, 0)])  8.89 us
    ppermute x4, waiting for transfers between devices, local(): weights[-step % RING] = lax.ppermute(weights[(1 - step) % RING], 'y', right)  7.31 us
    unnamed x32, local copies, waits for them, and re-layouts  6.4 us
  transfers between devices with their start and end apart: 17, of which 7 were waited for; matrix products, arithmetic and copies ran while one was open for 1% of the time, Pallas kernels for 5%

profile of v2, /device:TPU:25, one launch (start us, length us, event | category | flops | bytes accessed | tf_op | source)
XLA Modules:
  0.0 147.4 jit_solution(9795064255743434334)
XLA Ops:
  5.0 2.1 %shard_map.73 = bf16[8,336,128]{2,1,0:T(8,128)(2,1)S(1)} custom-call(f32[4,512]{1,0:T(4,128)S(1)} %copy-done.4, s32[1,512]{1,0:T(1,128)S(1)} %bitcast.6, bf16[512,512]{1,0:T(8,128)(2,1)S(1)} %copy-done, bf16[512,512]{1,0:T(8,128)(2,1)S(1)} %copy-done.2, bf16[64,512]{1,0:T(8,128)(2,1)S(1)} %collective-permute-done.weight_in), custom_call_target="tpu_custom_call" | custom-call | flops 100000000 | bytes 1048576 | tf_op jit(solution)/shard_map/pallas_call | solution.py:207
  7.1 24.6 %all_to_all.10.states_ref = bf16[8,336,128]{2,1,0:T(8,128)(2,1)S(1)} all-to-all(bf16[8,336,128]{2,1,0:T(8,128)(2,1)S(1)} %shard_map.73), channel_id=1, replica_groups=mesh['y'=8,'z'=8,'x'=4,'c'=2] {'z'}, dimensions={0} | all-to-all | bytes 1376256 | tf_op jit(solution)/shard_map/all_to_all | solution.py:242
  31.8 12.4 %collective-permute-start.11 = (bf16[8,256,128]{2,1,0:T(8,128)(2,1)S(1)}, bf16[8,256,128]{2,1,0:T(8,128)(2,1)S(1)}, u32[]{:S(2)}, u32[]{:S(2)}) collective-permute-start(bf16[8,256,128]{2,1,0:T(8,128)(2,1)S(1)} %get-tuple-element.8.refs_5_), channel_id=1, source_target_pairs={{0,64},{64,128},{128,192},{192,256},{256,320},{320,384},{384,448},... | collective-permute-start | bytes 1572872 | tf_op jit(solution)/shard_map/ppermute | solution.py:253
  44.2 1.9 %collective-permute-start.8 = (bf16[8,256,128]{2,1,0:T(8,128)(2,1)S(1)}, bf16[8,256,128]{2,1,0:T(8,128)(2,1)S(1)}, u32[]{:S(2)}, u32[]{:S(2)}) collective-permute-start(bf16[8,256,128]{2,1,0:T(8,128)(2,1)S(1)} %get-tuple-element.8.refs_5_), channel_id=1, source_target_pairs={{0,448},{64,0},{128,64},{192,128},{256,192},{320,256},{384,320},{4... | collective-permute-start | bytes 1572872 | tf_op jit(solution)/shard_map/ppermute | solution.py:255
  46.1 7.3 %collective-permute-done.11.refs_12_ = bf16[8,256,128]{2,1,0:T(8,128)(2,1)S(1)} collective-permute-done((bf16[8,256,128]{2,1,0:T(8,128)(2,1)S(1)}, bf16[8,256,128]{2,1,0:T(8,128)(2,1)S(1)}, u32[]{:S(2)}, u32[]{:S(2)}) %collective-permute-start.11) | collective-permute-done | bytes 524320 | tf_op jit(solution)/shard_map/ppermute | solution.py:253
  53.4 5.0 %collective-permute-start.12 = (bf16[8,256,128]{2,1,0:T(8,128)(2,1)S(1)}, bf16[8,256,128]{2,1,0:T(8,128)(2,1)}, u32[]{:S(2)}, u32[]{:S(2)}) collective-permute-start(bf16[8,256,128]{2,1,0:T(8,128)(2,1)S(1)} %collective-permute-done.11.refs_12_), channel_id=1, source_target_pairs={{0,64},{64,128},{128,192},{192,256},{256,320},{320,384},{384,448},... | collective-permute-start | bytes 1572872 | tf_op jit(solution)/shard_map/ppermute | solution.py:253
  58.5 3.4 %collective-permute-start.1 = (bf16[80,128]{1,0:T(8,128)(2,1)S(1)}, bf16[80,128]{1,0:T(8,128)(2,1)S(1)}, u32[]{:S(2)}, u32[]{:S(2)}) collective-permute-start(bf16[80,128]{1,0:T(8,128)(2,1)S(1)} %get-tuple-element.7.later_ref), channel_id=1, source_target_pairs={{0,64},{64,128},{128,192},{192,256},{256,320},{320,384},{384,448},... | collective-permute-start | bytes 61448 | tf_op jit(solution)/shard_map/ppermute | solution.py:245
  61.8 8.5 %collective-permute-done.1.earlier_ref = bf16[80,128]{1,0:T(8,128)(2,1)S(1)} collective-permute-done((bf16[80,128]{1,0:T(8,128)(2,1)S(1)}, bf16[80,128]{1,0:T(8,128)(2,1)S(1)}, u32[]{:S(2)}, u32[]{:S(2)}) %collective-permute-start.1) | collective-permute-done | bytes 20512 | tf_op jit(solution)/shard_map/ppermute | solution.py:245
  70.4 4.7 %collective-permute-start.2 = (bf16[80,128]{1,0:T(8,128)(2,1)S(1)}, bf16[80,128]{1,0:T(8,128)(2,1)S(1)}, u32[]{:S(2)}, u32[]{:S(2)}) collective-permute-start(bf16[80,128]{1,0:T(8,128)(2,1)S(1)} %shard_map.75.later_ref), channel_id=1, source_target_pairs={{0,128},{64,192},{128,256},{192,320},{256,384},{320,448},{1,129},{... | collective-permute-start | bytes 61448 | tf_op jit(solution)/shard_map/ppermute | solution.py:245
  76.0 6.7 %collective-permute-start.3 = (bf16[80,128]{1,0:T(8,128)(2,1)S(1)}, bf16[80,128]{1,0:T(8,128)(2,1)S(1)}, u32[]{:S(2)}, u32[]{:S(2)}) collective-permute-start(bf16[80,128]{1,0:T(8,128)(2,1)S(1)} %shard_map.76), channel_id=1, source_target_pairs={{0,64},{64,128},{128,192},{192,256},{256,320},{320,384},{384,448},... | collective-permute-start | bytes 61448 | tf_op jit(solution)/shard_map/ppermute | solution.py:245
  84.3 3.5 %all-to-all-start.1 = ((bf16[8,80,128]{2,1,0:T(8,128)(2,1)}), bf16[8,80,128]{2,1,0:T(8,128)(2,1)S(1)}, u32[]{:S(2)}, u32[]{:S(2)}) async-start(bf16[8,80,128]{2,1,0:T(8,128)(2,1)} %shard_map.77), calls=%async_computation.1 | async-start | bytes 327680 | tf_op jit(solution)/shard_map/all_to_all | solution.py:258
  87.8 1.9 %collective-permute-start.9 = (bf16[8,256,128]{2,1,0:T(8,128)(2,1)S(1)}, bf16[8,256,128]{2,1,0:T(8,128)(2,1)}, u32[]{:S(2)}, u32[]{:S(2)}) collective-permute-start(bf16[8,256,128]{2,1,0:T(8,128)(2,1)S(1)} %collective-permute-done.8.refs_6_), channel_id=1, source_target_pairs={{0,448},{64,0},{128,64},{192,128},{256,192},{320,256},{384,320},{4... | collective-permute-start | bytes 1572872 | tf_op jit(solution)/shard_map/ppermute | solution.py:255
  89.7 4.8 %collective-permute-start.13 = (bf16[8,256,128]{2,1,0:T(8,128)(2,1)}, bf16[8,256,128]{2,1,0:T(8,128)(2,1)}, u32[]{:S(2)}, u32[]{:S(2)}) collective-permute-start(bf16[8,256,128]{2,1,0:T(8,128)(2,1)} %collective-permute-done.12.refs_11_), channel_id=1, source_target_pairs={{0,64},{64,128},{128,192},{192,256},{256,320},{320,384},{384,448},... | collective-permute-start | bytes 1572872 | tf_op jit(solution)/shard_map/ppermute | solution.py:253
  96.1 3.4 %shard_map.78.refs_0_ = bf16[512,512]{1,0:T(8,128)(2,1)S(1)} custom-call(f32[4,512]{1,0:T(4,128)S(1)} %copy-done.5, s32[1,512]{1,0:T(1,128)S(1)} %bitcast.7, bf16[512,512]{1,0:T(8,128)(2,1)S(1)} %copy-done.8, bf16[512,512]{1,0:T(8,128)(2,1)S(1)} %copy-done.1, bf16[512,512]{1,0:T(8,128)(2,1)S(1)} %copy-done.3, f32[1,512]{1,0:T(1,128)S(1)} %bitcast.8, ...), custom_call_target="tpu_custom_call" | custom-call | flops 1000000000 | bytes 1048576 | tf_op jit(solution)/shard_map/pallas_call | solution.py:207
  99.5 4.4 %collective-permute-start.5 = (bf16[512,512]{1,0:T(8,128)(2,1)S(1)}, bf16[512,512]{1,0:T(8,128)(2,1)S(1)}, u32[]{:S(2)}, u32[]{:S(2)}) collective-permute-start(bf16[512,512]{1,0:T(8,128)(2,1)S(1)} %shard_map.78.refs_0_), channel_id=1, source_target_pairs={{0,6},{2,0},{4,2},{6,4},{1,7},{3,1},{5,3},{7,5},{8,14},{10,8},{12,... | collective-permute-start | bytes 1572872 | tf_op jit(solution)/shard_map/ppermute | solution.py:273
  103.9 1.9 %collective-permute-start.4 = (bf16[512,512]{1,0:T(8,128)(2,1)S(1)}, bf16[512,512]{1,0:T(8,128)(2,1)S(1)}, u32[]{:S(2)}, u32[]{:S(2)}) collective-permute-start(bf16[512,512]{1,0:T(8,128)(2,1)S(1)} %shard_map.78.refs_0_), channel_id=1, source_target_pairs={{0,2},{2,4},{4,6},{6,0},{1,3},{3,5},{5,7},{7,1},{8,10},{10,12},{12... | collective-permute-start | bytes 1572872 | tf_op jit(solution)/shard_map/ppermute | solution.py:272
  105.9 1.9 %collective-permute-start.10 = (bf16[8,256,128]{2,1,0:T(8,128)(2,1)}, bf16[8,256,128]{2,1,0:T(8,128)(2,1)S(1)}, u32[]{:S(2)}, u32[]{:S(2)}) collective-permute-start(bf16[8,256,128]{2,1,0:T(8,128)(2,1)} %collective-permute-done.9.refs_7_), channel_id=1, source_target_pairs={{0,448},{64,0},{128,64},{192,128},{256,192},{320,256},{384,320},{4... | collective-permute-start | bytes 1572872 | tf_op jit(solution)/shard_map/ppermute | solution.py:255
  107.8 4.8 %collective-permute-start.14 = (bf16[8,256,128]{2,1,0:T(8,128)(2,1)}, bf16[8,256,128]{2,1,0:T(8,128)(2,1)}, u32[]{:S(2)}, u32[]{:S(2)}) collective-permute-start(bf16[8,256,128]{2,1,0:T(8,128)(2,1)} %collective-permute-done.13.refs_10_), channel_id=1, source_target_pairs={{0,64},{64,128},{128,192},{192,256},{256,320},{320,384},{384,448},... | collective-permute-start | bytes 1572872 | tf_op jit(solution)/shard_map/ppermute | solution.py:253
  113.4 4.6 %collective-permute-start.7 = (bf16[256,512]{1,0:T(8,128)(2,1)}, bf16[256,512]{1,0:T(8,128)(2,1)}, u32[]{:S(2)}, u32[]{:S(2)}) collective-permute-start(bf16[256,512]{1,0:T(8,128)(2,1)} %slice.9), channel_id=1, source_target_pairs={{0,6},{2,0},{4,2},{6,4},{1,7},{3,1},{5,3},{7,5},{8,14},{10,8},{12,... | collective-permute-start | bytes 786440 | tf_op jit(solution)/shard_map/ppermute | solution.py:276
  118.7 1.9 %collective-permute-start.6 = (bf16[256,512]{1,0:T(8,128)(2,1)}, bf16[256,512]{1,0:T(8,128)(2,1)}, u32[]{:S(2)}, u32[]{:S(2)}) collective-permute-start(bf16[256,512]{1,0:T(8,128)(2,1)} %slice.8), channel_id=1, source_target_pairs={{0,2},{2,4},{4,6},{6,0},{1,3},{3,5},{5,7},{7,1},{8,10},{10,12},{12... | collective-permute-start | bytes 786440 | tf_op jit(solution)/shard_map/ppermute | solution.py:275
  121.6 5.8 %collective-permute-done.6.refs_3_ = bf16[256,512]{1,0:T(8,128)(2,1)} collective-permute-done((bf16[256,512]{1,0:T(8,128)(2,1)}, bf16[256,512]{1,0:T(8,128)(2,1)}, u32[]{:S(2)}, u32[]{:S(2)}) %collective-permute-start.6) | collective-permute-done | bytes 262176 | tf_op jit(solution)/shard_map/ppermute | solution.py:275
  130.2 3.6 %shard_map.80 = f32[512,512]{1,0:T(8,128)S(1)} custom-call(s32[4]{0:T(128)S(1)} %get-tuple-element.9.places_ref, bf16[512,512]{1,0:T(8,128)(2,1)S(1)} %copy-done.10, bf16[512,512]{1,0:T(8,128)(2,1)S(1)} %collective-permute-done.4.refs_1_, bf16[512,512]{1,0:T(8,128)(2,1)S(1)} %collective-permute-done.5.refs_2_, ...), custom_call_target="tpu_custom_call" | custom-call | flops 2000000000 | bytes 1048576 | tf_op jit(solution)/shard_map/pallas_call | solution.py:207
  133.9 8.9 %collective-permute-start.15 = (f32[512,512]{1,0:T(8,128)S(1)}, f32[512,512]{1,0:T(8,128)S(1)}, u32[]{:S(2)}, u32[]{:S(2)}) collective-permute-start(f32[512,512]{1,0:T(8,128)S(1)} %shard_map.80), channel_id=1, source_target_pairs={{0,1},{1,0},{2,3},{3,2},{4,5},{5,4},{6,7},{7,6},{8,9},{9,8},{10,11... | collective-permute-start | bytes 3145736 | tf_op jit(solution)/shard_map/ppermute | solution.py:287
  142.8 3.6 %shard_map.79 = f32[512,512]{1,0:T(8,128)S(1)} custom-call(s32[4]{0:T(128)S(1)} %and_select_fusion.1.places_ref, bf16[512,512]{1,0:T(8,128)(2,1)S(1)} %copy-done.11, bf16[512,512]{1,0:T(8,128)(2,1)S(1)} %collective-permute-done.4.refs_1_, bf16[512,512]{1,0:T(8,128)(2,1)S(1)} %collective-permute-done.5.refs_2_, ...), custom_call_target="tpu_custom_call" | custom-call | flops 2000000000 | bytes 1048576 | tf_op jit(solution)/shard_map/pallas_call | solution.py:207
  (56 shorter events, 15.3 us)
Async XLA Ops:
  0.0 1.5 %collective-permute-start = (bf16[64,512]{1,0:T(8,128)(2,1)}, bf16[64,512]{1,0:T(8,128)(2,1)S(1)}, u32[]{:S(2)}, u32[]{:S(2)}) collective-permute-start(bf16[64,512]{1,0:T(8,128)(2,1)} %param.13), channel_id=1, source_target_pairs={{0,0},{1,64},{2,2},{3,66},{4,4},{5,68},{6,6},{7,70},{8,8},{9,72},{... | collective-permute-start | bytes 196616 | tf_op jit(solution)/shard_map/ppermute | solution.py:231
  31.7 64.4 %copy-start.8 = (bf16[512,512]{1,0:T(8,128)(2,1)S(1)}, bf16[512,512]{1,0:T(8,128)(2,1)}, u32[]{:S(2)}) copy-start(bf16[512,512]{1,0:T(8,128)(2,1)} %query_in.1) | copy-start | bytes 1572868
  31.8 21.7 %collective-permute-start.11 = (bf16[8,256,128]{2,1,0:T(8,128)(2,1)S(1)}, bf16[8,256,128]{2,1,0:T(8,128)(2,1)S(1)}, u32[]{:S(2)}, u32[]{:S(2)}) collective-permute-start(bf16[8,256,128]{2,1,0:T(8,128)(2,1)S(1)} %get-tuple-element.8.refs_5_), channel_id=1, source_target_pairs={{0,64},{64,128},{128,192},{192,256},{256,320},{320,384},{384,448},... | collective-permute-start | bytes 1572872 | tf_op jit(solution)/shard_map/ppermute | solution.py:253
  44.2 43.6 %collective-permute-start.8 = (bf16[8,256,128]{2,1,0:T(8,128)(2,1)S(1)}, bf16[8,256,128]{2,1,0:T(8,128)(2,1)S(1)}, u32[]{:S(2)}, u32[]{:S(2)}) collective-permute-start(bf16[8,256,128]{2,1,0:T(8,128)(2,1)S(1)} %get-tuple-element.8.refs_5_), channel_id=1, source_target_pairs={{0,448},{64,0},{128,64},{192,128},{256,192},{320,256},{384,320},{4... | collective-permute-start | bytes 1572872 | tf_op jit(solution)/shard_map/ppermute | solution.py:255
  53.4 36.3 %collective-permute-start.12 = (bf16[8,256,128]{2,1,0:T(8,128)(2,1)S(1)}, bf16[8,256,128]{2,1,0:T(8,128)(2,1)}, u32[]{:S(2)}, u32[]{:S(2)}) collective-permute-start(bf16[8,256,128]{2,1,0:T(8,128)(2,1)S(1)} %collective-permute-done.11.refs_12_), channel_id=1, source_target_pairs={{0,64},{64,128},{128,192},{192,256},{256,320},{320,384},{384,448},... | collective-permute-start | bytes 1572872 | tf_op jit(solution)/shard_map/ppermute | solution.py:253
  58.5 11.9 %collective-permute-start.1 = (bf16[80,128]{1,0:T(8,128)(2,1)S(1)}, bf16[80,128]{1,0:T(8,128)(2,1)S(1)}, u32[]{:S(2)}, u32[]{:S(2)}) collective-permute-start(bf16[80,128]{1,0:T(8,128)(2,1)S(1)} %get-tuple-element.7.later_ref), channel_id=1, source_target_pairs={{0,64},{64,128},{128,192},{192,256},{256,320},{320,384},{384,448},... | collective-permute-start | bytes 61448 | tf_op jit(solution)/shard_map/ppermute | solution.py:245
  70.4 5.5 %collective-permute-start.2 = (bf16[80,128]{1,0:T(8,128)(2,1)S(1)}, bf16[80,128]{1,0:T(8,128)(2,1)S(1)}, u32[]{:S(2)}, u32[]{:S(2)}) collective-permute-start(bf16[80,128]{1,0:T(8,128)(2,1)S(1)} %shard_map.75.later_ref), channel_id=1, source_target_pairs={{0,128},{64,192},{128,256},{192,320},{256,384},{320,448},{1,129},{... | collective-permute-start | bytes 61448 | tf_op jit(solution)/shard_map/ppermute | solution.py:245
  76.0 20.1 %copy-start.1 = (bf16[512,512]{1,0:T(8,128)(2,1)S(1)}, bf16[512,512]{1,0:T(8,128)(2,1)}, u32[]{:S(2)}) copy-start(bf16[512,512]{1,0:T(8,128)(2,1)} %key_in.3) | copy-start | bytes 1572868
  76.0 20.1 %copy-start.3 = (bf16[512,512]{1,0:T(8,128)(2,1)S(1)}, bf16[512,512]{1,0:T(8,128)(2,1)}, u32[]{:S(2)}) copy-start(bf16[512,512]{1,0:T(8,128)(2,1)} %value_in.3) | copy-start | bytes 1572868
  76.0 7.6 %collective-permute-start.3 = (bf16[80,128]{1,0:T(8,128)(2,1)S(1)}, bf16[80,128]{1,0:T(8,128)(2,1)S(1)}, u32[]{:S(2)}, u32[]{:S(2)}) collective-permute-start(bf16[80,128]{1,0:T(8,128)(2,1)S(1)} %shard_map.76), channel_id=1, source_target_pairs={{0,64},{64,128},{128,192},{192,256},{256,320},{320,384},{384,448},... | collective-permute-start | bytes 61448 | tf_op jit(solution)/shard_map/ppermute | solution.py:245
  84.3 11.8 %copy-start.15 = (f32[512]{0:T(512)S(1)}, f32[512]{0:T(512)}, u32[]{:S(2)}) copy-start(f32[512]{0:T(512)} %param.12) | copy-start | bytes 6148
  84.3 11.8 %all-to-all-start.1 = ((bf16[8,80,128]{2,1,0:T(8,128)(2,1)}), bf16[8,80,128]{2,1,0:T(8,128)(2,1)S(1)}, u32[]{:S(2)}, u32[]{:S(2)}) async-start(bf16[8,80,128]{2,1,0:T(8,128)(2,1)} %shard_map.77), calls=%async_computation.1 | async-start | bytes 327680 | tf_op jit(solution)/shard_map/all_to_all | solution.py:258
  87.8 18.1 %collective-permute-start.9 = (bf16[8,256,128]{2,1,0:T(8,128)(2,1)S(1)}, bf16[8,256,128]{2,1,0:T(8,128)(2,1)}, u32[]{:S(2)}, u32[]{:S(2)}) collective-permute-start(bf16[8,256,128]{2,1,0:T(8,128)(2,1)S(1)} %collective-permute-done.8.refs_6_), channel_id=1, source_target_pairs={{0,448},{64,0},{128,64},{192,128},{256,192},{320,256},{384,320},{4... | collective-permute-start | bytes 1572872 | tf_op jit(solution)/shard_map/ppermute | solution.py:255
  89.7 18.1 %collective-permute-start.13 = (bf16[8,256,128]{2,1,0:T(8,128)(2,1)}, bf16[8,256,128]{2,1,0:T(8,128)(2,1)}, u32[]{:S(2)}, u32[]{:S(2)}) collective-permute-start(bf16[8,256,128]{2,1,0:T(8,128)(2,1)} %collective-permute-done.12.refs_11_), channel_id=1, source_target_pairs={{0,64},{64,128},{128,192},{192,256},{256,320},{320,384},{384,448},... | collective-permute-start | bytes 1572872 | tf_op jit(solution)/shard_map/ppermute | solution.py:253
  99.5 19.2 %copy-start.9 = (bf16[512,512]{1,0:T(8,128)(2,1)}, bf16[512,512]{1,0:T(8,128)(2,1)S(1)}, u32[]{:S(2)}) copy-start(bf16[512,512]{1,0:T(8,128)(2,1)S(1)} %shard_map.78.refs_0_) | copy-start | bytes 1572868
  99.5 13.1 %collective-permute-start.5 = (bf16[512,512]{1,0:T(8,128)(2,1)S(1)}, bf16[512,512]{1,0:T(8,128)(2,1)S(1)}, u32[]{:S(2)}, u32[]{:S(2)}) collective-permute-start(bf16[512,512]{1,0:T(8,128)(2,1)S(1)} %shard_map.78.refs_0_), channel_id=1, source_target_pairs={{0,6},{2,0},{4,2},{6,4},{1,7},{3,1},{5,3},{7,5},{8,14},{10,8},{12,... | collective-permute-start | bytes 1572872 | tf_op jit(solution)/shard_map/ppermute | solution.py:273
  103.9 14.0 %collective-permute-start.4 = (bf16[512,512]{1,0:T(8,128)(2,1)S(1)}, bf16[512,512]{1,0:T(8,128)(2,1)S(1)}, u32[]{:S(2)}, u32[]{:S(2)}) collective-permute-start(bf16[512,512]{1,0:T(8,128)(2,1)S(1)} %shard_map.78.refs_0_), channel_id=1, source_target_pairs={{0,2},{2,4},{4,6},{6,0},{1,3},{3,5},{5,7},{7,1},{8,10},{10,12},{12... | collective-permute-start | bytes 1572872 | tf_op jit(solution)/shard_map/ppermute | solution.py:272
  105.9 21.5 %collective-permute-start.10 = (bf16[8,256,128]{2,1,0:T(8,128)(2,1)}, bf16[8,256,128]{2,1,0:T(8,128)(2,1)S(1)}, u32[]{:S(2)}, u32[]{:S(2)}) collective-permute-start(bf16[8,256,128]{2,1,0:T(8,128)(2,1)} %collective-permute-done.9.refs_7_), channel_id=1, source_target_pairs={{0,448},{64,0},{128,64},{192,128},{256,192},{320,256},{384,320},{4... | collective-permute-start | bytes 1572872 | tf_op jit(solution)/shard_map/ppermute | solution.py:255
  107.8 20.3 %collective-permute-start.14 = (bf16[8,256,128]{2,1,0:T(8,128)(2,1)}, bf16[8,256,128]{2,1,0:T(8,128)(2,1)}, u32[]{:S(2)}, u32[]{:S(2)}) collective-permute-start(bf16[8,256,128]{2,1,0:T(8,128)(2,1)} %collective-permute-done.13.refs_10_), channel_id=1, source_target_pairs={{0,64},{64,128},{128,192},{192,256},{256,320},{320,384},{384,448},... | collective-permute-start | bytes 1572872 | tf_op jit(solution)/shard_map/ppermute | solution.py:253
  113.4 8.2 %collective-permute-start.7 = (bf16[256,512]{1,0:T(8,128)(2,1)}, bf16[256,512]{1,0:T(8,128)(2,1)}, u32[]{:S(2)}, u32[]{:S(2)}) collective-permute-start(bf16[256,512]{1,0:T(8,128)(2,1)} %slice.9), channel_id=1, source_target_pairs={{0,6},{2,0},{4,2},{6,4},{1,7},{3,1},{5,3},{7,5},{8,14},{10,8},{12,... | collective-permute-start | bytes 786440 | tf_op jit(solution)/shard_map/ppermute | solution.py:276
  118.7 8.6 %collective-permute-start.6 = (bf16[256,512]{1,0:T(8,128)(2,1)}, bf16[256,512]{1,0:T(8,128)(2,1)}, u32[]{:S(2)}, u32[]{:S(2)}) collective-permute-start(bf16[256,512]{1,0:T(8,128)(2,1)} %slice.8), channel_id=1, source_target_pairs={{0,2},{2,4},{4,6},{6,0},{1,3},{3,5},{5,7},{7,1},{8,10},{10,12},{12... | collective-permute-start | bytes 786440 | tf_op jit(solution)/shard_map/ppermute | solution.py:275
  130.2 12.6 %copy-start.11 = (bf16[512,512]{1,0:T(8,128)(2,1)S(1)}, bf16[512,512]{1,0:T(8,128)(2,1)}, u32[]{:S(2)}) copy-start(bf16[512,512]{1,0:T(8,128)(2,1)} %copy-done.9) | copy-start | bytes 1572868
  130.2 12.6 %copy-start.14 = (bf16[8,256,128]{2,1,0:T(8,128)(2,1)S(1)}, bf16[8,256,128]{2,1,0:T(8,128)(2,1)}, u32[]{:S(2)}) copy-start(bf16[8,256,128]{2,1,0:T(8,128)(2,1)} %copy-done.12) | copy-start | bytes 1572868
  133.9 12.5 %collective-permute-start.15 = (f32[512,512]{1,0:T(8,128)S(1)}, f32[512,512]{1,0:T(8,128)S(1)}, u32[]{:S(2)}, u32[]{:S(2)}) collective-permute-start(f32[512,512]{1,0:T(8,128)S(1)} %shard_map.80), channel_id=1, source_target_pairs={{0,1},{1,0},{2,3},{3,2},{4,5},{5,4},{6,7},{7,6},{8,9},{9,8},{10,11... | collective-permute-start | bytes 3145736 | tf_op jit(solution)/shard_map/ppermute | solution.py:287
  (9 other events, 30.0 us)

commit v3 on v2

v3 whole, which is shorter than its diff:
```python
import jax
import jax.numpy as jnp
from jax import lax
from jax.experimental import pallas as pl
from jax.experimental.pallas import tpu as pltpu
from jax.sharding import Mesh, PartitionSpec as P

HD = 128
BLOCK = 512
HEADS = 4
RING = 8
SLICE = HEADS * HD // RING
ROWS = SLICE + 16
GRANT = 62
FULL = ROWS + 4 * 64
ALL = ("y", "z", "x", "c")
NT = (((1,), (1,)), ((), ()))
TN = (((0,), (0,)), ((), ()))
VMEM = pl.BlockSpec(memory_space=pltpu.VMEM)
ANY = pl.BlockSpec(memory_space=pl.ANY)
SMEM = pl.BlockSpec(memory_space=pltpu.SMEM)


def parts_of(value):
    high = value.astype(jnp.bfloat16)
    rest = value - high.astype(jnp.float32)
    middle = rest.astype(jnp.bfloat16)
    low = (rest - middle.astype(jnp.float32)).astype(jnp.bfloat16)
    return high, middle, low


def dot(a, b, dims=(((1,), (0,)), ((), ()))):
    return lax.dot_general(a, b, dims, preferred_element_type=jnp.float32)


def running(log, doc, stage):
    stage[...] = jnp.zeros_like(stage)
    stage[0:HEADS, :] = log
    total = stage[...]
    lane = lax.broadcasted_iota(jnp.int32, total.shape, 1)
    step = 1
    while step < BLOCK:
        total = total + jnp.where(lane >= step, pltpu.roll(total, step, 1), 0.0)
        step *= 2
    stage[0:HEADS, :] = total[0:HEADS, :]
    stage[HEADS : HEADS + 1, :] = doc.astype(jnp.float32)
    across = stage[...]
    return across, jnp.transpose(across)


def fetch(sources, targets, sems):
    copies = [pltpu.make_async_copy(s, t, sems.at[i]) for i, (s, t) in enumerate(zip(sources, targets))]
    for copy in copies:
        copy.start()
    return copies


def meta_of(log, last):
    row = lax.broadcasted_iota(jnp.int32, (16, HD), 0)
    high, middle, low = [part.astype(jnp.float32) for part in parts_of(log)]
    meta = jnp.where(row == 0, high, jnp.where(row == 1, middle, jnp.where(row == 2, low, 0.0)))
    return jnp.where(row == 3, last, meta).astype(jnp.bfloat16)


def read_meta(meta):
    meta = meta.astype(jnp.float32)
    return meta[0:1] + meta[1:2] + meta[2:3], meta[3:4]


def state_kernel(log_in, doc_in, key_in, value_in, weight_in, out_ref, log, doc, key, value, weight, stage, sems):
    copies = fetch(
        (log_in, doc_in, key_in, value_in, weight_in), (log, doc, key, value, weight), sems
    )
    copies[0].wait()
    copies[1].wait()
    _, down = running(log[...], doc[...], stage)
    final = down[BLOCK - 1 : BLOCK, :]
    kept = down[:, HEADS : HEADS + 1] == final[:, HEADS : HEADS + 1]
    to_end = jnp.where(kept, jnp.exp(final - down), 0.0)
    copies[2].wait()
    copies[3].wait()
    for h in range(HEADS):
        span = slice(h * HD, (h + 1) * HD)
        decayed = (key[:, span].astype(jnp.float32) * to_end[:, h : h + 1]).astype(jnp.bfloat16)
        state = dot(decayed, value[:, span], TN).astype(jnp.bfloat16)
        meta = meta_of(final[:, h : h + 1], final[:, HEADS : HEADS + 1])
        for half in range(2):
            out_ref[2 * h + half, 0:SLICE, :] = state[half * SLICE : (half + 1) * SLICE]
            out_ref[2 * h + half, SLICE:ROWS, :] = meta
    copies[4].wait()
    for k in range(RING):
        for j in range(4):
            out_ref[k, ROWS + 64 * j : ROWS + 64 * (j + 1), :] = weight[:, j * HD : (j + 1) * HD]


def row_kernel(states_ref, out_ref, weight_ref):
    total = jnp.zeros((SLICE, HD), jnp.float32)
    logs = jnp.zeros((1, HD), jnp.float32)
    prior = None
    for k in range(RING):
        log, last = read_meta(states_ref[k, SLICE:ROWS, :])
        if k:
            total = total * jnp.where(last == prior, jnp.exp(log), 0.0)
        total = total + states_ref[k, 0:SLICE, :].astype(jnp.float32)
        logs = logs + log
        prior = last
    for k in range(RING):
        out_ref[k, 0:SLICE, :] = total.astype(jnp.bfloat16)
        out_ref[k, SLICE:ROWS, :] = meta_of(logs, prior)
    weight_ref[...] = states_ref[:, ROWS:FULL, :]


def enter_kernel(states_ref, rows_ref, out_ref):
    here = lax.axis_index("y")
    entering = jnp.zeros((SLICE, HD), jnp.float32)
    memory = entering
    prior = jnp.zeros((1, HD), jnp.float32)
    prior_row = prior
    for k in range(RING):
        log, last = read_meta(rows_ref[k, SLICE:ROWS, :])
        memory = jnp.where(here == k, entering, memory)
        prior = jnp.where(here == k, prior_row, prior)
        entering = entering * jnp.where(last == prior_row, jnp.exp(log), 0.0)
        entering = entering + rows_ref[k, 0:SLICE, :].astype(jnp.float32)
        prior_row = last
    for k in range(RING):
        out_ref[k, 0:SLICE, :] = memory.astype(jnp.bfloat16)
        out_ref[k, SLICE:ROWS, :] = jnp.broadcast_to(prior, (16, HD)).astype(jnp.bfloat16)
        log, last = read_meta(states_ref[k, SLICE:ROWS, :])
        memory = memory * jnp.where(last == prior, jnp.exp(log), 0.0)
        memory = memory + states_ref[k, 0:SLICE, :].astype(jnp.float32)
        prior = last


def attend_kernel(
    log_in, doc_in, query_in, key_in, value_in, out_ref, down_ref,
    log, doc, query_ref, key_ref, value_ref, stage, mask, sems,
):
    copies = fetch(
        (log_in, doc_in, query_in, key_in, value_in), (log, doc, query_ref, key_ref, value_ref), sems
    )
    copies[0].wait()
    copies[1].wait()
    across, down = running(log[...], doc[...], stage)
    down_ref[...] = down
    doc_down = down[:, HEADS : HEADS + 1]
    row = lax.broadcasted_iota(jnp.int32, (BLOCK, BLOCK), 0)
    column = lax.broadcasted_iota(jnp.int32, (BLOCK, BLOCK), 1)
    seen = jnp.logical_and(row >= column, doc_down == across[HEADS : HEADS + 1, :])
    mask[...] = jnp.where(seen, 0.0, -1e30)
    part_rows = BLOCK // 2
    for copy in copies[2:]:
        copy.wait()
    for h in range(HEADS):
        span = slice(h * HD, (h + 1) * HD)
        for i in range(2):
            rows = slice(i * part_rows, (i + 1) * part_rows)
            seen = slice(0, (i + 1) * part_rows)
            scores = dot(query_ref[rows, span], key_ref[seen, span], NT)
            gap = down[rows, h : h + 1] - across[h : h + 1, seen] + mask[rows, seen]
            weighted = (scores * jnp.exp(gap)).astype(jnp.bfloat16)
            out_ref[rows, span] = dot(weighted, value_ref[seen, span])


def finish_kernel(
    down_in, memory_in, gain_in, query_in, local_in, out_ref,
    down_ref, memory_ref, gain_ref, query_ref, local_ref, sems,
):
    copies = fetch(
        (down_in, memory_in, gain_in, query_in, local_in),
        (down_ref, memory_ref, gain_ref, query_ref, local_ref),
        sems,
    )
    for copy in copies[:3]:
        copy.wait()
    down = down_ref[...]
    prior = memory_ref[0, SLICE : SLICE + 16, :].astype(jnp.float32)[0:1, 0:1]
    reach = jnp.where(down[:, HEADS : HEADS + 1] == prior, jnp.exp(down), 0.0)
    for copy in copies[3:]:
        copy.wait()
    for h in range(HEADS):
        span = slice(h * HD, (h + 1) * HD)
        memory = jnp.concatenate([memory_ref[2 * h, 0:SLICE, :], memory_ref[2 * h + 1, 0:SLICE, :]], axis=0)
        heads = local_ref[:, span] + reach[:, h : h + 1] * dot(query_ref[:, span], memory)
        scale = lax.rsqrt(jnp.mean(heads * heads, axis=-1, keepdims=True) + 1e-06)
        out_ref[:, span] = (heads * scale * gain_ref[:, span]).astype(jnp.bfloat16)


def unpack(held, s):
    return jnp.concatenate(
        [held[s, :, 64 * j : 64 * (j + 1), :].reshape(BLOCK, HD) for j in range(4)], axis=1
    )


def project_kernel(*refs):
    sources, (weight_in, out_ref, total, blocks, held, sems) = refs[:RING], refs[RING:]
    chips = lax.axis_size("x")
    x, c = lax.axis_index("x"), lax.axis_index("c")
    half = BLOCK // 2
    copies = []
    for s in range(RING):
        place = 2 * lax.rem(x + (0, -1, 1, 2)[s // 2] + chips, chips) + (1 - c if s % 2 else c)
        copies.append([pltpu.make_async_copy(weight_in.at[place], held.at[s], sems.at[s, 0])])
        copies[s].append(pltpu.make_async_copy(sources[s], blocks.at[s], sems.at[s, 1]))
        for copy in copies[s]:
            copy.start()
    for s in range(RING):
        for copy in copies[s]:
            copy.wait()
        for t in range(2):
            rows = slice(t * half, (t + 1) * half)
            product = dot(blocks[s, rows], unpack(held, s))
            if s == 0:
                total[rows] = product
            elif s < RING - 1:
                total[rows] += product
            else:
                out_ref[rows, :] = (total[rows] + product).astype(jnp.bfloat16)


def call(kernel, out_shape, args, specs, scratch=(), flops=0, transcendentals=0, grant=16):
    return pl.pallas_call(
        kernel,
        out_shape=out_shape,
        in_specs=specs,
        out_specs=jax.tree.map(lambda _: VMEM, out_shape),
        scratch_shapes=list(scratch),
        compiler_params=pltpu.CompilerParams(vmem_limit_bytes=grant * 2**20),
        cost_estimate=pl.CostEstimate(flops=flops, bytes_accessed=2**20, transcendentals=transcendentals),
    )(*args)


def local(sizes, queries, key_rows, value_rows, log_decay, doc_ids, head_gain, out_weight):
    nx = sizes[2]
    shape = lambda *dims: jax.ShapeDtypeStruct(dims, jnp.bfloat16)
    docs, gains = doc_ids.reshape(1, BLOCK), head_gain.reshape(1, -1)
    wide = pltpu.VMEM(queries.shape, jnp.bfloat16)
    logs_held = pltpu.VMEM(log_decay.shape, jnp.float32)
    docs_held = pltpu.VMEM(docs.shape, jnp.int32)
    stage = pltpu.VMEM((8, BLOCK), jnp.float32)

    states = call(
        state_kernel,
        shape(RING, FULL, HD),
        (log_decay, docs, key_rows, value_rows, out_weight),
        [ANY] * 5,
        [logs_held, docs_held, wide, wide, pltpu.VMEM(out_weight.shape, jnp.bfloat16), stage, pltpu.SemaphoreType.DMA((5,))],
        10**8,
        4096,
        GRANT,
    )
    states = lax.all_to_all(states, "z", 0, 0, tiled=True)
    rows, weight = call(
        row_kernel, (shape(RING, ROWS, HD), shape(RING, 256, HD)), (states,), [VMEM]
    )
    weight = lax.all_gather(weight, "y")
    rows = lax.all_to_all(rows, "y", 0, 0, tiled=True)
    entering = call(
        enter_kernel, shape(RING, ROWS, HD), (states, rows), [VMEM, VMEM]
    )
    entering = lax.all_to_all(entering, "z", 0, 0, tiled=True)

    alone, down = call(
        attend_kernel,
        (jax.ShapeDtypeStruct(queries.shape, jnp.float32), jax.ShapeDtypeStruct((BLOCK, 8), jnp.float32)),
        (log_decay, docs, queries, key_rows, value_rows),
        [ANY] * 5,
        [logs_held, docs_held, wide, wide, wide, stage, pltpu.VMEM((BLOCK, BLOCK), jnp.float32)]
        + [pltpu.SemaphoreType.DMA((5,))],
        6 * 10**8,
        2**20,
        GRANT,
    )
    normed = call(
        finish_kernel,
        shape(*queries.shape),
        (down, entering, gains, queries, alone),
        [ANY] * 5,
        [
            pltpu.VMEM(down.shape, jnp.float32),
            pltpu.VMEM(entering.shape, jnp.bfloat16),
            pltpu.VMEM(gains.shape, jnp.float32),
            wide,
            pltpu.VMEM(alone.shape, jnp.float32),
            pltpu.SemaphoreType.DMA((5,)),
        ],
        10**8,
        0,
        GRANT,
    )

    right = [(i, (i + 1) % nx) for i in range(nx)]
    left = [(i, (i - 1) % nx) for i in range(nx)]
    before = lax.ppermute(normed, "x", right)
    after = lax.ppermute(normed, "x", left)
    half = BLOCK // 2
    far_one = lax.ppermute(before[:half], "x", right)
    far_two = lax.ppermute(after[half:], "x", left)
    cross = lambda block: lax.ppermute(block, "c", [(0, 1), (1, 0)])

    near = [normed, cross(normed), before, cross(before), after, cross(after)]
    far = jnp.concatenate([far_one, far_two])
    far = [far, cross(far)]
    return call(
        project_kernel,
        shape(*queries.shape),
        (*near, *far, weight),
        [ANY] * 9,
        [
            pltpu.VMEM(queries.shape, jnp.float32),
            pltpu.VMEM((RING, *queries.shape), jnp.bfloat16),
            pltpu.VMEM(weight.shape, jnp.bfloat16),
            pltpu.SemaphoreType.DMA((RING, 2)),
        ],
        2 * 10**9,
        0,
        GRANT,
    )


def solution(mesh):
    sizes = (8, 8, 4, 2)
    split = Mesh(mesh.devices.reshape(sizes), ALL)
    ctx, tp = ("y", "z"), ("x", "c")
    return jax.shard_map(
        lambda *args: local(sizes, *args),
        mesh=split,
        in_specs=(P(ctx, tp), P(ctx, tp), P(ctx, tp), P(tp, ctx), P(ctx), P(tp), P(ctx, tp)),
        out_specs=P(ctx, tp),
        check_vma=False,
    )
```

time: 148 us -> 120 us (0.81)
  the two profiles are of different devices: /device:TPU:25 before, /device:TPU:1 now
where the time goes in v3:
time: 120 us; the launch traced here: 119 us
  blocking collectives  45.3 us (38%)
  starting transfers between devices  31 us (26%)
  Pallas kernels  17 us (14%)
  between operations  13.6 us (11%)
  waiting for transfers between devices  9.69 us (8%)
  local copies, waits for them, and re-layouts  2.51 us (2%)
    all_to_all x1, blocking collectives, local(): states = lax.all_to_all(states, 'z', 0, 0, tiled=True)  30.3 us
    pallas_call x6, Pallas kernels, call(): pl.pallas_call(kernel, out_shape=out_shape, in_specs=specs, out_specs=jax...  17 us
    all_to_all x1, blocking collectives, local(): rows = lax.all_to_all(rows, 'y', 0, 0, tiled=True)  15 us
    ppermute x4, starting transfers between devices, local(): cross = lambda block: lax.ppermute(block, 'c', [(0, 1), (1, 0)])  14.6 us
    ppermute x1, waiting for transfers between devices, local(): before = lax.ppermute(normed, 'x', right)  5.24 us
    ppermute x1, starting transfers between devices, local(): far_two = lax.ppermute(after[half:], 'x', left)  4.57 us
    all_to_all x1, waiting for transfers between devices, local(): entering = lax.all_to_all(entering, 'z', 0, 0, tiled=True)  4.21 us
    all_to_all x1, starting transfers between devices, local(): entering = lax.all_to_all(entering, 'z', 0, 0, tiled=True)  3.38 us
  transfers between devices with their start and end apart: 10, of which 3 were waited for; matrix products, arithmetic and copies ran while one was open for 0% of the time, Pallas kernels for 7%

profile of v3, /device:TPU:1, one launch (start us, length us, event | category | flops | bytes accessed | tf_op | source)
XLA Modules:
  0.0 119.1 jit_solution(6981327800910901285)
XLA Ops:
  6.5 3.3 %shard_map.74 = bf16[8,336,128]{2,1,0:T(8,128)(2,1)} custom-call(f32[4,512]{1,0:T(4,128)} %log_in.3, s32[1,512]{1,0:T(1,128)} %bitcast.4, bf16[512,512]{1,0:T(8,128)(2,1)} %key_in.3, bf16[512,512]{1,0:T(8,128)(2,1)} %value_in.3, bf16[64,512]{1,0:T(8,128)(2,1)} %weight_in.1), custom_call_target="tpu_custom_call" | custom-call | flops 100000000 | bytes 1048576 | tf_op jit(solution)/shard_map/pallas_call | solution.py:222
  9.9 30.3 %all_to_all.15.states_ref = bf16[8,336,128]{2,1,0:T(8,128)(2,1)S(1)} all-to-all(bf16[8,336,128]{2,1,0:T(8,128)(2,1)} %shard_map.74), channel_id=1, replica_groups=mesh['y'=8,'z'=8,'x'=4,'c'=2] {'z'}, dimensions={0} | all-to-all | bytes 1376256 | tf_op jit(solution)/shard_map/all_to_all | solution.py:252
  40.2 0.8 shard_map.75
  41.1 15.0 %all_to_all.16.rows_ref = bf16[8,80,128]{2,1,0:T(8,128)(2,1)S(1)} all-to-all(bf16[8,80,128]{2,1,0:T(8,128)(2,1)S(1)} %get-tuple-element.10), channel_id=1, replica_groups=mesh['y'=8,'z'=8,'x'=4,'c'=2] {'y'}, dimensions={0} | all-to-all | bytes 327680 | tf_op jit(solution)/shard_map/all_to_all | solution.py:257
  56.0 0.8 shard_map.76
  56.8 3.4 %all-to-all-start.2 = ((bf16[8,80,128]{2,1,0:T(8,128)(2,1)}), bf16[8,80,128]{2,1,0:T(8,128)(2,1)S(1)}, u32[]{:S(2)}, u32[]{:S(2)}) async-start(bf16[8,80,128]{2,1,0:T(8,128)(2,1)} %shard_map.76), calls=%async_computation.2 | async-start | bytes 327680 | tf_op jit(solution)/shard_map/all_to_all | solution.py:261
  60.2 4.0 %shard_map.73 = (f32[512,512]{1,0:T(8,128)}, f32[512,8]{1,0:T(8,128)}) custom-call(f32[4,512]{1,0:T(4,128)} %log_in.3, s32[1,512]{1,0:T(1,128)} %bitcast.5, bf16[512,512]{1,0:T(8,128)(2,1)} %query_in.3, bf16[512,512]{1,0:T(8,128)(2,1)} %key_in.3, bf16[512,512]{1,0:T(8,128)(2,1)} %value_in.3), custom_call_target="tpu_custom_call" | custom-call | flops 600000000 | bytes 1048576 | tf_op jit(solution)/shard_map/pallas_call | solution.py:222
  64.2 4.2 %all-to-all-done.2.memory_in = bf16[8,80,128]{2,1,0:T(8,128)(2,1)S(1)} async-done(((bf16[8,80,128]{2,1,0:T(8,128)(2,1)}), bf16[8,80,128]{2,1,0:T(8,128)(2,1)S(1)}, u32[]{:S(2)}, u32[]{:S(2)}) %all-to-all-start.2) | async-done | bytes 163872 | tf_op jit(solution)/shard_map/all_to_all | solution.py:261
  68.4 0.7 copy-done.3
  69.0 3.3 %shard_map.77.refs_0_ = bf16[512,512]{1,0:T(8,128)(2,1)} custom-call(f32[512,8]{1,0:T(8,128)} %get-tuple-element.9.down_in, bf16[8,80,128]{2,1,0:T(8,128)(2,1)} %copy-done.3, f32[1,512]{1,0:T(1,128)} %bitcast.6, bf16[512,512]{1,0:T(8,128)(2,1)} %query_in.3, f32[512,512]{1,0:T(8,128)} %get-tuple-element.11.local_in), custom_call_target="tpu_custom_call" | custom-call | flops 100000000 | bytes 1048576 | tf_op jit(solution)/shard_map/pallas_call | solution.py:222
  72.3 3.1 %collective-permute-start.1 = (bf16[512,512]{1,0:T(8,128)(2,1)}, bf16[512,512]{1,0:T(8,128)(2,1)S(1)}, u32[]{:S(2)}, u32[]{:S(2)}) collective-permute-start(bf16[512,512]{1,0:T(8,128)(2,1)} %shard_map.77.refs_0_), channel_id=1, source_target_pairs={{0,2},{2,4},{4,6},{6,0},{1,3},{3,5},{5,7},{7,1},{8,10},{10,12},{12... | collective-permute-start | bytes 1572872 | tf_op jit(solution)/shard_map/ppermute | solution.py:294
  75.4 3.4 %collective-permute-start.3 = (bf16[512,512]{1,0:T(8,128)(2,1)}, bf16[512,512]{1,0:T(8,128)(2,1)S(1)}, u32[]{:S(2)}, u32[]{:S(2)}) collective-permute-start(bf16[512,512]{1,0:T(8,128)(2,1)} %shard_map.77.refs_0_), channel_id=1, source_target_pairs={{0,6},{2,0},{4,2},{6,4},{1,7},{3,1},{5,3},{7,5},{8,14},{10,8},{12,... | collective-permute-start | bytes 1572872 | tf_op jit(solution)/shard_map/ppermute | solution.py:295
  78.8 5.2 %collective-permute-done.1.refs_2_ = bf16[512,512]{1,0:T(8,128)(2,1)S(1)} collective-permute-done((bf16[512,512]{1,0:T(8,128)(2,1)}, bf16[512,512]{1,0:T(8,128)(2,1)S(1)}, u32[]{:S(2)}, u32[]{:S(2)}) %collective-permute-start.1) | collective-permute-done | bytes 524320 | tf_op jit(solution)/shard_map/ppermute | solution.py:294
  84.1 1.9 %collective-permute-start.5 = (bf16[256,512]{1,0:T(8,128)(2,1)S(1)}, bf16[256,512]{1,0:T(8,128)(2,1)S(1)}, u32[]{:S(2)}, u32[]{:S(2)}) collective-permute-start(bf16[256,512]{1,0:T(8,128)(2,1)S(1)} %slice.8), channel_id=1, source_target_pairs={{0,2},{2,4},{4,6},{6,0},{1,3},{3,5},{5,7},{7,1},{8,10},{10,12},{12... | collective-permute-start | bytes 786440 | tf_op jit(solution)/shard_map/ppermute | solution.py:297
  86.1 4.6 %collective-permute-start.6 = (bf16[256,512]{1,0:T(8,128)(2,1)S(1)}, bf16[256,512]{1,0:T(8,128)(2,1)S(1)}, u32[]{:S(2)}, u32[]{:S(2)}) collective-permute-start(bf16[256,512]{1,0:T(8,128)(2,1)S(1)} %slice.9), channel_id=1, source_target_pairs={{0,6},{2,0},{4,2},{6,4},{1,7},{3,1},{5,3},{7,5},{8,14},{10,8},{12,... | collective-permute-start | bytes 786440 | tf_op jit(solution)/shard_map/ppermute | solution.py:298
  90.6 8.4 %collective-permute-start = (bf16[512,512]{1,0:T(8,128)(2,1)}, bf16[512,512]{1,0:T(8,128)(2,1)S(1)}, u32[]{:S(2)}, u32[]{:S(2)}) collective-permute-start(bf16[512,512]{1,0:T(8,128)(2,1)} %shard_map.77.refs_0_), channel_id=1, source_target_pairs={{0,1},{1,0},{2,3},{3,2},{4,5},{5,4},{6,7},{7,6},{8,9},{9,8},{10,11... | collective-permute-start | bytes 1572872 | tf_op jit(solution)/shard_map/ppermute | solution.py:299
  99.0 1.9 %collective-permute-start.4 = (bf16[512,512]{1,0:T(8,128)(2,1)S(1)}, bf16[512,512]{1,0:T(8,128)(2,1)S(1)}, u32[]{:S(2)}, u32[]{:S(2)}) collective-permute-start(bf16[512,512]{1,0:T(8,128)(2,1)S(1)} %collective-permute-done.3.refs_4_), channel_id=1, source_target_pairs={{0,1},{1,0},{2,3},{3,2},{4,5},{5,4},{6,7},{7,6},{8,9},{9,8},{10,11... | collective-permute-start | bytes 1572872 | tf_op jit(solution)/shard_map/ppermute | solution.py:299
  101.0 2.4 %collective-permute-start.2 = (bf16[512,512]{1,0:T(8,128)(2,1)S(1)}, bf16[512,512]{1,0:T(8,128)(2,1)S(1)}, u32[]{:S(2)}, u32[]{:S(2)}) collective-permute-start(bf16[512,512]{1,0:T(8,128)(2,1)S(1)} %collective-permute-done.1.refs_2_), channel_id=1, source_target_pairs={{0,1},{1,0},{2,3},{3,2},{4,5},{5,4},{6,7},{7,6},{8,9},{9,8},{10,11... | collective-permute-start | bytes 1572872 | tf_op jit(solution)/shard_map/ppermute | solution.py:299
  103.5 1.9 %collective-permute-start.7 = (bf16[512,512]{1,0:T(8,128)(2,1)S(1)}, bf16[512,512]{1,0:T(8,128)(2,1)}, u32[]{:S(2)}, u32[]{:S(2)}) collective-permute-start(bf16[512,512]{1,0:T(8,128)(2,1)S(1)} %constant_dynamic-update-slice_fusion.refs_6_), channel_id=1, source_target_pairs={{0,1},{1,0},{2,3},{3,2},{4,5},{5,4},{6,7},{7,6},{8,9},{9,8},{10,11... | collective-permute-start | bytes 1572872 | tf_op jit(solution)/shard_map/ppermute | solution.py:299
  105.4 0.8 copy-done.4
  106.2 0.2 copy-done.5
  106.4 0.8 copy-done.6
  107.2 0.2 collective-permute-done.7.refs_7_
  107.4 4.9 %shard_map.78 = bf16[512,512]{1,0:T(8,128)(2,1)} custom-call(bf16[512,512]{1,0:T(8,128)(2,1)} %shard_map.77.refs_0_, bf16[512,512]{1,0:T(8,128)(2,1)} %copy-done.4, bf16[512,512]{1,0:T(8,128)(2,1)} %copy-done, bf16[512,512]{1,0:T(8,128)(2,1)} %copy-done.6, bf16[512,512]{1,0:T(8,128)(2,1)} %copy-done.1, bf16[512,512]{1,0:T(8,128)(2,1)} %copy-done.5, ...), custom_call_target="tpu_custom_call" | custom-call | flops 2000000000 | bytes 1048576 | tf_op jit(solution)/shard_map/pallas_call | solution.py:222
  (23 shorter events, 0.1 us)
Async XLA Ops:
  6.5 100.9 %all-gather.3.cloned.1.call-start = ((), (), s32[]{:S(2)}) async-start(), calls=%async_computation.3 | async-start | bytes 4718592 | tf_op jit(solution)/shard_map/all_gather | solution.py:256
  56.8 11.6 %all-to-all-start.2 = ((bf16[8,80,128]{2,1,0:T(8,128)(2,1)}), bf16[8,80,128]{2,1,0:T(8,128)(2,1)S(1)}, u32[]{:S(2)}, u32[]{:S(2)}) async-start(bf16[8,80,128]{2,1,0:T(8,128)(2,1)} %shard_map.76), calls=%async_computation.2 | async-start | bytes 327680 | tf_op jit(solution)/shard_map/all_to_all | solution.py:261
  68.4 0.7 copy-start.3
  72.3 11.7 %collective-permute-start.1 = (bf16[512,512]{1,0:T(8,128)(2,1)}, bf16[512,512]{1,0:T(8,128)(2,1)S(1)}, u32[]{:S(2)}, u32[]{:S(2)}) collective-permute-start(bf16[512,512]{1,0:T(8,128)(2,1)} %shard_map.77.refs_0_), channel_id=1, source_target_pairs={{0,2},{2,4},{4,6},{6,0},{1,3},{3,5},{5,7},{7,1},{8,10},{10,12},{12... | collective-permute-start | bytes 1572872 | tf_op jit(solution)/shard_map/ppermute | solution.py:294
  75.4 10.6 %collective-permute-start.3 = (bf16[512,512]{1,0:T(8,128)(2,1)}, bf16[512,512]{1,0:T(8,128)(2,1)S(1)}, u32[]{:S(2)}, u32[]{:S(2)}) collective-permute-start(bf16[512,512]{1,0:T(8,128)(2,1)} %shard_map.77.refs_0_), channel_id=1, source_target_pairs={{0,6},{2,0},{4,2},{6,4},{1,7},{3,1},{5,3},{7,5},{8,14},{10,8},{12,... | collective-permute-start | bytes 1572872 | tf_op jit(solution)/shard_map/ppermute | solution.py:295
  84.1 23.3 %copy-start = (bf16[512,512]{1,0:T(8,128)(2,1)}, bf16[512,512]{1,0:T(8,128)(2,1)S(1)}, u32[]{:S(2)}) copy-start(bf16[512,512]{1,0:T(8,128)(2,1)S(1)} %collective-permute-done.1.refs_2_) | copy-start | bytes 1572868
  84.1 19.3 %collective-permute-start.5 = (bf16[256,512]{1,0:T(8,128)(2,1)S(1)}, bf16[256,512]{1,0:T(8,128)(2,1)S(1)}, u32[]{:S(2)}, u32[]{:S(2)}) collective-permute-start(bf16[256,512]{1,0:T(8,128)(2,1)S(1)} %slice.8), channel_id=1, source_target_pairs={{0,2},{2,4},{4,6},{6,0},{1,3},{3,5},{5,7},{7,1},{8,10},{10,12},{12... | collective-permute-start | bytes 786440 | tf_op jit(solution)/shard_map/ppermute | solution.py:297
  86.0 21.4 %copy-start.1 = (bf16[512,512]{1,0:T(8,128)(2,1)}, bf16[512,512]{1,0:T(8,128)(2,1)S(1)}, u32[]{:S(2)}) copy-start(bf16[512,512]{1,0:T(8,128)(2,1)S(1)} %collective-permute-done.3.refs_4_) | copy-start | bytes 1572868
  86.1 17.3 %collective-permute-start.6 = (bf16[256,512]{1,0:T(8,128)(2,1)S(1)}, bf16[256,512]{1,0:T(8,128)(2,1)S(1)}, u32[]{:S(2)}, u32[]{:S(2)}) collective-permute-start(bf16[256,512]{1,0:T(8,128)(2,1)S(1)} %slice.9), channel_id=1, source_target_pairs={{0,6},{2,0},{4,2},{6,4},{1,7},{3,1},{5,3},{7,5},{8,14},{10,8},{12,... | collective-permute-start | bytes 786440 | tf_op jit(solution)/shard_map/ppermute | solution.py:298
  90.6 14.7 %collective-permute-start = (bf16[512,512]{1,0:T(8,128)(2,1)}, bf16[512,512]{1,0:T(8,128)(2,1)S(1)}, u32[]{:S(2)}, u32[]{:S(2)}) collective-permute-start(bf16[512,512]{1,0:T(8,128)(2,1)} %shard_map.77.refs_0_), channel_id=1, source_target_pairs={{0,1},{1,0},{2,3},{3,2},{4,5},{5,4},{6,7},{7,6},{8,9},{9,8},{10,11... | collective-permute-start | bytes 1572872 | tf_op jit(solution)/shard_map/ppermute | solution.py:299
  99.0 6.4 %collective-permute-start.4 = (bf16[512,512]{1,0:T(8,128)(2,1)S(1)}, bf16[512,512]{1,0:T(8,128)(2,1)S(1)}, u32[]{:S(2)}, u32[]{:S(2)}) collective-permute-start(bf16[512,512]{1,0:T(8,128)(2,1)S(1)} %collective-permute-done.3.refs_4_), channel_id=1, source_target_pairs={{0,1},{1,0},{2,3},{3,2},{4,5},{5,4},{6,7},{7,6},{8,9},{9,8},{10,11... | collective-permute-start | bytes 1572872 | tf_op jit(solution)/shard_map/ppermute | solution.py:299
  101.0 4.5 %collective-permute-start.2 = (bf16[512,512]{1,0:T(8,128)(2,1)S(1)}, bf16[512,512]{1,0:T(8,128)(2,1)S(1)}, u32[]{:S(2)}, u32[]{:S(2)}) collective-permute-start(bf16[512,512]{1,0:T(8,128)(2,1)S(1)} %collective-permute-done.1.refs_2_), channel_id=1, source_target_pairs={{0,1},{1,0},{2,3},{3,2},{4,5},{5,4},{6,7},{7,6},{8,9},{9,8},{10,11... | collective-permute-start | bytes 1572872 | tf_op jit(solution)/shard_map/ppermute | solution.py:299
  103.4 4.0 %copy-start.2 = (bf16[512,512]{1,0:T(8,128)(2,1)}, bf16[512,512]{1,0:T(8,128)(2,1)S(1)}, u32[]{:S(2)}) copy-start(bf16[512,512]{1,0:T(8,128)(2,1)S(1)} %constant_dynamic-update-slice_fusion.refs_6_) | copy-start | bytes 1572868
  103.5 3.9 %collective-permute-start.7 = (bf16[512,512]{1,0:T(8,128)(2,1)S(1)}, bf16[512,512]{1,0:T(8,128)(2,1)}, u32[]{:S(2)}, u32[]{:S(2)}) collective-permute-start(bf16[512,512]{1,0:T(8,128)(2,1)S(1)} %constant_dynamic-update-slice_fusion.refs_6_), channel_id=1, source_target_pairs={{0,1},{1,0},{2,3},{3,2},{4,5},{5,4},{6,7},{7,6},{8,9},{9,8},{10,11... | collective-permute-start | bytes 1572872 | tf_op jit(solution)/shard_map/ppermute | solution.py:299
  105.4 0.8 copy-start.4
  105.4 1.0 copy-start.5
  106.4 0.8 copy-start.6
Sparse Core Ops, SparseCore 0:
  41.2 55.9 all-gather.2

commit v4 on v3

--- a/solution.py
+++ b/solution.py
@@ -133,7 +133,7 @@
 
 
 def attend_kernel(
-    log_in, doc_in, query_in, key_in, value_in, out_ref, down_ref,
+    log_in, doc_in, query_in, key_in, value_in, out_ref, across_ref,
     log, doc, query_ref, key_ref, value_ref, stage, mask, sems,
 ):
     copies = fetch(
@@ -142,7 +142,7 @@
     copies[0].wait()
     copies[1].wait()
     across, down = running(log[...], doc[...], stage)
-    down_ref[...] = down
+    across_ref[...] = across
     doc_down = down[:, HEADS : HEADS + 1]
     row = lax.broadcasted_iota(jnp.int32, (BLOCK, BLOCK), 0)
     column = lax.broadcasted_iota(jnp.int32, (BLOCK, BLOCK), 1)
@@ -159,29 +159,29 @@
             scores = dot(query_ref[rows, span], key_ref[seen, span], NT)
             gap = down[rows, h : h + 1] - across[h : h + 1, seen] + mask[rows, seen]
             weighted = (scores * jnp.exp(gap)).astype(jnp.bfloat16)
-            out_ref[rows, span] = dot(weighted, value_ref[seen, span])
+            out_ref[rows, span] = dot(weighted, value_ref[seen, span]).astype(jnp.bfloat16)
 
 
 def finish_kernel(
-    down_in, memory_in, gain_in, query_in, local_in, out_ref,
-    down_ref, memory_ref, gain_ref, query_ref, local_ref, sems,
+    across_in, memory_in, gain_in, query_in, local_in, out_ref,
+    across_ref, memory_ref, gain_ref, query_ref, local_ref, sems,
 ):
     copies = fetch(
-        (down_in, memory_in, gain_in, query_in, local_in),
-        (down_ref, memory_ref, gain_ref, query_ref, local_ref),
+        (across_in, memory_in, gain_in, query_in, local_in),
+        (across_ref, memory_ref, gain_ref, query_ref, local_ref),
         sems,
     )
     for copy in copies[:3]:
         copy.wait()
-    down = down_ref[...]
+    across = across_ref[...]
     prior = memory_ref[0, SLICE : SLICE + 16, :].astype(jnp.float32)[0:1, 0:1]
-    reach = jnp.where(down[:, HEADS : HEADS + 1] == prior, jnp.exp(down), 0.0)
+    reach = jnp.transpose(jnp.where(across[HEADS : HEADS + 1, :] == prior, jnp.exp(across), 0.0))
     for copy in copies[3:]:
         copy.wait()
     for h in range(HEADS):
         span = slice(h * HD, (h + 1) * HD)
         memory = jnp.concatenate([memory_ref[2 * h, 0:SLICE, :], memory_ref[2 * h + 1, 0:SLICE, :]], axis=0)
-        heads = local_ref[:, span] + reach[:, h : h + 1] * dot(query_ref[:, span], memory)
+        heads = local_ref[:, span].astype(jnp.float32) + reach[:, h : h + 1] * dot(query_ref[:, span], memory)
         scale = lax.rsqrt(jnp.mean(heads * heads, axis=-1, keepdims=True) + 1e-06)
         out_ref[:, span] = (heads * scale * gain_ref[:, span]).astype(jnp.bfloat16)
 
@@ -260,9 +260,9 @@
     )
     entering = lax.all_to_all(entering, "z", 0, 0, tiled=True)
 
-    alone, down = call(
+    alone, across = call(
         attend_kernel,
-        (jax.ShapeDtypeStruct(queries.shape, jnp.float32), jax.ShapeDtypeStruct((BLOCK, 8), jnp.float32)),
+        (shape(*queries.shape), jax.ShapeDtypeStruct((8, BLOCK), jnp.float32)),
         (log_decay, docs, queries, key_rows, value_rows),
         [ANY] * 5,
         [logs_held, docs_held, wide, wide, wide, stage, pltpu.VMEM((BLOCK, BLOCK), jnp.float32)]
@@ -274,32 +274,29 @@
     normed = call(
         finish_kernel,
         shape(*queries.shape),
-        (down, entering, gains, queries, alone),
+        (across, entering, gains, queries, alone),
         [ANY] * 5,
         [
-            pltpu.VMEM(down.shape, jnp.float32),
+            pltpu.VMEM(across.shape, jnp.float32),
             pltpu.VMEM(entering.shape, jnp.bfloat16),
             pltpu.VMEM(gains.shape, jnp.float32),
             wide,
-            pltpu.VMEM(alone.shape, jnp.float32),
+            wide,
             pltpu.SemaphoreType.DMA((5,)),
         ],
         10**8,
         0,
-        GRANT,
+        32,
     )
 
     right = [(i, (i + 1) % nx) for i in range(nx)]
     left = [(i, (i - 1) % nx) for i in range(nx)]
     before = lax.ppermute(normed, "x", right)
     after = lax.ppermute(normed, "x", left)
-    half = BLOCK // 2
-    far_one = lax.ppermute(before[:half], "x", right)
-    far_two = lax.ppermute(after[half:], "x", left)
+    far = lax.ppermute(before, "x", right)
     cross = lambda block: lax.ppermute(block, "c", [(0, 1), (1, 0)])
 
     near = [normed, cross(normed), before, cross(before), after, cross(after)]
-    far = jnp.concatenate([far_one, far_two])
     far = [far, cross(far)]
     return call(
         project_kernel,

time: 120 us -> 117 us (0.975)
  Pallas kernels: 17 us -> 14.9 us
    ppermute x2 -> x1, starting transfers between devices: 6.49 us -> 1.91 us  [local(): far = lax.ppermute(before, 'x', right)]
    ppermute x4, starting transfers between devices: 14.6 us -> 18.1 us  [local(): cross = lambda block: lax.ppermute(block, 'c', [(0, 1), (1, 0)])]
    pallas_call x6, Pallas kernels: 17 us -> 14.9 us  [call(): pl.pallas_call(kernel, out_shape=out_shape, in_specs=specs, out_specs=jax...]
    unnamed x15 -> x22, local copies, waits for them, and re-layouts: 2.45 us -> 3.54 us
  transfers between devices with their start and end apart: 10 -> 9, of which waited for: 3 -> 2; matrix products, arithmetic and copies ran while one was open for 0% -> 0% of each run, Pallas kernels for 7% -> 5%
where the time goes in v4:
time: 117 us
  blocking collectives  45.3 us (39%)
  starting transfers between devices  29.9 us (26%)
  Pallas kernels  14.9 us (13%)
  between operations  13.6 us (12%)
  waiting for transfers between devices  9.45 us (8%)
  local copies, waits for them, and re-layouts  3.54 us (3%)
    all_to_all x1, blocking collectives, local(): states = lax.all_to_all(states, 'z', 0, 0, tiled=True)  30.3 us
    ppermute x4, starting transfers between devices, local(): cross = lambda block: lax.ppermute(block, 'c', [(0, 1), (1, 0)])  18.1 us
    all_to_all x1, blocking collectives, local(): rows = lax.all_to_all(rows, 'y', 0, 0, tiled=True)  15 us
    pallas_call x6, Pallas kernels, call(): pl.pallas_call(kernel, out_shape=out_shape, in_specs=specs, out_specs=jax...  14.9 us
    ppermute x1, waiting for transfers between devices, local(): before = lax.ppermute(normed, 'x', right)  5.03 us
    all_to_all x1, waiting for transfers between devices, local(): entering = lax.all_to_all(entering, 'z', 0, 0, tiled=True)  4.39 us
    unnamed x22, local copies, waits for them, and re-layouts  3.54 us
    all_to_all x1, starting transfers between devices, local(): entering = lax.all_to_all(entering, 'z', 0, 0, tiled=True)  3.38 us
  transfers between devices with their start and end apart: 9, of which 2 were waited for; matrix products, arithmetic and copies ran while one was open for 0% of the time, Pallas kernels for 5%

profile of v4, /device:TPU:1, one launch (start us, length us, event | category | flops | bytes accessed | tf_op | source)
XLA Modules:
  0.0 116.8 jit_solution(13341427464830328994)
XLA Ops:
  6.5 3.3 %shard_map.74 = bf16[8,336,128]{2,1,0:T(8,128)(2,1)} custom-call(f32[4,512]{1,0:T(4,128)} %log_in.3, s32[1,512]{1,0:T(1,128)} %bitcast.5, bf16[512,512]{1,0:T(8,128)(2,1)} %key_in.3, bf16[512,512]{1,0:T(8,128)(2,1)} %value_in.3, bf16[64,512]{1,0:T(8,128)(2,1)} %weight_in.1), custom_call_target="tpu_custom_call" | custom-call | flops 100000000 | bytes 1048576 | tf_op jit(solution)/shard_map/pallas_call | solution.py:222
  9.9 30.3 %all_to_all.15.states_ref = bf16[8,336,128]{2,1,0:T(8,128)(2,1)S(1)} all-to-all(bf16[8,336,128]{2,1,0:T(8,128)(2,1)} %shard_map.74), channel_id=1, replica_groups=mesh['y'=8,'z'=8,'x'=4,'c'=2] {'z'}, dimensions={0} | all-to-all | bytes 1376256 | tf_op jit(solution)/shard_map/all_to_all | solution.py:252
  40.2 0.8 shard_map.75
  41.1 0.0 all-gather.3.cloned.1.call-update
  41.1 15.0 %all_to_all.16.rows_ref = bf16[8,80,128]{2,1,0:T(8,128)(2,1)S(1)} all-to-all(bf16[8,80,128]{2,1,0:T(8,128)(2,1)S(1)} %get-tuple-element.10), channel_id=1, replica_groups=mesh['y'=8,'z'=8,'x'=4,'c'=2] {'y'}, dimensions={0} | all-to-all | bytes 327680 | tf_op jit(solution)/shard_map/all_to_all | solution.py:257
  56.1 0.7 shard_map.76
  56.9 3.4 %all-to-all-start.2 = ((bf16[8,80,128]{2,1,0:T(8,128)(2,1)}), bf16[8,80,128]{2,1,0:T(8,128)(2,1)S(1)}, u32[]{:S(2)}, u32[]{:S(2)}) async-start(bf16[8,80,128]{2,1,0:T(8,128)(2,1)} %shard_map.76), calls=%async_computation.2 | async-start | bytes 327680 | tf_op jit(solution)/shard_map/all_to_all | solution.py:261
  60.2 3.8 %shard_map.73 = (bf16[512,512]{1,0:T(8,128)(2,1)}, f32[8,512]{1,0:T(8,128)}) custom-call(f32[4,512]{1,0:T(4,128)} %log_in.3, s32[1,512]{1,0:T(1,128)} %bitcast.6, bf16[512,512]{1,0:T(8,128)(2,1)} %query_in.3, bf16[512,512]{1,0:T(8,128)(2,1)} %key_in.3, bf16[512,512]{1,0:T(8,128)(2,1)} %value_in.3), custom_call_target="tpu_custom_call" | custom-call | flops 600000000 | bytes 1048576 | tf_op jit(solution)/shard_map/pallas_call | solution.py:222
  64.0 4.4 %all-to-all-done.2.memory_in = bf16[8,80,128]{2,1,0:T(8,128)(2,1)S(1)} async-done(((bf16[8,80,128]{2,1,0:T(8,128)(2,1)}), bf16[8,80,128]{2,1,0:T(8,128)(2,1)S(1)}, u32[]{:S(2)}, u32[]{:S(2)}) %all-to-all-start.2) | async-done | bytes 163872 | tf_op jit(solution)/shard_map/all_to_all | solution.py:261
  68.4 1.0 copy-done.2
  69.5 0.7 copy-done.3
  70.2 1.4 %shard_map.77.refs_0_ = bf16[512,512]{1,0:T(8,128)(2,1)S(1)} custom-call(f32[8,512]{1,0:T(8,128)S(1)} %copy-done.3, bf16[8,80,128]{2,1,0:T(8,128)(2,1)S(1)} %all-to-all-done.2.memory_in, f32[1,512]{1,0:T(1,128)S(1)} %bitcast.3, bf16[512,512]{1,0:T(8,128)(2,1)S(1)} %copy-done.1, bf16[512,512]{1,0:T(8,128)(2,1)S(1)} %copy-done.2), custom_call_target="tpu_custom_call" | custom-call | flops 100000000 | bytes 1048576 | tf_op jit(solution)/shard_map/pallas_call | solution.py:222
  71.6 3.1 %collective-permute-start.1 = (bf16[512,512]{1,0:T(8,128)(2,1)S(1)}, bf16[512,512]{1,0:T(8,128)(2,1)S(1)}, u32[]{:S(2)}, u32[]{:S(2)}) collective-permute-start(bf16[512,512]{1,0:T(8,128)(2,1)S(1)} %shard_map.77.refs_0_), channel_id=1, source_target_pairs={{0,2},{2,4},{4,6},{6,0},{1,3},{3,5},{5,7},{7,1},{8,10},{10,12},{12... | collective-permute-start | bytes 1572872 | tf_op jit(solution)/shard_map/ppermute | solution.py:294
  74.7 3.4 %collective-permute-start.3 = (bf16[512,512]{1,0:T(8,128)(2,1)S(1)}, bf16[512,512]{1,0:T(8,128)(2,1)S(1)}, u32[]{:S(2)}, u32[]{:S(2)}) collective-permute-start(bf16[512,512]{1,0:T(8,128)(2,1)S(1)} %shard_map.77.refs_0_), channel_id=1, source_target_pairs={{0,6},{2,0},{4,2},{6,4},{1,7},{3,1},{5,3},{7,5},{8,14},{10,8},{12,... | collective-permute-start | bytes 1572872 | tf_op jit(solution)/shard_map/ppermute | solution.py:295
  78.1 5.0 %collective-permute-done.1.refs_2_ = bf16[512,512]{1,0:T(8,128)(2,1)S(1)} collective-permute-done((bf16[512,512]{1,0:T(8,128)(2,1)S(1)}, bf16[512,512]{1,0:T(8,128)(2,1)S(1)}, u32[]{:S(2)}, u32[]{:S(2)}) %collective-permute-start.1) | collective-permute-done | bytes 524320 | tf_op jit(solution)/shard_map/ppermute | solution.py:294
  83.1 1.9 %collective-permute-start.5 = (bf16[512,512]{1,0:T(8,128)(2,1)S(1)}, bf16[512,512]{1,0:T(8,128)(2,1)S(1)}, u32[]{:S(2)}, u32[]{:S(2)}) collective-permute-start(bf16[512,512]{1,0:T(8,128)(2,1)S(1)} %collective-permute-done.1.refs_2_), channel_id=1, source_target_pairs={{0,2},{2,4},{4,6},{6,0},{1,3},{3,5},{5,7},{7,1},{8,10},{10,12},{12... | collective-permute-start | bytes 1572872 | tf_op jit(solution)/shard_map/ppermute | solution.py:296
  85.0 8.9 %collective-permute-start = (bf16[512,512]{1,0:T(8,128)(2,1)S(1)}, bf16[512,512]{1,0:T(8,128)(2,1)S(1)}, u32[]{:S(2)}, u32[]{:S(2)}) collective-permute-start(bf16[512,512]{1,0:T(8,128)(2,1)S(1)} %shard_map.77.refs_0_), channel_id=1, source_target_pairs={{0,1},{1,0},{2,3},{3,2},{4,5},{5,4},{6,7},{7,6},{8,9},{9,8},{10,11... | collective-permute-start | bytes 1572872 | tf_op jit(solution)/shard_map/ppermute | solution.py:297
  94.0 1.9 %collective-permute-start.2 = (bf16[512,512]{1,0:T(8,128)(2,1)S(1)}, bf16[512,512]{1,0:T(8,128)(2,1)S(1)}, u32[]{:S(2)}, u32[]{:S(2)}) collective-permute-start(bf16[512,512]{1,0:T(8,128)(2,1)S(1)} %collective-permute-done.1.refs_2_), channel_id=1, source_target_pairs={{0,1},{1,0},{2,3},{3,2},{4,5},{5,4},{6,7},{7,6},{8,9},{9,8},{10,11... | collective-permute-start | bytes 1572872 | tf_op jit(solution)/shard_map/ppermute | solution.py:297
  95.9 2.4 %collective-permute-start.4 = (bf16[512,512]{1,0:T(8,128)(2,1)S(1)}, bf16[512,512]{1,0:T(8,128)(2,1)S(1)}, u32[]{:S(2)}, u32[]{:S(2)}) collective-permute-start(bf16[512,512]{1,0:T(8,128)(2,1)S(1)} %collective-permute-done.3.refs_4_), channel_id=1, source_target_pairs={{0,1},{1,0},{2,3},{3,2},{4,5},{5,4},{6,7},{7,6},{8,9},{9,8},{10,11... | collective-permute-start | bytes 1572872 | tf_op jit(solution)/shard_map/ppermute | solution.py:297
  98.3 4.8 %collective-permute-start.6 = (bf16[512,512]{1,0:T(8,128)(2,1)S(1)}, bf16[512,512]{1,0:T(8,128)(2,1)}, u32[]{:S(2)}, u32[]{:S(2)}) collective-permute-start(bf16[512,512]{1,0:T(8,128)(2,1)S(1)} %collective-permute-done.5.refs_6_), channel_id=1, source_target_pairs={{0,1},{1,0},{2,3},{3,2},{4,5},{5,4},{6,7},{7,6},{8,9},{9,8},{10,11... | collective-permute-start | bytes 1572872 | tf_op jit(solution)/shard_map/ppermute | solution.py:297
  103.3 0.8 copy-done.8
  104.0 0.2 copy-done.10
  104.2 0.8 copy-done.9
  105.0 4.9 %shard_map.78 = bf16[512,512]{1,0:T(8,128)(2,1)} custom-call(bf16[512,512]{1,0:T(8,128)(2,1)} %copy-done, bf16[512,512]{1,0:T(8,128)(2,1)} %copy-done.8, bf16[512,512]{1,0:T(8,128)(2,1)} %copy-done.5, bf16[512,512]{1,0:T(8,128)(2,1)} %copy-done.9, bf16[512,512]{1,0:T(8,128)(2,1)} %copy-done.6, bf16[512,512]{1,0:T(8,128)(2,1)} %copy-done.10, ...), custom_call_target="tpu_custom_call" | custom-call | flops 2000000000 | bytes 1048576 | tf_op jit(solution)/shard_map/pallas_call | solution.py:222
  (25 shorter events, 0.1 us)
Async XLA Ops:
  6.5 61.9 %copy-start.1 = (bf16[512,512]{1,0:T(8,128)(2,1)S(1)}, bf16[512,512]{1,0:T(8,128)(2,1)}, u32[]{:S(2)}) copy-start(bf16[512,512]{1,0:T(8,128)(2,1)} %query_in.3) | copy-start | bytes 1572868
  6.5 61.9 %copy-start.4 = (f32[512]{0:T(512)S(1)}, f32[512]{0:T(512)}, u32[]{:S(2)}) copy-start(f32[512]{0:T(512)} %param.12) | copy-start | bytes 6148
  6.5 98.5 %all-gather.3.cloned.1.call-start = ((), (), s32[]{:S(2)}) async-start(), calls=%async_computation.3 | async-start | bytes 4718592 | tf_op jit(solution)/shard_map/all_gather | solution.py:256
  56.9 11.6 %all-to-all-start.2 = ((bf16[8,80,128]{2,1,0:T(8,128)(2,1)}), bf16[8,80,128]{2,1,0:T(8,128)(2,1)S(1)}, u32[]{:S(2)}, u32[]{:S(2)}) async-start(bf16[8,80,128]{2,1,0:T(8,128)(2,1)} %shard_map.76), calls=%async_computation.2 | async-start | bytes 327680 | tf_op jit(solution)/shard_map/all_to_all | solution.py:261
  68.4 1.0 copy-start.2
  69.5 0.7 copy-start.3
  71.6 33.5 %copy-start = (bf16[512,512]{1,0:T(8,128)(2,1)}, bf16[512,512]{1,0:T(8,128)(2,1)S(1)}, u32[]{:S(2)}) copy-start(bf16[512,512]{1,0:T(8,128)(2,1)S(1)} %shard_map.77.refs_0_) | copy-start | bytes 1572868
  71.6 11.5 %collective-permute-start.1 = (bf16[512,512]{1,0:T(8,128)(2,1)S(1)}, bf16[512,512]{1,0:T(8,128)(2,1)S(1)}, u32[]{:S(2)}, u32[]{:S(2)}) collective-permute-start(bf16[512,512]{1,0:T(8,128)(2,1)S(1)} %shard_map.77.refs_0_), channel_id=1, source_target_pairs={{0,2},{2,4},{4,6},{6,0},{1,3},{3,5},{5,7},{7,1},{8,10},{10,12},{12... | collective-permute-start | bytes 1572872 | tf_op jit(solution)/shard_map/ppermute | solution.py:294
  74.7 21.2 %collective-permute-start.3 = (bf16[512,512]{1,0:T(8,128)(2,1)S(1)}, bf16[512,512]{1,0:T(8,128)(2,1)S(1)}, u32[]{:S(2)}, u32[]{:S(2)}) collective-permute-start(bf16[512,512]{1,0:T(8,128)(2,1)S(1)} %shard_map.77.refs_0_), channel_id=1, source_target_pairs={{0,6},{2,0},{4,2},{6,4},{1,7},{3,1},{5,3},{7,5},{8,14},{10,8},{12,... | collective-permute-start | bytes 1572872 | tf_op jit(solution)/shard_map/ppermute | solution.py:295
  83.1 21.9 %copy-start.5 = (bf16[512,512]{1,0:T(8,128)(2,1)}, bf16[512,512]{1,0:T(8,128)(2,1)S(1)}, u32[]{:S(2)}) copy-start(bf16[512,512]{1,0:T(8,128)(2,1)S(1)} %collective-permute-done.1.refs_2_) | copy-start | bytes 1572868
  83.1 15.2 %collective-permute-start.5 = (bf16[512,512]{1,0:T(8,128)(2,1)S(1)}, bf16[512,512]{1,0:T(8,128)(2,1)S(1)}, u32[]{:S(2)}, u32[]{:S(2)}) collective-permute-start(bf16[512,512]{1,0:T(8,128)(2,1)S(1)} %collective-permute-done.1.refs_2_), channel_id=1, source_target_pairs={{0,2},{2,4},{4,6},{6,0},{1,3},{3,5},{5,7},{7,1},{8,10},{10,12},{12... | collective-permute-start | bytes 1572872 | tf_op jit(solution)/shard_map/ppermute | solution.py:296
  85.0 18.2 %collective-permute-start = (bf16[512,512]{1,0:T(8,128)(2,1)S(1)}, bf16[512,512]{1,0:T(8,128)(2,1)S(1)}, u32[]{:S(2)}, u32[]{:S(2)}) collective-permute-start(bf16[512,512]{1,0:T(8,128)(2,1)S(1)} %shard_map.77.refs_0_), channel_id=1, source_target_pairs={{0,1},{1,0},{2,3},{3,2},{4,5},{5,4},{6,7},{7,6},{8,9},{9,8},{10,11... | collective-permute-start | bytes 1572872 | tf_op jit(solution)/shard_map/ppermute | solution.py:297
  94.0 9.3 %collective-permute-start.2 = (bf16[512,512]{1,0:T(8,128)(2,1)S(1)}, bf16[512,512]{1,0:T(8,128)(2,1)S(1)}, u32[]{:S(2)}, u32[]{:S(2)}) collective-permute-start(bf16[512,512]{1,0:T(8,128)(2,1)S(1)} %collective-permute-done.1.refs_2_), channel_id=1, source_target_pairs={{0,1},{1,0},{2,3},{3,2},{4,5},{5,4},{6,7},{7,6},{8,9},{9,8},{10,11... | collective-permute-start | bytes 1572872 | tf_op jit(solution)/shard_map/ppermute | solution.py:297
  95.9 9.1 %copy-start.6 = (bf16[512,512]{1,0:T(8,128)(2,1)}, bf16[512,512]{1,0:T(8,128)(2,1)S(1)}, u32[]{:S(2)}) copy-start(bf16[512,512]{1,0:T(8,128)(2,1)S(1)} %collective-permute-done.3.refs_4_) | copy-start | bytes 1572868
  95.9 7.3 %collective-permute-start.4 = (bf16[512,512]{1,0:T(8,128)(2,1)S(1)}, bf16[512,512]{1,0:T(8,128)(2,1)S(1)}, u32[]{:S(2)}, u32[]{:S(2)}) collective-permute-start(bf16[512,512]{1,0:T(8,128)(2,1)S(1)} %collective-permute-done.3.refs_4_), channel_id=1, source_target_pairs={{0,1},{1,0},{2,3},{3,2},{4,5},{5,4},{6,7},{7,6},{8,9},{9,8},{10,11... | collective-permute-start | bytes 1572872 | tf_op jit(solution)/shard_map/ppermute | solution.py:297
  98.3 4.9 %copy-start.7 = (bf16[512,512]{1,0:T(8,128)(2,1)}, bf16[512,512]{1,0:T(8,128)(2,1)S(1)}, u32[]{:S(2)}) copy-start(bf16[512,512]{1,0:T(8,128)(2,1)S(1)} %collective-permute-done.5.refs_6_) | copy-start | bytes 1572868
  98.3 6.7 %collective-permute-start.6 = (bf16[512,512]{1,0:T(8,128)(2,1)S(1)}, bf16[512,512]{1,0:T(8,128)(2,1)}, u32[]{:S(2)}, u32[]{:S(2)}) collective-permute-start(bf16[512,512]{1,0:T(8,128)(2,1)S(1)} %collective-permute-done.5.refs_6_), channel_id=1, source_target_pairs={{0,1},{1,0},{2,3},{3,2},{4,5},{5,4},{6,7},{7,6},{8,9},{9,8},{10,11... | collective-permute-start | bytes 1572872 | tf_op jit(solution)/shard_map/ppermute | solution.py:297
  103.2 0.8 copy-start.8
  103.2 1.0 copy-start.10
  104.2 0.8 copy-start.9
Sparse Core Ops, SparseCore 0:
  41.2 55.9 all-gather.2

commit v5 on v4

--- a/solution.py
+++ b/solution.py
@@ -269,7 +269,7 @@
         + [pltpu.SemaphoreType.DMA((5,))],
         6 * 10**8,
         2**20,
-        GRANT,
+        32,
     )
     normed = call(
         finish_kernel,
@@ -311,7 +311,7 @@
         ],
         2 * 10**9,
         0,
-        GRANT,
+        58,
     )
 
 

time: 117 us -> 116 us (level)
  local copies, waits for them, and re-layouts: 3.54 us -> 0.88 us
  waiting for transfers between devices: 9.45 us -> 11.5 us
  Pallas kernels: 14.9 us -> 13.7 us
    unnamed x22 -> x26, local copies, waits for them, and re-layouts: 3.54 us -> 0.88 us
    all_to_all x1, waiting for transfers between devices: 4.39 us -> 5.72 us  [local(): entering = lax.all_to_all(entering, 'z', 0, 0, tiled=True)]
    pallas_call x6, Pallas kernels: 14.9 us -> 13.7 us  [call(): pl.pallas_call(kernel, out_shape=out_shape, in_specs=specs, out_specs=jax...]
  transfers between devices with their start and end apart: 9 -> 9, of which waited for: 2 -> 3; matrix products, arithmetic and copies ran while one was open for 0% -> 0% of each run, Pallas kernels for 5% -> 4%
where the time goes in v5:
time: 116 us; the launch traced here: 115 us
  blocking collectives  45.3 us (39%)
  starting transfers between devices  29.9 us (26%)
  Pallas kernels  13.7 us (12%)
  between operations  13.7 us (12%)
  waiting for transfers between devices  11.5 us (10%)
    all_to_all x1, blocking collectives, local(): states = lax.all_to_all(states, 'z', 0, 0, tiled=True)  30.3 us
    ppermute x4, starting transfers between devices, local(): cross = lambda block: lax.ppermute(block, 'c', [(0, 1), (1, 0)])  18.1 us
    all_to_all x1, blocking collectives, local(): rows = lax.all_to_all(rows, 'y', 0, 0, tiled=True)  15 us
    pallas_call x6, Pallas kernels, call(): pl.pallas_call(kernel, out_shape=out_shape, in_specs=specs, out_specs=jax...  13.7 us
    all_to_all x1, waiting for transfers between devices, local(): entering = lax.all_to_all(entering, 'z', 0, 0, tiled=True)  5.72 us
    ppermute x1, waiting for transfers between devices, local(): before = lax.ppermute(normed, 'x', right)  5.03 us
    all_to_all x1, starting transfers between devices, local(): entering = lax.all_to_all(entering, 'z', 0, 0, tiled=True)  3.38 us
    ppermute x1, starting transfers between devices, local(): after = lax.ppermute(normed, 'x', left)  3.38 us
  transfers between devices with their start and end apart: 9, of which 3 were waited for; matrix products, arithmetic and copies ran while one was open for 0% of the time, Pallas kernels for 4%

profile of v5, /device:TPU:1, one launch (start us, length us, event | category | flops | bytes accessed | tf_op | source)
XLA Modules:
  0.0 115.0 jit_solution(15399872937397345580)
XLA Ops:
  6.6 0.0 all-gather.3.cloned.1.call-start
  6.6 3.4 %shard_map.74 = bf16[8,336,128]{2,1,0:T(8,128)(2,1)} custom-call(f32[4,512]{1,0:T(4,128)} %log_in.3, s32[1,512]{1,0:T(1,128)} %bitcast.4, bf16[512,512]{1,0:T(8,128)(2,1)} %key_in.3, bf16[512,512]{1,0:T(8,128)(2,1)} %value_in.3, bf16[64,512]{1,0:T(8,128)(2,1)} %weight_in.1), custom_call_target="tpu_custom_call" | custom-call | flops 100000000 | bytes 1048576 | tf_op jit(solution)/shard_map/pallas_call | solution.py:222
  10.0 30.3 %all_to_all.15.states_ref = bf16[8,336,128]{2,1,0:T(8,128)(2,1)S(1)} all-to-all(bf16[8,336,128]{2,1,0:T(8,128)(2,1)} %shard_map.74), channel_id=1, replica_groups=mesh['y'=8,'z'=8,'x'=4,'c'=2] {'z'}, dimensions={0} | all-to-all | bytes 1376256 | tf_op jit(solution)/shard_map/all_to_all | solution.py:252
  40.4 0.8 shard_map.75
  41.2 0.0 all-gather.3.cloned.1.call-update
  41.2 15.0 %all_to_all.16.rows_ref = bf16[8,80,128]{2,1,0:T(8,128)(2,1)S(1)} all-to-all(bf16[8,80,128]{2,1,0:T(8,128)(2,1)S(1)} %get-tuple-element.10), channel_id=1, replica_groups=mesh['y'=8,'z'=8,'x'=4,'c'=2] {'y'}, dimensions={0} | all-to-all | bytes 327680 | tf_op jit(solution)/shard_map/all_to_all | solution.py:257
  56.2 0.8 shard_map.76
  57.0 3.4 %all-to-all-start.2 = ((bf16[8,80,128]{2,1,0:T(8,128)(2,1)}), bf16[8,80,128]{2,1,0:T(8,128)(2,1)S(1)}, u32[]{:S(2)}, u32[]{:S(2)}) async-start(bf16[8,80,128]{2,1,0:T(8,128)(2,1)} %shard_map.76), calls=%async_computation.2 | async-start | bytes 327680 | tf_op jit(solution)/shard_map/all_to_all | solution.py:261
  60.4 2.4 %shard_map.73 = (bf16[512,512]{1,0:T(8,128)(2,1)S(1)}, f32[8,512]{1,0:T(8,128)S(1)}) custom-call(f32[4,512]{1,0:T(4,128)S(1)} %copy-done.4, s32[1,512]{1,0:T(1,128)S(1)} %bitcast.5, bf16[512,512]{1,0:T(8,128)(2,1)S(1)} %copy-done.3, bf16[512,512]{1,0:T(8,128)(2,1)S(1)} %copy-done.1, bf16[512,512]{1,0:T(8,128)(2,1)S(1)} %copy-done.2), custom_call_target="tpu_custom_call" | custom-call | flops 600000000 | bytes 1048576 | tf_op jit(solution)/shard_map/pallas_call | solution.py:222
  62.8 5.7 %all-to-all-done.2.memory_in = bf16[8,80,128]{2,1,0:T(8,128)(2,1)S(1)} async-done(((bf16[8,80,128]{2,1,0:T(8,128)(2,1)}), bf16[8,80,128]{2,1,0:T(8,128)(2,1)S(1)}, u32[]{:S(2)}, u32[]{:S(2)}) %all-to-all-start.2) | async-done | bytes 163872 | tf_op jit(solution)/shard_map/all_to_all | solution.py:261
  68.5 1.4 %shard_map.77.refs_0_ = bf16[512,512]{1,0:T(8,128)(2,1)S(1)} custom-call(f32[8,512]{1,0:T(8,128)S(1)} %get-tuple-element.9.across_in, bf16[8,80,128]{2,1,0:T(8,128)(2,1)S(1)} %all-to-all-done.2.memory_in, f32[1,512]{1,0:T(1,128)S(1)} %bitcast.3, bf16[512,512]{1,0:T(8,128)(2,1)S(1)} %copy-done.3, bf16[512,512]{1,0:T(8,128)(2,1)S(1)} %get-tuple-element.11.local_in), custom_call_target="tpu_custom_call" | custom-call | flops 100000000 | bytes 1048576 | tf_op jit(solution)/shard_map/pallas_call | solution.py:222
  69.9 3.1 %collective-permute-start.1 = (bf16[512,512]{1,0:T(8,128)(2,1)S(1)}, bf16[512,512]{1,0:T(8,128)(2,1)S(1)}, u32[]{:S(2)}, u32[]{:S(2)}) collective-permute-start(bf16[512,512]{1,0:T(8,128)(2,1)S(1)} %shard_map.77.refs_0_), channel_id=1, source_target_pairs={{0,2},{2,4},{4,6},{6,0},{1,3},{3,5},{5,7},{7,1},{8,10},{10,12},{12... | collective-permute-start | bytes 1572872 | tf_op jit(solution)/shard_map/ppermute | solution.py:294
  73.1 3.4 %collective-permute-start.3 = (bf16[512,512]{1,0:T(8,128)(2,1)S(1)}, bf16[512,512]{1,0:T(8,128)(2,1)S(1)}, u32[]{:S(2)}, u32[]{:S(2)}) collective-permute-start(bf16[512,512]{1,0:T(8,128)(2,1)S(1)} %shard_map.77.refs_0_), channel_id=1, source_target_pairs={{0,6},{2,0},{4,2},{6,4},{1,7},{3,1},{5,3},{7,5},{8,14},{10,8},{12,... | collective-permute-start | bytes 1572872 | tf_op jit(solution)/shard_map/ppermute | solution.py:295
  76.4 5.0 %collective-permute-done.1.refs_2_ = bf16[512,512]{1,0:T(8,128)(2,1)S(1)} collective-permute-done((bf16[512,512]{1,0:T(8,128)(2,1)S(1)}, bf16[512,512]{1,0:T(8,128)(2,1)S(1)}, u32[]{:S(2)}, u32[]{:S(2)}) %collective-permute-start.1) | collective-permute-done | bytes 524320 | tf_op jit(solution)/shard_map/ppermute | solution.py:294
  81.5 1.9 %collective-permute-start.5 = (bf16[512,512]{1,0:T(8,128)(2,1)S(1)}, bf16[512,512]{1,0:T(8,128)(2,1)S(1)}, u32[]{:S(2)}, u32[]{:S(2)}) collective-permute-start(bf16[512,512]{1,0:T(8,128)(2,1)S(1)} %collective-permute-done.1.refs_2_), channel_id=1, source_target_pairs={{0,2},{2,4},{4,6},{6,0},{1,3},{3,5},{5,7},{7,1},{8,10},{10,12},{12... | collective-permute-start | bytes 1572872 | tf_op jit(solution)/shard_map/ppermute | solution.py:296
  83.4 8.9 %collective-permute-start = (bf16[512,512]{1,0:T(8,128)(2,1)S(1)}, bf16[512,512]{1,0:T(8,128)(2,1)S(1)}, u32[]{:S(2)}, u32[]{:S(2)}) collective-permute-start(bf16[512,512]{1,0:T(8,128)(2,1)S(1)} %shard_map.77.refs_0_), channel_id=1, source_target_pairs={{0,1},{1,0},{2,3},{3,2},{4,5},{5,4},{6,7},{7,6},{8,9},{9,8},{10,11... | collective-permute-start | bytes 1572872 | tf_op jit(solution)/shard_map/ppermute | solution.py:297
  92.3 1.9 %collective-permute-start.2 = (bf16[512,512]{1,0:T(8,128)(2,1)S(1)}, bf16[512,512]{1,0:T(8,128)(2,1)S(1)}, u32[]{:S(2)}, u32[]{:S(2)}) collective-permute-start(bf16[512,512]{1,0:T(8,128)(2,1)S(1)} %collective-permute-done.1.refs_2_), channel_id=1, source_target_pairs={{0,1},{1,0},{2,3},{3,2},{4,5},{5,4},{6,7},{7,6},{8,9},{9,8},{10,11... | collective-permute-start | bytes 1572872 | tf_op jit(solution)/shard_map/ppermute | solution.py:297
  94.3 2.4 %collective-permute-start.4 = (bf16[512,512]{1,0:T(8,128)(2,1)S(1)}, bf16[512,512]{1,0:T(8,128)(2,1)S(1)}, u32[]{:S(2)}, u32[]{:S(2)}) collective-permute-start(bf16[512,512]{1,0:T(8,128)(2,1)S(1)} %collective-permute-done.3.refs_4_), channel_id=1, source_target_pairs={{0,1},{1,0},{2,3},{3,2},{4,5},{5,4},{6,7},{7,6},{8,9},{9,8},{10,11... | collective-permute-start | bytes 1572872 | tf_op jit(solution)/shard_map/ppermute | solution.py:297
  96.7 4.9 %collective-permute-start.6 = (bf16[512,512]{1,0:T(8,128)(2,1)S(1)}, bf16[512,512]{1,0:T(8,128)(2,1)}, u32[]{:S(2)}, u32[]{:S(2)}) collective-permute-start(bf16[512,512]{1,0:T(8,128)(2,1)S(1)} %collective-permute-done.5.refs_6_), channel_id=1, source_target_pairs={{0,1},{1,0},{2,3},{3,2},{4,5},{5,4},{6,7},{7,6},{8,9},{9,8},{10,11... | collective-permute-start | bytes 1572872 | tf_op jit(solution)/shard_map/ppermute | solution.py:297
  101.6 0.0 collective-permute-done.4.refs_5_
  101.6 0.8 copy-done.12
  102.4 0.8 collective-permute-done.6.refs_7_
  103.2 0.0 copy-done.11
  103.3 4.9 %shard_map.78 = bf16[512,512]{1,0:T(8,128)(2,1)} custom-call(bf16[512,512]{1,0:T(8,128)(2,1)} %copy-done, bf16[512,512]{1,0:T(8,128)(2,1)} %copy-done.10, bf16[512,512]{1,0:T(8,128)(2,1)} %copy-done.7, bf16[512,512]{1,0:T(8,128)(2,1)} %copy-done.11, bf16[512,512]{1,0:T(8,128)(2,1)} %copy-done.8, bf16[512,512]{1,0:T(8,128)(2,1)} %copy-done.12, ...), custom_call_target="tpu_custom_call" | custom-call | flops 2000000000 | bytes 1048576 | tf_op jit(solution)/shard_map/pallas_call | solution.py:222
  (29 shorter events, 0.1 us)
Async XLA Ops:
  6.5 53.8 %copy-start.4 = (f32[4,512]{1,0:T(4,128)S(1)}, f32[4,512]{1,0:T(4,128)}, u32[]{:S(2)}) copy-start(f32[4,512]{1,0:T(4,128)} %log_in.3) | copy-start | bytes 24580
  6.5 53.8 %copy-start.2 = (bf16[512,512]{1,0:T(8,128)(2,1)S(1)}, bf16[512,512]{1,0:T(8,128)(2,1)}, u32[]{:S(2)}) copy-start(bf16[512,512]{1,0:T(8,128)(2,1)} %value_in.3) | copy-start | bytes 1572868
  6.5 53.8 %copy-start.1 = (bf16[512,512]{1,0:T(8,128)(2,1)S(1)}, bf16[512,512]{1,0:T(8,128)(2,1)}, u32[]{:S(2)}) copy-start(bf16[512,512]{1,0:T(8,128)(2,1)} %key_in.3) | copy-start | bytes 1572868
  6.5 53.9 %copy-start.6 = (s32[512]{0:T(512)S(1)}, s32[512]{0:T(512)}, u32[]{:S(2)}) copy-start(s32[512]{0:T(512)} %param.11) | copy-start | bytes 6148
  6.5 53.9 %copy-start.3 = (bf16[512,512]{1,0:T(8,128)(2,1)S(1)}, bf16[512,512]{1,0:T(8,128)(2,1)}, u32[]{:S(2)}) copy-start(bf16[512,512]{1,0:T(8,128)(2,1)} %query_in.3) | copy-start | bytes 1572868
  6.5 62.0 %copy-start.5 = (f32[512]{0:T(512)S(1)}, f32[512]{0:T(512)}, u32[]{:S(2)}) copy-start(f32[512]{0:T(512)} %param.12) | copy-start | bytes 6148
  6.6 96.7 %all-gather.3.cloned.1.call-start = ((), (), s32[]{:S(2)}) async-start(), calls=%async_computation.3 | async-start | bytes 4718592 | tf_op jit(solution)/shard_map/all_gather | solution.py:256
  57.0 11.6 %all-to-all-start.2 = ((bf16[8,80,128]{2,1,0:T(8,128)(2,1)}), bf16[8,80,128]{2,1,0:T(8,128)(2,1)S(1)}, u32[]{:S(2)}, u32[]{:S(2)}) async-start(bf16[8,80,128]{2,1,0:T(8,128)(2,1)} %shard_map.76), calls=%async_computation.2 | async-start | bytes 327680 | tf_op jit(solution)/shard_map/all_to_all | solution.py:261
  69.9 33.3 %copy-start = (bf16[512,512]{1,0:T(8,128)(2,1)}, bf16[512,512]{1,0:T(8,128)(2,1)S(1)}, u32[]{:S(2)}) copy-start(bf16[512,512]{1,0:T(8,128)(2,1)S(1)} %shard_map.77.refs_0_) | copy-start | bytes 1572868
  69.9 11.5 %collective-permute-start.1 = (bf16[512,512]{1,0:T(8,128)(2,1)S(1)}, bf16[512,512]{1,0:T(8,128)(2,1)S(1)}, u32[]{:S(2)}, u32[]{:S(2)}) collective-permute-start(bf16[512,512]{1,0:T(8,128)(2,1)S(1)} %shard_map.77.refs_0_), channel_id=1, source_target_pairs={{0,2},{2,4},{4,6},{6,0},{1,3},{3,5},{5,7},{7,1},{8,10},{10,12},{12... | collective-permute-start | bytes 1572872 | tf_op jit(solution)/shard_map/ppermute | solution.py:294
  73.1 21.2 %collective-permute-start.3 = (bf16[512,512]{1,0:T(8,128)(2,1)S(1)}, bf16[512,512]{1,0:T(8,128)(2,1)S(1)}, u32[]{:S(2)}, u32[]{:S(2)}) collective-permute-start(bf16[512,512]{1,0:T(8,128)(2,1)S(1)} %shard_map.77.refs_0_), channel_id=1, source_target_pairs={{0,6},{2,0},{4,2},{6,4},{1,7},{3,1},{5,3},{7,5},{8,14},{10,8},{12,... | collective-permute-start | bytes 1572872 | tf_op jit(solution)/shard_map/ppermute | solution.py:295
  81.5 21.7 %copy-start.7 = (bf16[512,512]{1,0:T(8,128)(2,1)}, bf16[512,512]{1,0:T(8,128)(2,1)S(1)}, u32[]{:S(2)}) copy-start(bf16[512,512]{1,0:T(8,128)(2,1)S(1)} %collective-permute-done.1.refs_2_) | copy-start | bytes 1572868
  81.5 15.2 %collective-permute-start.5 = (bf16[512,512]{1,0:T(8,128)(2,1)S(1)}, bf16[512,512]{1,0:T(8,128)(2,1)S(1)}, u32[]{:S(2)}, u32[]{:S(2)}) collective-permute-start(bf16[512,512]{1,0:T(8,128)(2,1)S(1)} %collective-permute-done.1.refs_2_), channel_id=1, source_target_pairs={{0,2},{2,4},{4,6},{6,0},{1,3},{3,5},{5,7},{7,1},{8,10},{10,12},{12... | collective-permute-start | bytes 1572872 | tf_op jit(solution)/shard_map/ppermute | solution.py:296
  83.4 18.2 %collective-permute-start = (bf16[512,512]{1,0:T(8,128)(2,1)S(1)}, bf16[512,512]{1,0:T(8,128)(2,1)S(1)}, u32[]{:S(2)}, u32[]{:S(2)}) collective-permute-start(bf16[512,512]{1,0:T(8,128)(2,1)S(1)} %shard_map.77.refs_0_), channel_id=1, source_target_pairs={{0,1},{1,0},{2,3},{3,2},{4,5},{5,4},{6,7},{7,6},{8,9},{9,8},{10,11... | collective-permute-start | bytes 1572872 | tf_op jit(solution)/shard_map/ppermute | solution.py:297
  92.3 9.3 %collective-permute-start.2 = (bf16[512,512]{1,0:T(8,128)(2,1)S(1)}, bf16[512,512]{1,0:T(8,128)(2,1)S(1)}, u32[]{:S(2)}, u32[]{:S(2)}) collective-permute-start(bf16[512,512]{1,0:T(8,128)(2,1)S(1)} %collective-permute-done.1.refs_2_), channel_id=1, source_target_pairs={{0,1},{1,0},{2,3},{3,2},{4,5},{5,4},{6,7},{7,6},{8,9},{9,8},{10,11... | collective-permute-start | bytes 1572872 | tf_op jit(solution)/shard_map/ppermute | solution.py:297
  94.3 9.0 %copy-start.8 = (bf16[512,512]{1,0:T(8,128)(2,1)}, bf16[512,512]{1,0:T(8,128)(2,1)S(1)}, u32[]{:S(2)}) copy-start(bf16[512,512]{1,0:T(8,128)(2,1)S(1)} %collective-permute-done.3.refs_4_) | copy-start | bytes 1572868
  94.3 7.3 %collective-permute-start.4 = (bf16[512,512]{1,0:T(8,128)(2,1)S(1)}, bf16[512,512]{1,0:T(8,128)(2,1)S(1)}, u32[]{:S(2)}, u32[]{:S(2)}) collective-permute-start(bf16[512,512]{1,0:T(8,128)(2,1)S(1)} %collective-permute-done.3.refs_4_), channel_id=1, source_target_pairs={{0,1},{1,0},{2,3},{3,2},{4,5},{5,4},{6,7},{7,6},{8,9},{9,8},{10,11... | collective-permute-start | bytes 1572872 | tf_op jit(solution)/shard_map/ppermute | solution.py:297
  96.7 6.5 %copy-start.9 = (bf16[512,512]{1,0:T(8,128)(2,1)}, bf16[512,512]{1,0:T(8,128)(2,1)S(1)}, u32[]{:S(2)}) copy-start(bf16[512,512]{1,0:T(8,128)(2,1)S(1)} %collective-permute-done.5.refs_6_) | copy-start | bytes 1572868
  96.7 6.5 %collective-permute-start.6 = (bf16[512,512]{1,0:T(8,128)(2,1)S(1)}, bf16[512,512]{1,0:T(8,128)(2,1)}, u32[]{:S(2)}, u32[]{:S(2)}) collective-permute-start(bf16[512,512]{1,0:T(8,128)(2,1)S(1)} %collective-permute-done.5.refs_6_), channel_id=1, source_target_pairs={{0,1},{1,0},{2,3},{3,2},{4,5},{5,4},{6,7},{7,6},{8,9},{9,8},{10,11... | collective-permute-start | bytes 1572872 | tf_op jit(solution)/shard_map/ppermute | solution.py:297
  101.6 1.7 %copy-start.10 = (bf16[512,512]{1,0:T(8,128)(2,1)}, bf16[512,512]{1,0:T(8,128)(2,1)S(1)}, u32[]{:S(2)}) copy-start(bf16[512,512]{1,0:T(8,128)(2,1)S(1)} %collective-permute-done.refs_1_) | copy-start | bytes 1572868
  101.6 0.8 copy-start.12
  102.4 0.8 copy-start.11
Sparse Core Ops, SparseCore 0:
  41.3 55.9 all-gather.2

commit v6 on v5

--- a/solution.py
+++ b/solution.py
@@ -190,6 +190,11 @@
     return jnp.concatenate(
         [held[s, :, 64 * j : 64 * (j + 1), :].reshape(BLOCK, HD) for j in range(4)], axis=1
     )
+
+
+def half_kernel(block_ref, crossed_ref, out_ref):
+    del crossed_ref
+    out_ref[...] = block_ref[out_ref.shape[0] :, :]
 
 
 def project_kernel(*refs):
@@ -293,10 +298,15 @@
     left = [(i, (i - 1) % nx) for i in range(nx)]
     before = lax.ppermute(normed, "x", right)
     after = lax.ppermute(normed, "x", left)
-    far = lax.ppermute(before, "x", right)
+    half = BLOCK // 2
+    crossed = lax.ppermute(normed, "c", [(0, 1), (1, 0)])
+    last = call(half_kernel, shape(half, queries.shape[1]), (after, crossed), [VMEM, ANY])
+    far_one = lax.ppermute(before[:half], "x", right)
+    far_two = lax.ppermute(last, "x", left)
     cross = lambda block: lax.ppermute(block, "c", [(0, 1), (1, 0)])
 
-    near = [normed, cross(normed), before, cross(before), after, cross(after)]
+    near = [normed, crossed, before, cross(before), after, cross(after)]
+    far = jnp.concatenate([far_one, far_two])
     far = [far, cross(far)]
     return call(
         project_kernel,

time: 116 us -> 115 us (level)
  waiting for transfers between devices: 11.5 us -> 5.8 us
  starting transfers between devices: 29.9 us -> 34.1 us
    ppermute x1 -> x3, starting transfers between devices: 1.91 us -> 14.1 us  [the longest x1 7.61 us: local(): crossed = lax.ppermute(normed, 'c', [(0, 1), (1, 0)])]
    ppermute x4 -> x3, starting transfers between devices: 18.1 us -> 10.1 us  [local(): cross = lambda block: lax.ppermute(block, 'c', [(0, 1), (1, 0)])]
    ppermute x1, waiting for transfers between devices: 5.03 us -> 0.01 us  [local(): before = lax.ppermute(normed, 'x', right)]
    pallas_call x6 -> x7, Pallas kernels: 13.7 us -> 13.7 us  [call(): pl.pallas_call(kernel, out_shape=out_shape, in_specs=specs, out_specs=jax...]
  transfers between devices with their start and end apart: 9 -> 10, of which waited for: 3 -> 1; matrix products, arithmetic and copies ran while one was open for 0% -> 0% of each run, Pallas kernels for 4% -> 4%
where the time goes in v6:
time: 115 us; the launch traced here: 114 us
  blocking collectives  45.3 us (39%)
  starting transfers between devices  34.1 us (30%)
  Pallas kernels  13.7 us (12%)
  between operations  13.7 us (12%)
  waiting for transfers between devices  5.8 us (5%)
  local copies, waits for them, and re-layouts  1.67 us (1%)
    all_to_all x1, blocking collectives, local(): states = lax.all_to_all(states, 'z', 0, 0, tiled=True)  30.3 us
    all_to_all x1, blocking collectives, local(): rows = lax.all_to_all(rows, 'y', 0, 0, tiled=True)  15 us
    pallas_call x7, Pallas kernels, call(): pl.pallas_call(kernel, out_shape=out_shape, in_specs=specs, out_specs=jax...  13.7 us
    ppermute x3, starting transfers between devices, local(): cross = lambda block: lax.ppermute(block, 'c', [(0, 1), (1, 0)])  10.1 us
    ppermute x1, starting transfers between devices, local(): crossed = lax.ppermute(normed, 'c', [(0, 1), (1, 0)])  7.61 us
    all_to_all x1, waiting for transfers between devices, local(): entering = lax.all_to_all(entering, 'z', 0, 0, tiled=True)  5.72 us
    ppermute x1, starting transfers between devices, local(): far_two = lax.ppermute(last, 'x', left)  4.57 us
    all_to_all x1, starting transfers between devices, local(): entering = lax.all_to_all(entering, 'z', 0, 0, tiled=True)  3.38 us
  transfers between devices with their start and end apart: 10, of which 1 were waited for; matrix products, arithmetic and copies ran while one was open for 0% of the time, Pallas kernels for 4%

profile of v6, /device:TPU:1, one launch (start us, length us, event | category | flops | bytes accessed | tf_op | source)
XLA Modules:
  0.0 114.3 jit_solution(10228084534388269292)
XLA Ops:
  6.6 0.0 all-gather.3.cloned.1.call-start
  6.6 3.4 %shard_map.74 = bf16[8,336,128]{2,1,0:T(8,128)(2,1)} custom-call(f32[4,512]{1,0:T(4,128)} %log_in.3, s32[1,512]{1,0:T(1,128)} %bitcast.4, bf16[512,512]{1,0:T(8,128)(2,1)} %key_in.3, bf16[512,512]{1,0:T(8,128)(2,1)} %value_in.3, bf16[64,512]{1,0:T(8,128)(2,1)} %weight_in.1), custom_call_target="tpu_custom_call" | custom-call | flops 100000000 | bytes 1048576 | tf_op jit(solution)/shard_map/pallas_call | solution.py:227
  10.0 30.3 %all_to_all.15.states_ref = bf16[8,336,128]{2,1,0:T(8,128)(2,1)S(1)} all-to-all(bf16[8,336,128]{2,1,0:T(8,128)(2,1)} %shard_map.74), channel_id=1, replica_groups=mesh['y'=8,'z'=8,'x'=4,'c'=2] {'z'}, dimensions={0} | all-to-all | bytes 1376256 | tf_op jit(solution)/shard_map/all_to_all | solution.py:257
  40.3 0.8 shard_map.75
  41.2 0.0 all-gather.3.cloned.1.call-update
  41.2 15.0 %all_to_all.16.rows_ref = bf16[8,80,128]{2,1,0:T(8,128)(2,1)S(1)} all-to-all(bf16[8,80,128]{2,1,0:T(8,128)(2,1)S(1)} %get-tuple-element.10), channel_id=1, replica_groups=mesh['y'=8,'z'=8,'x'=4,'c'=2] {'y'}, dimensions={0} | all-to-all | bytes 327680 | tf_op jit(solution)/shard_map/all_to_all | solution.py:262
  56.2 0.8 shard_map.76
  57.0 3.4 %all-to-all-start.2 = ((bf16[8,80,128]{2,1,0:T(8,128)(2,1)}), bf16[8,80,128]{2,1,0:T(8,128)(2,1)S(1)}, u32[]{:S(2)}, u32[]{:S(2)}) async-start(bf16[8,80,128]{2,1,0:T(8,128)(2,1)} %shard_map.76), calls=%async_computation.2 | async-start | bytes 327680 | tf_op jit(solution)/shard_map/all_to_all | solution.py:266
  60.4 2.4 %shard_map.73 = (bf16[512,512]{1,0:T(8,128)(2,1)S(1)}, f32[8,512]{1,0:T(8,128)S(1)}) custom-call(f32[4,512]{1,0:T(4,128)S(1)} %copy-done.6, s32[1,512]{1,0:T(1,128)S(1)} %bitcast.5, bf16[512,512]{1,0:T(8,128)(2,1)S(1)} %copy-done.5, bf16[512,512]{1,0:T(8,128)(2,1)S(1)} %copy-done.3, bf16[512,512]{1,0:T(8,128)(2,1)S(1)} %copy-done.4), custom_call_target="tpu_custom_call" | custom-call | flops 600000000 | bytes 1048576 | tf_op jit(solution)/shard_map/pallas_call | solution.py:227
  62.8 5.7 %all-to-all-done.2.memory_in = bf16[8,80,128]{2,1,0:T(8,128)(2,1)S(1)} async-done(((bf16[8,80,128]{2,1,0:T(8,128)(2,1)}), bf16[8,80,128]{2,1,0:T(8,128)(2,1)S(1)}, u32[]{:S(2)}, u32[]{:S(2)}) %all-to-all-start.2) | async-done | bytes 163872 | tf_op jit(solution)/shard_map/all_to_all | solution.py:266
  68.5 1.4 %shard_map.77.refs_0_ = bf16[512,512]{1,0:T(8,128)(2,1)S(1)} custom-call(f32[8,512]{1,0:T(8,128)S(1)} %get-tuple-element.9.across_in, bf16[8,80,128]{2,1,0:T(8,128)(2,1)S(1)} %all-to-all-done.2.memory_in, f32[1,512]{1,0:T(1,128)S(1)} %bitcast.3, bf16[512,512]{1,0:T(8,128)(2,1)S(1)} %copy-done.5, bf16[512,512]{1,0:T(8,128)(2,1)S(1)} %get-tuple-element.11.local_in), custom_call_target="tpu_custom_call" | custom-call | flops 100000000 | bytes 1048576 | tf_op jit(solution)/shard_map/pallas_call | solution.py:227
  69.9 3.1 %collective-permute-start.1 = (bf16[512,512]{1,0:T(8,128)(2,1)S(1)}, bf16[512,512]{1,0:T(8,128)(2,1)S(1)}, u32[]{:S(2)}, u32[]{:S(2)}) collective-permute-start(bf16[512,512]{1,0:T(8,128)(2,1)S(1)} %shard_map.77.refs_0_), channel_id=1, source_target_pairs={{0,2},{2,4},{4,6},{6,0},{1,3},{3,5},{5,7},{7,1},{8,10},{10,12},{12... | collective-permute-start | bytes 1572872 | tf_op jit(solution)/shard_map/ppermute | solution.py:299
  73.0 3.4 %collective-permute-start.3 = (bf16[512,512]{1,0:T(8,128)(2,1)S(1)}, bf16[512,512]{1,0:T(8,128)(2,1)S(1)}, u32[]{:S(2)}, u32[]{:S(2)}) collective-permute-start(bf16[512,512]{1,0:T(8,128)(2,1)S(1)} %shard_map.77.refs_0_), channel_id=1, source_target_pairs={{0,6},{2,0},{4,2},{6,4},{1,7},{3,1},{5,3},{7,5},{8,14},{10,8},{12,... | collective-permute-start | bytes 1572872 | tf_op jit(solution)/shard_map/ppermute | solution.py:300
  76.4 7.6 %collective-permute-start = (bf16[512,512]{1,0:T(8,128)(2,1)S(1)}, bf16[512,512]{1,0:T(8,128)(2,1)S(1)}, u32[]{:S(2)}, u32[]{:S(2)}) collective-permute-start(bf16[512,512]{1,0:T(8,128)(2,1)S(1)} %shard_map.77.refs_0_), channel_id=1, source_target_pairs={{0,1},{1,0},{2,3},{3,2},{4,5},{5,4},{6,7},{7,6},{8,9},{9,8},{10,11... | collective-permute-start | bytes 1572872 | tf_op jit(solution)/shard_map/ppermute | solution.py:302
  84.0 0.0 collective-permute-done.1.refs_2_
  84.1 1.9 %collective-permute-start.5 = (bf16[256,512]{1,0:T(8,128)(2,1)S(1)}, bf16[256,512]{1,0:T(8,128)(2,1)S(1)}, u32[]{:S(2)}, u32[]{:S(2)}) collective-permute-start(bf16[256,512]{1,0:T(8,128)(2,1)S(1)} %slice.4), channel_id=1, source_target_pairs={{0,2},{2,4},{4,6},{6,0},{1,3},{3,5},{5,7},{7,1},{8,10},{10,12},{12... | collective-permute-start | bytes 786440 | tf_op jit(solution)/shard_map/ppermute | solution.py:304
  86.1 4.6 %collective-permute-start.6 = (bf16[256,512]{1,0:T(8,128)(2,1)S(1)}, bf16[256,512]{1,0:T(8,128)(2,1)S(1)}, u32[]{:S(2)}, u32[]{:S(2)}) collective-permute-start(bf16[256,512]{1,0:T(8,128)(2,1)S(1)} %shard_map.78), channel_id=1, source_target_pairs={{0,6},{2,0},{4,2},{6,4},{1,7},{3,1},{5,3},{7,5},{8,14},{10,8},{12,... | collective-permute-start | bytes 786440 | tf_op jit(solution)/shard_map/ppermute | solution.py:305
  90.7 5.8 %collective-permute-start.4 = (bf16[512,512]{1,0:T(8,128)(2,1)S(1)}, bf16[512,512]{1,0:T(8,128)(2,1)S(1)}, u32[]{:S(2)}, u32[]{:S(2)}) collective-permute-start(bf16[512,512]{1,0:T(8,128)(2,1)S(1)} %collective-permute-done.3.block_ref.refs_4_), channel_id=1, source_target_pairs={{0,1},{1,0},{2,3},{3,2},{4,5},{5,4},{6,7},{7,6},{8,9},{9,8},{10,11... | collective-permute-start | bytes 1572872 | tf_op jit(solution)/shard_map/ppermute | solution.py:306
  96.4 1.9 %collective-permute-start.2 = (bf16[512,512]{1,0:T(8,128)(2,1)S(1)}, bf16[512,512]{1,0:T(8,128)(2,1)S(1)}, u32[]{:S(2)}, u32[]{:S(2)}) collective-permute-start(bf16[512,512]{1,0:T(8,128)(2,1)S(1)} %collective-permute-done.1.refs_2_), channel_id=1, source_target_pairs={{0,1},{1,0},{2,3},{3,2},{4,5},{5,4},{6,7},{7,6},{8,9},{9,8},{10,11... | collective-permute-start | bytes 1572872 | tf_op jit(solution)/shard_map/ppermute | solution.py:306
  98.4 2.4 %collective-permute-start.7 = (bf16[512,512]{1,0:T(8,128)(2,1)S(1)}, bf16[512,512]{1,0:T(8,128)(2,1)}, u32[]{:S(2)}, u32[]{:S(2)}) collective-permute-start(bf16[512,512]{1,0:T(8,128)(2,1)S(1)} %constant_dynamic-update-slice_fusion.refs_6_), channel_id=1, source_target_pairs={{0,1},{1,0},{2,3},{3,2},{4,5},{5,4},{6,7},{7,6},{8,9},{9,8},{10,11... | collective-permute-start | bytes 1572872 | tf_op jit(solution)/shard_map/ppermute | solution.py:306
  100.9 0.8 copy-done.11
  101.7 0.8 copy-done.12
  102.5 0.0 collective-permute-done.7.refs_7_
  102.5 4.9 %shard_map.79 = bf16[512,512]{1,0:T(8,128)(2,1)} custom-call(bf16[512,512]{1,0:T(8,128)(2,1)} %copy-done.2, bf16[512,512]{1,0:T(8,128)(2,1)} %copy-done.1, bf16[512,512]{1,0:T(8,128)(2,1)} %copy-done.9, bf16[512,512]{1,0:T(8,128)(2,1)} %copy-done.12, bf16[512,512]{1,0:T(8,128)(2,1)} %copy-done, bf16[512,512]{1,0:T(8,128)(2,1)} %copy-done.11, ...), custom_call_target="tpu_custom_call" | custom-call | flops 2000000000 | bytes 1048576 | tf_op jit(solution)/shard_map/pallas_call | solution.py:227
  (35 shorter events, 0.1 us)
Async XLA Ops:
  6.5 53.8 %copy-start.6 = (f32[4,512]{1,0:T(4,128)S(1)}, f32[4,512]{1,0:T(4,128)}, u32[]{:S(2)}) copy-start(f32[4,512]{1,0:T(4,128)} %log_in.3) | copy-start | bytes 24580
  6.5 53.8 %copy-start.4 = (bf16[512,512]{1,0:T(8,128)(2,1)S(1)}, bf16[512,512]{1,0:T(8,128)(2,1)}, u32[]{:S(2)}) copy-start(bf16[512,512]{1,0:T(8,128)(2,1)} %value_in.3) | copy-start | bytes 1572868
  6.5 53.8 %copy-start.3 = (bf16[512,512]{1,0:T(8,128)(2,1)S(1)}, bf16[512,512]{1,0:T(8,128)(2,1)}, u32[]{:S(2)}) copy-start(bf16[512,512]{1,0:T(8,128)(2,1)} %key_in.3) | copy-start | bytes 1572868
  6.5 53.8 %copy-start.8 = (s32[512]{0:T(512)S(1)}, s32[512]{0:T(512)}, u32[]{:S(2)}) copy-start(s32[512]{0:T(512)} %param.11) | copy-start | bytes 6148
  6.5 53.8 %copy-start.5 = (bf16[512,512]{1,0:T(8,128)(2,1)S(1)}, bf16[512,512]{1,0:T(8,128)(2,1)}, u32[]{:S(2)}) copy-start(bf16[512,512]{1,0:T(8,128)(2,1)} %query_in.3) | copy-start | bytes 1572868
  6.5 62.0 %copy-start.7 = (f32[512]{0:T(512)S(1)}, f32[512]{0:T(512)}, u32[]{:S(2)}) copy-start(f32[512]{0:T(512)} %param.12) | copy-start | bytes 6148
  6.6 96.0 %all-gather.3.cloned.1.call-start = ((), (), s32[]{:S(2)}) async-start(), calls=%async_computation.3 | async-start | bytes 4718592 | tf_op jit(solution)/shard_map/all_gather | solution.py:261
  57.0 11.6 %all-to-all-start.2 = ((bf16[8,80,128]{2,1,0:T(8,128)(2,1)}), bf16[8,80,128]{2,1,0:T(8,128)(2,1)S(1)}, u32[]{:S(2)}, u32[]{:S(2)}) async-start(bf16[8,80,128]{2,1,0:T(8,128)(2,1)} %shard_map.76), calls=%async_computation.2 | async-start | bytes 327680 | tf_op jit(solution)/shard_map/all_to_all | solution.py:266
  69.9 32.6 %copy-start.2 = (bf16[512,512]{1,0:T(8,128)(2,1)}, bf16[512,512]{1,0:T(8,128)(2,1)S(1)}, u32[]{:S(2)}) copy-start(bf16[512,512]{1,0:T(8,128)(2,1)S(1)} %shard_map.77.refs_0_) | copy-start | bytes 1572868
  69.9 14.1 %collective-permute-start.1 = (bf16[512,512]{1,0:T(8,128)(2,1)S(1)}, bf16[512,512]{1,0:T(8,128)(2,1)S(1)}, u32[]{:S(2)}, u32[]{:S(2)}) collective-permute-start(bf16[512,512]{1,0:T(8,128)(2,1)S(1)} %shard_map.77.refs_0_), channel_id=1, source_target_pairs={{0,2},{2,4},{4,6},{6,0},{1,3},{3,5},{5,7},{7,1},{8,10},{10,12},{12... | collective-permute-start | bytes 1572872 | tf_op jit(solution)/shard_map/ppermute | solution.py:299
  73.0 13.0 %collective-permute-start.3 = (bf16[512,512]{1,0:T(8,128)(2,1)S(1)}, bf16[512,512]{1,0:T(8,128)(2,1)S(1)}, u32[]{:S(2)}, u32[]{:S(2)}) collective-permute-start(bf16[512,512]{1,0:T(8,128)(2,1)S(1)} %shard_map.77.refs_0_), channel_id=1, source_target_pairs={{0,6},{2,0},{4,2},{6,4},{1,7},{3,1},{5,3},{7,5},{8,14},{10,8},{12,... | collective-permute-start | bytes 1572872 | tf_op jit(solution)/shard_map/ppermute | solution.py:300
  76.4 9.6 %collective-permute-start = (bf16[512,512]{1,0:T(8,128)(2,1)S(1)}, bf16[512,512]{1,0:T(8,128)(2,1)S(1)}, u32[]{:S(2)}, u32[]{:S(2)}) collective-permute-start(bf16[512,512]{1,0:T(8,128)(2,1)S(1)} %shard_map.77.refs_0_), channel_id=1, source_target_pairs={{0,1},{1,0},{2,3},{3,2},{4,5},{5,4},{6,7},{7,6},{8,9},{9,8},{10,11... | collective-permute-start | bytes 1572872 | tf_op jit(solution)/shard_map/ppermute | solution.py:302
  84.1 18.5 %copy-start.9 = (bf16[512,512]{1,0:T(8,128)(2,1)}, bf16[512,512]{1,0:T(8,128)(2,1)S(1)}, u32[]{:S(2)}) copy-start(bf16[512,512]{1,0:T(8,128)(2,1)S(1)} %collective-permute-done.1.refs_2_) | copy-start | bytes 1572868
  84.1 14.3 %collective-permute-start.5 = (bf16[256,512]{1,0:T(8,128)(2,1)S(1)}, bf16[256,512]{1,0:T(8,128)(2,1)S(1)}, u32[]{:S(2)}, u32[]{:S(2)}) collective-permute-start(bf16[256,512]{1,0:T(8,128)(2,1)S(1)} %slice.4), channel_id=1, source_target_pairs={{0,2},{2,4},{4,6},{6,0},{1,3},{3,5},{5,7},{7,1},{8,10},{10,12},{12... | collective-permute-start | bytes 786440 | tf_op jit(solution)/shard_map/ppermute | solution.py:304
  86.0 16.5 %copy-start = (bf16[512,512]{1,0:T(8,128)(2,1)}, bf16[512,512]{1,0:T(8,128)(2,1)S(1)}, u32[]{:S(2)}) copy-start(bf16[512,512]{1,0:T(8,128)(2,1)S(1)} %collective-permute-done.3.block_ref.refs_4_) | copy-start | bytes 1572868
  86.0 16.5 %copy-start.1 = (bf16[512,512]{1,0:T(8,128)(2,1)}, bf16[512,512]{1,0:T(8,128)(2,1)S(1)}, u32[]{:S(2)}) copy-start(bf16[512,512]{1,0:T(8,128)(2,1)S(1)} %collective-permute-done.crossed_ref.refs_1_) | copy-start | bytes 1572868
  86.1 12.3 %collective-permute-start.6 = (bf16[256,512]{1,0:T(8,128)(2,1)S(1)}, bf16[256,512]{1,0:T(8,128)(2,1)S(1)}, u32[]{:S(2)}, u32[]{:S(2)}) collective-permute-start(bf16[256,512]{1,0:T(8,128)(2,1)S(1)} %shard_map.78), channel_id=1, source_target_pairs={{0,6},{2,0},{4,2},{6,4},{1,7},{3,1},{5,3},{7,5},{8,14},{10,8},{12,... | collective-permute-start | bytes 786440 | tf_op jit(solution)/shard_map/ppermute | solution.py:305
  90.7 10.2 %collective-permute-start.4 = (bf16[512,512]{1,0:T(8,128)(2,1)S(1)}, bf16[512,512]{1,0:T(8,128)(2,1)S(1)}, u32[]{:S(2)}, u32[]{:S(2)}) collective-permute-start(bf16[512,512]{1,0:T(8,128)(2,1)S(1)} %collective-permute-done.3.block_ref.refs_4_), channel_id=1, source_target_pairs={{0,1},{1,0},{2,3},{3,2},{4,5},{5,4},{6,7},{7,6},{8,9},{9,8},{10,11... | collective-permute-start | bytes 1572872 | tf_op jit(solution)/shard_map/ppermute | solution.py:306
  96.4 4.5 %collective-permute-start.2 = (bf16[512,512]{1,0:T(8,128)(2,1)S(1)}, bf16[512,512]{1,0:T(8,128)(2,1)S(1)}, u32[]{:S(2)}, u32[]{:S(2)}) collective-permute-start(bf16[512,512]{1,0:T(8,128)(2,1)S(1)} %collective-permute-done.1.refs_2_), channel_id=1, source_target_pairs={{0,1},{1,0},{2,3},{3,2},{4,5},{5,4},{6,7},{7,6},{8,9},{9,8},{10,11... | collective-permute-start | bytes 1572872 | tf_op jit(solution)/shard_map/ppermute | solution.py:306
  98.4 4.1 %copy-start.10 = (bf16[512,512]{1,0:T(8,128)(2,1)}, bf16[512,512]{1,0:T(8,128)(2,1)S(1)}, u32[]{:S(2)}) copy-start(bf16[512,512]{1,0:T(8,128)(2,1)S(1)} %constant_dynamic-update-slice_fusion.refs_6_) | copy-start | bytes 1572868
  98.4 4.1 %collective-permute-start.7 = (bf16[512,512]{1,0:T(8,128)(2,1)S(1)}, bf16[512,512]{1,0:T(8,128)(2,1)}, u32[]{:S(2)}, u32[]{:S(2)}) collective-permute-start(bf16[512,512]{1,0:T(8,128)(2,1)S(1)} %constant_dynamic-update-slice_fusion.refs_6_), channel_id=1, source_target_pairs={{0,1},{1,0},{2,3},{3,2},{4,5},{5,4},{6,7},{7,6},{8,9},{9,8},{10,11... | collective-permute-start | bytes 1572872 | tf_op jit(solution)/shard_map/ppermute | solution.py:306
  100.9 0.8 copy-start.11
  101.7 0.8 copy-start.12
Sparse Core Ops, SparseCore 0:
  41.3 55.9 all-gather.2

commit v7 on v6

--- a/solution.py
+++ b/solution.py
@@ -162,22 +162,10 @@
             out_ref[rows, span] = dot(weighted, value_ref[seen, span]).astype(jnp.bfloat16)
 
 
-def finish_kernel(
-    across_in, memory_in, gain_in, query_in, local_in, out_ref,
-    across_ref, memory_ref, gain_ref, query_ref, local_ref, sems,
-):
-    copies = fetch(
-        (across_in, memory_in, gain_in, query_in, local_in),
-        (across_ref, memory_ref, gain_ref, query_ref, local_ref),
-        sems,
-    )
-    for copy in copies[:3]:
-        copy.wait()
+def finish_kernel(across_ref, memory_ref, gain_ref, query_ref, local_ref, out_ref):
     across = across_ref[...]
     prior = memory_ref[0, SLICE : SLICE + 16, :].astype(jnp.float32)[0:1, 0:1]
     reach = jnp.transpose(jnp.where(across[HEADS : HEADS + 1, :] == prior, jnp.exp(across), 0.0))
-    for copy in copies[3:]:
-        copy.wait()
     for h in range(HEADS):
         span = slice(h * HD, (h + 1) * HD)
         memory = jnp.concatenate([memory_ref[2 * h, 0:SLICE, :], memory_ref[2 * h + 1, 0:SLICE, :]], axis=0)
@@ -280,15 +268,8 @@
         finish_kernel,
         shape(*queries.shape),
         (across, entering, gains, queries, alone),
-        [ANY] * 5,
-        [
-            pltpu.VMEM(across.shape, jnp.float32),
-            pltpu.VMEM(entering.shape, jnp.bfloat16),
-            pltpu.VMEM(gains.shape, jnp.float32),
-            wide,
-            wide,
-            pltpu.SemaphoreType.DMA((5,)),
-        ],
+        [VMEM] * 5,
+        [],
         10**8,
         0,
         32,

time: 115 us -> 114 us (level)
  no operation moved by 1% of the time
where the time goes in v7:
time: 114 us
  blocking collectives  45.3 us (40%)
  starting transfers between devices  34.1 us (30%)
  between operations  13.7 us (12%)
  Pallas kernels  13.3 us (12%)
  waiting for transfers between devices  5.8 us (5%)
  local copies, waits for them, and re-layouts  1.67 us (1%)
    all_to_all x1, blocking collectives, local(): states = lax.all_to_all(states, 'z', 0, 0, tiled=True)  30.3 us
    all_to_all x1, blocking collectives, local(): rows = lax.all_to_all(rows, 'y', 0, 0, tiled=True)  15 us
    pallas_call x7, Pallas kernels, call(): pl.pallas_call(kernel, out_shape=out_shape, in_specs=specs, out_specs=jax...  13.3 us
    ppermute x3, starting transfers between devices, local(): cross = lambda block: lax.ppermute(block, 'c', [(0, 1), (1, 0)])  10.1 us
    ppermute x1, starting transfers between devices, local(): crossed = lax.ppermute(normed, 'c', [(0, 1), (1, 0)])  7.61 us
    all_to_all x1, waiting for transfers between devices, local(): entering = lax.all_to_all(entering, 'z', 0, 0, tiled=True)  5.72 us
    ppermute x1, starting transfers between devices, local(): far_two = lax.ppermute(last, 'x', left)  4.57 us
    all_to_all x1, starting transfers between devices, local(): entering = lax.all_to_all(entering, 'z', 0, 0, tiled=True)  3.38 us
  transfers between devices with their start and end apart: 10, of which 1 were waited for; matrix products, arithmetic and copies ran while one was open for 0% of the time, Pallas kernels for 4%

profile of v7, /device:TPU:1, one launch (start us, length us, event | category | flops | bytes accessed | tf_op | source)
XLA Modules:
  0.0 113.9 jit_solution(9661081610700174292)
XLA Ops:
  6.6 0.0 all-gather.3.cloned.1.call-start
  6.6 3.4 %shard_map.74 = bf16[8,336,128]{2,1,0:T(8,128)(2,1)} custom-call(f32[4,512]{1,0:T(4,128)} %log_in.3, s32[1,512]{1,0:T(1,128)} %bitcast.4, bf16[512,512]{1,0:T(8,128)(2,1)} %key_in.3, bf16[512,512]{1,0:T(8,128)(2,1)} %value_in.3, bf16[64,512]{1,0:T(8,128)(2,1)} %weight_in.1), custom_call_target="tpu_custom_call" | custom-call | flops 100000000 | bytes 1048576 | tf_op jit(solution)/shard_map/pallas_call | solution.py:215
  10.0 30.3 %all_to_all.15.states_ref = bf16[8,336,128]{2,1,0:T(8,128)(2,1)S(1)} all-to-all(bf16[8,336,128]{2,1,0:T(8,128)(2,1)} %shard_map.74), channel_id=1, replica_groups=mesh['y'=8,'z'=8,'x'=4,'c'=2] {'z'}, dimensions={0} | all-to-all | bytes 1376256 | tf_op jit(solution)/shard_map/all_to_all | solution.py:245
  40.3 0.8 shard_map.75
  41.2 0.0 all-gather.3.cloned.1.call-update
  41.2 15.0 %all_to_all.16.rows_ref = bf16[8,80,128]{2,1,0:T(8,128)(2,1)S(1)} all-to-all(bf16[8,80,128]{2,1,0:T(8,128)(2,1)S(1)} %get-tuple-element.10), channel_id=1, replica_groups=mesh['y'=8,'z'=8,'x'=4,'c'=2] {'y'}, dimensions={0} | all-to-all | bytes 327680 | tf_op jit(solution)/shard_map/all_to_all | solution.py:250
  56.2 0.8 shard_map.76
  57.0 3.4 %all-to-all-start.2 = ((bf16[8,80,128]{2,1,0:T(8,128)(2,1)}), bf16[8,80,128]{2,1,0:T(8,128)(2,1)S(1)}, u32[]{:S(2)}, u32[]{:S(2)}) async-start(bf16[8,80,128]{2,1,0:T(8,128)(2,1)} %shard_map.76), calls=%async_computation.2 | async-start | bytes 327680 | tf_op jit(solution)/shard_map/all_to_all | solution.py:254
  60.4 2.4 %shard_map.73 = (bf16[512,512]{1,0:T(8,128)(2,1)S(1)}, f32[8,512]{1,0:T(8,128)S(1)}) custom-call(f32[4,512]{1,0:T(4,128)S(1)} %copy-done.6, s32[1,512]{1,0:T(1,128)S(1)} %bitcast.5, bf16[512,512]{1,0:T(8,128)(2,1)S(1)} %copy-done.5, bf16[512,512]{1,0:T(8,128)(2,1)S(1)} %copy-done.3, bf16[512,512]{1,0:T(8,128)(2,1)S(1)} %copy-done.4), custom_call_target="tpu_custom_call" | custom-call | flops 600000000 | bytes 1048576 | tf_op jit(solution)/shard_map/pallas_call | solution.py:215
  62.8 5.7 %all-to-all-done.2.memory_ref = bf16[8,80,128]{2,1,0:T(8,128)(2,1)S(1)} async-done(((bf16[8,80,128]{2,1,0:T(8,128)(2,1)}), bf16[8,80,128]{2,1,0:T(8,128)(2,1)S(1)}, u32[]{:S(2)}, u32[]{:S(2)}) %all-to-all-start.2) | async-done | bytes 163872 | tf_op jit(solution)/shard_map/all_to_all | solution.py:254
  68.5 1.0 shard_map.77.refs_0_
  69.6 3.1 %collective-permute-start.1 = (bf16[512,512]{1,0:T(8,128)(2,1)S(1)}, bf16[512,512]{1,0:T(8,128)(2,1)S(1)}, u32[]{:S(2)}, u32[]{:S(2)}) collective-permute-start(bf16[512,512]{1,0:T(8,128)(2,1)S(1)} %shard_map.77.refs_0_), channel_id=1, source_target_pairs={{0,2},{2,4},{4,6},{6,0},{1,3},{3,5},{5,7},{7,1},{8,10},{10,12},{12... | collective-permute-start | bytes 1572872 | tf_op jit(solution)/shard_map/ppermute | solution.py:280
  72.7 3.4 %collective-permute-start.3 = (bf16[512,512]{1,0:T(8,128)(2,1)S(1)}, bf16[512,512]{1,0:T(8,128)(2,1)S(1)}, u32[]{:S(2)}, u32[]{:S(2)}) collective-permute-start(bf16[512,512]{1,0:T(8,128)(2,1)S(1)} %shard_map.77.refs_0_), channel_id=1, source_target_pairs={{0,6},{2,0},{4,2},{6,4},{1,7},{3,1},{5,3},{7,5},{8,14},{10,8},{12,... | collective-permute-start | bytes 1572872 | tf_op jit(solution)/shard_map/ppermute | solution.py:281
  76.1 7.6 %collective-permute-start = (bf16[512,512]{1,0:T(8,128)(2,1)S(1)}, bf16[512,512]{1,0:T(8,128)(2,1)S(1)}, u32[]{:S(2)}, u32[]{:S(2)}) collective-permute-start(bf16[512,512]{1,0:T(8,128)(2,1)S(1)} %shard_map.77.refs_0_), channel_id=1, source_target_pairs={{0,1},{1,0},{2,3},{3,2},{4,5},{5,4},{6,7},{7,6},{8,9},{9,8},{10,11... | collective-permute-start | bytes 1572872 | tf_op jit(solution)/shard_map/ppermute | solution.py:283
  83.7 0.0 collective-permute-done.1.refs_2_
  83.7 1.9 %collective-permute-start.5 = (bf16[256,512]{1,0:T(8,128)(2,1)S(1)}, bf16[256,512]{1,0:T(8,128)(2,1)S(1)}, u32[]{:S(2)}, u32[]{:S(2)}) collective-permute-start(bf16[256,512]{1,0:T(8,128)(2,1)S(1)} %slice.4), channel_id=1, source_target_pairs={{0,2},{2,4},{4,6},{6,0},{1,3},{3,5},{5,7},{7,1},{8,10},{10,12},{12... | collective-permute-start | bytes 786440 | tf_op jit(solution)/shard_map/ppermute | solution.py:285
  85.7 4.6 %collective-permute-start.6 = (bf16[256,512]{1,0:T(8,128)(2,1)S(1)}, bf16[256,512]{1,0:T(8,128)(2,1)S(1)}, u32[]{:S(2)}, u32[]{:S(2)}) collective-permute-start(bf16[256,512]{1,0:T(8,128)(2,1)S(1)} %shard_map.78), channel_id=1, source_target_pairs={{0,6},{2,0},{4,2},{6,4},{1,7},{3,1},{5,3},{7,5},{8,14},{10,8},{12,... | collective-permute-start | bytes 786440 | tf_op jit(solution)/shard_map/ppermute | solution.py:286
  90.3 5.8 %collective-permute-start.4 = (bf16[512,512]{1,0:T(8,128)(2,1)S(1)}, bf16[512,512]{1,0:T(8,128)(2,1)S(1)}, u32[]{:S(2)}, u32[]{:S(2)}) collective-permute-start(bf16[512,512]{1,0:T(8,128)(2,1)S(1)} %collective-permute-done.3.block_ref.refs_4_), channel_id=1, source_target_pairs={{0,1},{1,0},{2,3},{3,2},{4,5},{5,4},{6,7},{7,6},{8,9},{9,8},{10,11... | collective-permute-start | bytes 1572872 | tf_op jit(solution)/shard_map/ppermute | solution.py:287
  96.1 1.9 %collective-permute-start.2 = (bf16[512,512]{1,0:T(8,128)(2,1)S(1)}, bf16[512,512]{1,0:T(8,128)(2,1)S(1)}, u32[]{:S(2)}, u32[]{:S(2)}) collective-permute-start(bf16[512,512]{1,0:T(8,128)(2,1)S(1)} %collective-permute-done.1.refs_2_), channel_id=1, source_target_pairs={{0,1},{1,0},{2,3},{3,2},{4,5},{5,4},{6,7},{7,6},{8,9},{9,8},{10,11... | collective-permute-start | bytes 1572872 | tf_op jit(solution)/shard_map/ppermute | solution.py:287
  98.1 2.4 %collective-permute-start.7 = (bf16[512,512]{1,0:T(8,128)(2,1)S(1)}, bf16[512,512]{1,0:T(8,128)(2,1)}, u32[]{:S(2)}, u32[]{:S(2)}) collective-permute-start(bf16[512,512]{1,0:T(8,128)(2,1)S(1)} %constant_dynamic-update-slice_fusion.refs_6_), channel_id=1, source_target_pairs={{0,1},{1,0},{2,3},{3,2},{4,5},{5,4},{6,7},{7,6},{8,9},{9,8},{10,11... | collective-permute-start | bytes 1572872 | tf_op jit(solution)/shard_map/ppermute | solution.py:287
  100.5 0.8 copy-done.11
  101.3 0.8 copy-done.12
  102.1 0.0 collective-permute-done.7.refs_7_
  102.2 4.9 %shard_map.79 = bf16[512,512]{1,0:T(8,128)(2,1)} custom-call(bf16[512,512]{1,0:T(8,128)(2,1)} %copy-done.2, bf16[512,512]{1,0:T(8,128)(2,1)} %copy-done.1, bf16[512,512]{1,0:T(8,128)(2,1)} %copy-done.9, bf16[512,512]{1,0:T(8,128)(2,1)} %copy-done.12, bf16[512,512]{1,0:T(8,128)(2,1)} %copy-done, bf16[512,512]{1,0:T(8,128)(2,1)} %copy-done.11, ...), custom_call_target="tpu_custom_call" | custom-call | flops 2000000000 | bytes 1048576 | tf_op jit(solution)/shard_map/pallas_call | solution.py:215
  (35 shorter events, 0.1 us)
Async XLA Ops:
  6.5 53.8 %copy-start.6 = (f32[4,512]{1,0:T(4,128)S(1)}, f32[4,512]{1,0:T(4,128)}, u32[]{:S(2)}) copy-start(f32[4,512]{1,0:T(4,128)} %log_in.3) | copy-start | bytes 24580
  6.5 53.8 %copy-start.4 = (bf16[512,512]{1,0:T(8,128)(2,1)S(1)}, bf16[512,512]{1,0:T(8,128)(2,1)}, u32[]{:S(2)}) copy-start(bf16[512,512]{1,0:T(8,128)(2,1)} %value_in.3) | copy-start | bytes 1572868
  6.5 53.8 %copy-start.3 = (bf16[512,512]{1,0:T(8,128)(2,1)S(1)}, bf16[512,512]{1,0:T(8,128)(2,1)}, u32[]{:S(2)}) copy-start(bf16[512,512]{1,0:T(8,128)(2,1)} %key_in.3) | copy-start | bytes 1572868
  6.5 53.8 %copy-start.8 = (s32[512]{0:T(512)S(1)}, s32[512]{0:T(512)}, u32[]{:S(2)}) copy-start(s32[512]{0:T(512)} %param.11) | copy-start | bytes 6148
  6.5 53.8 %copy-start.5 = (bf16[512,512]{1,0:T(8,128)(2,1)S(1)}, bf16[512,512]{1,0:T(8,128)(2,1)}, u32[]{:S(2)}) copy-start(bf16[512,512]{1,0:T(8,128)(2,1)} %query_ref.1) | copy-start | bytes 1572868
  6.5 62.0 %copy-start.7 = (f32[512]{0:T(512)S(1)}, f32[512]{0:T(512)}, u32[]{:S(2)}) copy-start(f32[512]{0:T(512)} %param.12) | copy-start | bytes 6148
  6.6 95.6 %all-gather.3.cloned.1.call-start = ((), (), s32[]{:S(2)}) async-start(), calls=%async_computation.3 | async-start | bytes 4718592 | tf_op jit(solution)/shard_map/all_gather | solution.py:249
  57.0 11.6 %all-to-all-start.2 = ((bf16[8,80,128]{2,1,0:T(8,128)(2,1)}), bf16[8,80,128]{2,1,0:T(8,128)(2,1)S(1)}, u32[]{:S(2)}, u32[]{:S(2)}) async-start(bf16[8,80,128]{2,1,0:T(8,128)(2,1)} %shard_map.76), calls=%async_computation.2 | async-start | bytes 327680 | tf_op jit(solution)/shard_map/all_to_all | solution.py:254
  69.6 32.6 %copy-start.2 = (bf16[512,512]{1,0:T(8,128)(2,1)}, bf16[512,512]{1,0:T(8,128)(2,1)S(1)}, u32[]{:S(2)}) copy-start(bf16[512,512]{1,0:T(8,128)(2,1)S(1)} %shard_map.77.refs_0_) | copy-start | bytes 1572868
  69.6 14.1 %collective-permute-start.1 = (bf16[512,512]{1,0:T(8,128)(2,1)S(1)}, bf16[512,512]{1,0:T(8,128)(2,1)S(1)}, u32[]{:S(2)}, u32[]{:S(2)}) collective-permute-start(bf16[512,512]{1,0:T(8,128)(2,1)S(1)} %shard_map.77.refs_0_), channel_id=1, source_target_pairs={{0,2},{2,4},{4,6},{6,0},{1,3},{3,5},{5,7},{7,1},{8,10},{10,12},{12... | collective-permute-start | bytes 1572872 | tf_op jit(solution)/shard_map/ppermute | solution.py:280
  72.7 13.0 %collective-permute-start.3 = (bf16[512,512]{1,0:T(8,128)(2,1)S(1)}, bf16[512,512]{1,0:T(8,128)(2,1)S(1)}, u32[]{:S(2)}, u32[]{:S(2)}) collective-permute-start(bf16[512,512]{1,0:T(8,128)(2,1)S(1)} %shard_map.77.refs_0_), channel_id=1, source_target_pairs={{0,6},{2,0},{4,2},{6,4},{1,7},{3,1},{5,3},{7,5},{8,14},{10,8},{12,... | collective-permute-start | bytes 1572872 | tf_op jit(solution)/shard_map/ppermute | solution.py:281
  76.1 9.6 %collective-permute-start = (bf16[512,512]{1,0:T(8,128)(2,1)S(1)}, bf16[512,512]{1,0:T(8,128)(2,1)S(1)}, u32[]{:S(2)}, u32[]{:S(2)}) collective-permute-start(bf16[512,512]{1,0:T(8,128)(2,1)S(1)} %shard_map.77.refs_0_), channel_id=1, source_target_pairs={{0,1},{1,0},{2,3},{3,2},{4,5},{5,4},{6,7},{7,6},{8,9},{9,8},{10,11... | collective-permute-start | bytes 1572872 | tf_op jit(solution)/shard_map/ppermute | solution.py:283
  83.7 18.5 %copy-start.9 = (bf16[512,512]{1,0:T(8,128)(2,1)}, bf16[512,512]{1,0:T(8,128)(2,1)S(1)}, u32[]{:S(2)}) copy-start(bf16[512,512]{1,0:T(8,128)(2,1)S(1)} %collective-permute-done.1.refs_2_) | copy-start | bytes 1572868
  83.7 14.3 %collective-permute-start.5 = (bf16[256,512]{1,0:T(8,128)(2,1)S(1)}, bf16[256,512]{1,0:T(8,128)(2,1)S(1)}, u32[]{:S(2)}, u32[]{:S(2)}) collective-permute-start(bf16[256,512]{1,0:T(8,128)(2,1)S(1)} %slice.4), channel_id=1, source_target_pairs={{0,2},{2,4},{4,6},{6,0},{1,3},{3,5},{5,7},{7,1},{8,10},{10,12},{12... | collective-permute-start | bytes 786440 | tf_op jit(solution)/shard_map/ppermute | solution.py:285
  85.7 16.5 %copy-start = (bf16[512,512]{1,0:T(8,128)(2,1)}, bf16[512,512]{1,0:T(8,128)(2,1)S(1)}, u32[]{:S(2)}) copy-start(bf16[512,512]{1,0:T(8,128)(2,1)S(1)} %collective-permute-done.3.block_ref.refs_4_) | copy-start | bytes 1572868
  85.7 16.5 %copy-start.1 = (bf16[512,512]{1,0:T(8,128)(2,1)}, bf16[512,512]{1,0:T(8,128)(2,1)S(1)}, u32[]{:S(2)}) copy-start(bf16[512,512]{1,0:T(8,128)(2,1)S(1)} %collective-permute-done.crossed_ref.refs_1_) | copy-start | bytes 1572868
  85.7 12.3 %collective-permute-start.6 = (bf16[256,512]{1,0:T(8,128)(2,1)S(1)}, bf16[256,512]{1,0:T(8,128)(2,1)S(1)}, u32[]{:S(2)}, u32[]{:S(2)}) collective-permute-start(bf16[256,512]{1,0:T(8,128)(2,1)S(1)} %shard_map.78), channel_id=1, source_target_pairs={{0,6},{2,0},{4,2},{6,4},{1,7},{3,1},{5,3},{7,5},{8,14},{10,8},{12,... | collective-permute-start | bytes 786440 | tf_op jit(solution)/shard_map/ppermute | solution.py:286
  90.3 10.2 %collective-permute-start.4 = (bf16[512,512]{1,0:T(8,128)(2,1)S(1)}, bf16[512,512]{1,0:T(8,128)(2,1)S(1)}, u32[]{:S(2)}, u32[]{:S(2)}) collective-permute-start(bf16[512,512]{1,0:T(8,128)(2,1)S(1)} %collective-permute-done.3.block_ref.refs_4_), channel_id=1, source_target_pairs={{0,1},{1,0},{2,3},{3,2},{4,5},{5,4},{6,7},{7,6},{8,9},{9,8},{10,11... | collective-permute-start | bytes 1572872 | tf_op jit(solution)/shard_map/ppermute | solution.py:287
  96.1 4.5 %collective-permute-start.2 = (bf16[512,512]{1,0:T(8,128)(2,1)S(1)}, bf16[512,512]{1,0:T(8,128)(2,1)S(1)}, u32[]{:S(2)}, u32[]{:S(2)}) collective-permute-start(bf16[512,512]{1,0:T(8,128)(2,1)S(1)} %collective-permute-done.1.refs_2_), channel_id=1, source_target_pairs={{0,1},{1,0},{2,3},{3,2},{4,5},{5,4},{6,7},{7,6},{8,9},{9,8},{10,11... | collective-permute-start | bytes 1572872 | tf_op jit(solution)/shard_map/ppermute | solution.py:287
  98.1 4.1 %copy-start.10 = (bf16[512,512]{1,0:T(8,128)(2,1)}, bf16[512,512]{1,0:T(8,128)(2,1)S(1)}, u32[]{:S(2)}) copy-start(bf16[512,512]{1,0:T(8,128)(2,1)S(1)} %constant_dynamic-update-slice_fusion.refs_6_) | copy-start | bytes 1572868
  98.1 4.1 %collective-permute-start.7 = (bf16[512,512]{1,0:T(8,128)(2,1)S(1)}, bf16[512,512]{1,0:T(8,128)(2,1)}, u32[]{:S(2)}, u32[]{:S(2)}) collective-permute-start(bf16[512,512]{1,0:T(8,128)(2,1)S(1)} %constant_dynamic-update-slice_fusion.refs_6_), channel_id=1, source_target_pairs={{0,1},{1,0},{2,3},{3,2},{4,5},{5,4},{6,7},{7,6},{8,9},{9,8},{10,11... | collective-permute-start | bytes 1572872 | tf_op jit(solution)/shard_map/ppermute | solution.py:287
  100.5 0.8 copy-start.11
  101.3 0.8 copy-start.12
Sparse Core Ops, SparseCore 0:
  41.3 55.9 all-gather.2

commit v8 on v7

--- a/solution.py
+++ b/solution.py
@@ -93,7 +93,8 @@
             out_ref[k, ROWS + 64 * j : ROWS + 64 * (j + 1), :] = weight[:, j * HD : (j + 1) * HD]
 
 
-def row_kernel(states_ref, out_ref, weight_ref):
+def row_kernel(states_ref, out_ref, weight_out, sems):
+    (copy,) = fetch([states_ref.at[:, ROWS:FULL]], [weight_out], sems)
     total = jnp.zeros((SLICE, HD), jnp.float32)
     logs = jnp.zeros((1, HD), jnp.float32)
     prior = None
@@ -107,7 +108,7 @@
     for k in range(RING):
         out_ref[k, 0:SLICE, :] = total.astype(jnp.bfloat16)
         out_ref[k, SLICE:ROWS, :] = meta_of(logs, prior)
-    weight_ref[...] = states_ref[:, ROWS:FULL, :]
+    copy.wait()
 
 
 def enter_kernel(states_ref, rows_ref, out_ref):
@@ -211,12 +212,12 @@
                 out_ref[rows, :] = (total[rows] + product).astype(jnp.bfloat16)
 
 
-def call(kernel, out_shape, args, specs, scratch=(), flops=0, transcendentals=0, grant=16):
+def call(kernel, out_shape, args, specs, scratch=(), flops=0, transcendentals=0, grant=16, outs=None):
     return pl.pallas_call(
         kernel,
         out_shape=out_shape,
         in_specs=specs,
-        out_specs=jax.tree.map(lambda _: VMEM, out_shape),
+        out_specs=outs or jax.tree.map(lambda _: VMEM, out_shape),
         scratch_shapes=list(scratch),
         compiler_params=pltpu.CompilerParams(vmem_limit_bytes=grant * 2**20),
         cost_estimate=pl.CostEstimate(flops=flops, bytes_accessed=2**20, transcendentals=transcendentals),
@@ -244,7 +245,12 @@
     )
     states = lax.all_to_all(states, "z", 0, 0, tiled=True)
     rows, weight = call(
-        row_kernel, (shape(RING, ROWS, HD), shape(RING, 256, HD)), (states,), [VMEM]
+        row_kernel,
+        (shape(RING, ROWS, HD), shape(RING, 256, HD)),
+        (states,),
+        [VMEM],
+        [pltpu.SemaphoreType.DMA((1,))],
+        outs=[VMEM, ANY],
     )
     weight = lax.all_gather(weight, "y")
     rows = lax.all_to_all(rows, "y", 0, 0, tiled=True)

time: 114 us -> 114 us (level)
  no operation moved by 1% of the time
where the time goes in v8:
time: 114 us
  blocking collectives  45.3 us (40%)
  starting transfers between devices  34.1 us (30%)
  between operations  13.7 us (12%)
  Pallas kernels  13.3 us (12%)
  waiting for transfers between devices  5.8 us (5%)
  local copies, waits for them, and re-layouts  1.67 us (1%)
    all_to_all x1, blocking collectives, local(): states = lax.all_to_all(states, 'z', 0, 0, tiled=True)  30.3 us
    all_to_all x1, blocking collectives, local(): rows = lax.all_to_all(rows, 'y', 0, 0, tiled=True)  15 us
    pallas_call x7, Pallas kernels, call(): pl.pallas_call(kernel, out_shape=out_shape, in_specs=specs, out_specs=out...  13.3 us
    ppermute x3, starting transfers between devices, local(): cross = lambda block: lax.ppermute(block, 'c', [(0, 1), (1, 0)])  10.1 us
    ppermute x1, starting transfers between devices, local(): crossed = lax.ppermute(normed, 'c', [(0, 1), (1, 0)])  7.61 us
    all_to_all x1, waiting for transfers between devices, local(): entering = lax.all_to_all(entering, 'z', 0, 0, tiled=True)  5.72 us
    ppermute x1, starting transfers between devices, local(): far_two = lax.ppermute(last, 'x', left)  4.57 us
    all_to_all x1, starting transfers between devices, local(): entering = lax.all_to_all(entering, 'z', 0, 0, tiled=True)  3.38 us
  transfers between devices with their start and end apart: 10, of which 1 were waited for; matrix products, arithmetic and copies ran while one was open for 0% of the time, Pallas kernels for 4%

profile of v8, /device:TPU:1, one launch (start us, length us, event | category | flops | bytes accessed | tf_op | source)
XLA Modules:
  0.0 113.9 jit_solution(17845399889741994310)
XLA Ops:
  6.6 0.0 all-gather.3.cloned.1.call-start
  6.6 3.4 %shard_map.74 = bf16[8,336,128]{2,1,0:T(8,128)(2,1)} custom-call(f32[4,512]{1,0:T(4,128)} %log_in.3, s32[1,512]{1,0:T(1,128)} %bitcast.4, bf16[512,512]{1,0:T(8,128)(2,1)} %key_in.3, bf16[512,512]{1,0:T(8,128)(2,1)} %value_in.3, bf16[64,512]{1,0:T(8,128)(2,1)} %weight_in.1), custom_call_target="tpu_custom_call" | custom-call | flops 100000000 | bytes 1048576 | tf_op jit(solution)/shard_map/pallas_call | solution.py:216
  10.0 30.3 %all_to_all.15.states_ref = bf16[8,336,128]{2,1,0:T(8,128)(2,1)S(1)} all-to-all(bf16[8,336,128]{2,1,0:T(8,128)(2,1)} %shard_map.74), channel_id=1, replica_groups=mesh['y'=8,'z'=8,'x'=4,'c'=2] {'z'}, dimensions={0} | all-to-all | bytes 1376256 | tf_op jit(solution)/shard_map/all_to_all | solution.py:246
  40.3 0.8 shard_map.75
  41.2 0.0 all-gather.3.cloned.1.call-update
  41.2 15.0 %all_to_all.16.rows_ref = bf16[8,80,128]{2,1,0:T(8,128)(2,1)S(1)} all-to-all(bf16[8,80,128]{2,1,0:T(8,128)(2,1)S(1)} %get-tuple-element.10), channel_id=1, replica_groups=mesh['y'=8,'z'=8,'x'=4,'c'=2] {'y'}, dimensions={0} | all-to-all | bytes 327680 | tf_op jit(solution)/shard_map/all_to_all | solution.py:256
  56.2 0.8 shard_map.76
  56.9 3.4 %all-to-all-start.2 = ((bf16[8,80,128]{2,1,0:T(8,128)(2,1)}), bf16[8,80,128]{2,1,0:T(8,128)(2,1)S(1)}, u32[]{:S(2)}, u32[]{:S(2)}) async-start(bf16[8,80,128]{2,1,0:T(8,128)(2,1)} %shard_map.76), calls=%async_computation.2 | async-start | bytes 327680 | tf_op jit(solution)/shard_map/all_to_all | solution.py:260
  60.4 2.4 %shard_map.73 = (bf16[512,512]{1,0:T(8,128)(2,1)S(1)}, f32[8,512]{1,0:T(8,128)S(1)}) custom-call(f32[4,512]{1,0:T(4,128)S(1)} %copy-done.6, s32[1,512]{1,0:T(1,128)S(1)} %bitcast.5, bf16[512,512]{1,0:T(8,128)(2,1)S(1)} %copy-done.5, bf16[512,512]{1,0:T(8,128)(2,1)S(1)} %copy-done.3, bf16[512,512]{1,0:T(8,128)(2,1)S(1)} %copy-done.4), custom_call_target="tpu_custom_call" | custom-call | flops 600000000 | bytes 1048576 | tf_op jit(solution)/shard_map/pallas_call | solution.py:216
  62.8 5.7 %all-to-all-done.2.memory_ref = bf16[8,80,128]{2,1,0:T(8,128)(2,1)S(1)} async-done(((bf16[8,80,128]{2,1,0:T(8,128)(2,1)}), bf16[8,80,128]{2,1,0:T(8,128)(2,1)S(1)}, u32[]{:S(2)}, u32[]{:S(2)}) %all-to-all-start.2) | async-done | bytes 163872 | tf_op jit(solution)/shard_map/all_to_all | solution.py:260
  68.5 1.0 shard_map.77.refs_0_
  69.5 3.1 %collective-permute-start.1 = (bf16[512,512]{1,0:T(8,128)(2,1)S(1)}, bf16[512,512]{1,0:T(8,128)(2,1)S(1)}, u32[]{:S(2)}, u32[]{:S(2)}) collective-permute-start(bf16[512,512]{1,0:T(8,128)(2,1)S(1)} %shard_map.77.refs_0_), channel_id=1, source_target_pairs={{0,2},{2,4},{4,6},{6,0},{1,3},{3,5},{5,7},{7,1},{8,10},{10,12},{12... | collective-permute-start | bytes 1572872 | tf_op jit(solution)/shard_map/ppermute | solution.py:286
  72.7 3.4 %collective-permute-start.3 = (bf16[512,512]{1,0:T(8,128)(2,1)S(1)}, bf16[512,512]{1,0:T(8,128)(2,1)S(1)}, u32[]{:S(2)}, u32[]{:S(2)}) collective-permute-start(bf16[512,512]{1,0:T(8,128)(2,1)S(1)} %shard_map.77.refs_0_), channel_id=1, source_target_pairs={{0,6},{2,0},{4,2},{6,4},{1,7},{3,1},{5,3},{7,5},{8,14},{10,8},{12,... | collective-permute-start | bytes 1572872 | tf_op jit(solution)/shard_map/ppermute | solution.py:287
  76.0 7.6 %collective-permute-start = (bf16[512,512]{1,0:T(8,128)(2,1)S(1)}, bf16[512,512]{1,0:T(8,128)(2,1)S(1)}, u32[]{:S(2)}, u32[]{:S(2)}) collective-permute-start(bf16[512,512]{1,0:T(8,128)(2,1)S(1)} %shard_map.77.refs_0_), channel_id=1, source_target_pairs={{0,1},{1,0},{2,3},{3,2},{4,5},{5,4},{6,7},{7,6},{8,9},{9,8},{10,11... | collective-permute-start | bytes 1572872 | tf_op jit(solution)/shard_map/ppermute | solution.py:289
  83.7 0.0 collective-permute-done.1.refs_2_
  83.7 1.9 %collective-permute-start.5 = (bf16[256,512]{1,0:T(8,128)(2,1)S(1)}, bf16[256,512]{1,0:T(8,128)(2,1)S(1)}, u32[]{:S(2)}, u32[]{:S(2)}) collective-permute-start(bf16[256,512]{1,0:T(8,128)(2,1)S(1)} %slice.4), channel_id=1, source_target_pairs={{0,2},{2,4},{4,6},{6,0},{1,3},{3,5},{5,7},{7,1},{8,10},{10,12},{12... | collective-permute-start | bytes 786440 | tf_op jit(solution)/shard_map/ppermute | solution.py:291
  85.7 4.6 %collective-permute-start.6 = (bf16[256,512]{1,0:T(8,128)(2,1)S(1)}, bf16[256,512]{1,0:T(8,128)(2,1)S(1)}, u32[]{:S(2)}, u32[]{:S(2)}) collective-permute-start(bf16[256,512]{1,0:T(8,128)(2,1)S(1)} %shard_map.78), channel_id=1, source_target_pairs={{0,6},{2,0},{4,2},{6,4},{1,7},{3,1},{5,3},{7,5},{8,14},{10,8},{12,... | collective-permute-start | bytes 786440 | tf_op jit(solution)/shard_map/ppermute | solution.py:292
  90.3 5.8 %collective-permute-start.4 = (bf16[512,512]{1,0:T(8,128)(2,1)S(1)}, bf16[512,512]{1,0:T(8,128)(2,1)S(1)}, u32[]{:S(2)}, u32[]{:S(2)}) collective-permute-start(bf16[512,512]{1,0:T(8,128)(2,1)S(1)} %collective-permute-done.3.block_ref.refs_4_), channel_id=1, source_target_pairs={{0,1},{1,0},{2,3},{3,2},{4,5},{5,4},{6,7},{7,6},{8,9},{9,8},{10,11... | collective-permute-start | bytes 1572872 | tf_op jit(solution)/shard_map/ppermute | solution.py:293
  96.1 1.9 %collective-permute-start.2 = (bf16[512,512]{1,0:T(8,128)(2,1)S(1)}, bf16[512,512]{1,0:T(8,128)(2,1)S(1)}, u32[]{:S(2)}, u32[]{:S(2)}) collective-permute-start(bf16[512,512]{1,0:T(8,128)(2,1)S(1)} %collective-permute-done.1.refs_2_), channel_id=1, source_target_pairs={{0,1},{1,0},{2,3},{3,2},{4,5},{5,4},{6,7},{7,6},{8,9},{9,8},{10,11... | collective-permute-start | bytes 1572872 | tf_op jit(solution)/shard_map/ppermute | solution.py:293
  98.1 2.4 %collective-permute-start.7 = (bf16[512,512]{1,0:T(8,128)(2,1)S(1)}, bf16[512,512]{1,0:T(8,128)(2,1)}, u32[]{:S(2)}, u32[]{:S(2)}) collective-permute-start(bf16[512,512]{1,0:T(8,128)(2,1)S(1)} %constant_dynamic-update-slice_fusion.refs_6_), channel_id=1, source_target_pairs={{0,1},{1,0},{2,3},{3,2},{4,5},{5,4},{6,7},{7,6},{8,9},{9,8},{10,11... | collective-permute-start | bytes 1572872 | tf_op jit(solution)/shard_map/ppermute | solution.py:293
  100.5 0.8 copy-done.11
  101.3 0.8 copy-done.12
  102.1 0.0 collective-permute-done.7.refs_7_
  102.2 4.9 %shard_map.79 = bf16[512,512]{1,0:T(8,128)(2,1)} custom-call(bf16[512,512]{1,0:T(8,128)(2,1)} %copy-done.2, bf16[512,512]{1,0:T(8,128)(2,1)} %copy-done.1, bf16[512,512]{1,0:T(8,128)(2,1)} %copy-done.9, bf16[512,512]{1,0:T(8,128)(2,1)} %copy-done.12, bf16[512,512]{1,0:T(8,128)(2,1)} %copy-done, bf16[512,512]{1,0:T(8,128)(2,1)} %copy-done.11, ...), custom_call_target="tpu_custom_call" | custom-call | flops 2000000000 | bytes 1048576 | tf_op jit(solution)/shard_map/pallas_call | solution.py:216
  (35 shorter events, 0.1 us)
Async XLA Ops:
  6.5 53.8 %copy-start.6 = (f32[4,512]{1,0:T(4,128)S(1)}, f32[4,512]{1,0:T(4,128)}, u32[]{:S(2)}) copy-start(f32[4,512]{1,0:T(4,128)} %log_in.3) | copy-start | bytes 24580
  6.5 53.8 %copy-start.4 = (bf16[512,512]{1,0:T(8,128)(2,1)S(1)}, bf16[512,512]{1,0:T(8,128)(2,1)}, u32[]{:S(2)}) copy-start(bf16[512,512]{1,0:T(8,128)(2,1)} %value_in.3) | copy-start | bytes 1572868
  6.5 53.8 %copy-start.3 = (bf16[512,512]{1,0:T(8,128)(2,1)S(1)}, bf16[512,512]{1,0:T(8,128)(2,1)}, u32[]{:S(2)}) copy-start(bf16[512,512]{1,0:T(8,128)(2,1)} %key_in.3) | copy-start | bytes 1572868
  6.5 53.8 %copy-start.8 = (s32[512]{0:T(512)S(1)}, s32[512]{0:T(512)}, u32[]{:S(2)}) copy-start(s32[512]{0:T(512)} %param.11) | copy-start | bytes 6148
  6.5 53.8 %copy-start.5 = (bf16[512,512]{1,0:T(8,128)(2,1)S(1)}, bf16[512,512]{1,0:T(8,128)(2,1)}, u32[]{:S(2)}) copy-start(bf16[512,512]{1,0:T(8,128)(2,1)} %query_ref.1) | copy-start | bytes 1572868
  6.5 62.0 %copy-start.7 = (f32[512]{0:T(512)S(1)}, f32[512]{0:T(512)}, u32[]{:S(2)}) copy-start(f32[512]{0:T(512)} %param.12) | copy-start | bytes 6148
  6.6 95.6 %all-gather.3.cloned.1.call-start = ((), (), s32[]{:S(2)}) async-start(), calls=%async_computation.3 | async-start | bytes 4718592 | tf_op jit(solution)/shard_map/all_gather | solution.py:255
  56.9 11.6 %all-to-all-start.2 = ((bf16[8,80,128]{2,1,0:T(8,128)(2,1)}), bf16[8,80,128]{2,1,0:T(8,128)(2,1)S(1)}, u32[]{:S(2)}, u32[]{:S(2)}) async-start(bf16[8,80,128]{2,1,0:T(8,128)(2,1)} %shard_map.76), calls=%async_computation.2 | async-start | bytes 327680 | tf_op jit(solution)/shard_map/all_to_all | solution.py:260
  69.5 32.6 %copy-start.2 = (bf16[512,512]{1,0:T(8,128)(2,1)}, bf16[512,512]{1,0:T(8,128)(2,1)S(1)}, u32[]{:S(2)}) copy-start(bf16[512,512]{1,0:T(8,128)(2,1)S(1)} %shard_map.77.refs_0_) | copy-start | bytes 1572868
  69.5 14.1 %collective-permute-start.1 = (bf16[512,512]{1,0:T(8,128)(2,1)S(1)}, bf16[512,512]{1,0:T(8,128)(2,1)S(1)}, u32[]{:S(2)}, u32[]{:S(2)}) collective-permute-start(bf16[512,512]{1,0:T(8,128)(2,1)S(1)} %shard_map.77.refs_0_), channel_id=1, source_target_pairs={{0,2},{2,4},{4,6},{6,0},{1,3},{3,5},{5,7},{7,1},{8,10},{10,12},{12... | collective-permute-start | bytes 1572872 | tf_op jit(solution)/shard_map/ppermute | solution.py:286
  72.7 13.0 %collective-permute-start.3 = (bf16[512,512]{1,0:T(8,128)(2,1)S(1)}, bf16[512,512]{1,0:T(8,128)(2,1)S(1)}, u32[]{:S(2)}, u32[]{:S(2)}) collective-permute-start(bf16[512,512]{1,0:T(8,128)(2,1)S(1)} %shard_map.77.refs_0_), channel_id=1, source_target_pairs={{0,6},{2,0},{4,2},{6,4},{1,7},{3,1},{5,3},{7,5},{8,14},{10,8},{12,... | collective-permute-start | bytes 1572872 | tf_op jit(solution)/shard_map/ppermute | solution.py:287
  76.0 9.6 %collective-permute-start = (bf16[512,512]{1,0:T(8,128)(2,1)S(1)}, bf16[512,512]{1,0:T(8,128)(2,1)S(1)}, u32[]{:S(2)}, u32[]{:S(2)}) collective-permute-start(bf16[512,512]{1,0:T(8,128)(2,1)S(1)} %shard_map.77.refs_0_), channel_id=1, source_target_pairs={{0,1},{1,0},{2,3},{3,2},{4,5},{5,4},{6,7},{7,6},{8,9},{9,8},{10,11... | collective-permute-start | bytes 1572872 | tf_op jit(solution)/shard_map/ppermute | solution.py:289
  83.7 18.5 %copy-start.9 = (bf16[512,512]{1,0:T(8,128)(2,1)}, bf16[512,512]{1,0:T(8,128)(2,1)S(1)}, u32[]{:S(2)}) copy-start(bf16[512,512]{1,0:T(8,128)(2,1)S(1)} %collective-permute-done.1.refs_2_) | copy-start | bytes 1572868
  83.7 14.3 %collective-permute-start.5 = (bf16[256,512]{1,0:T(8,128)(2,1)S(1)}, bf16[256,512]{1,0:T(8,128)(2,1)S(1)}, u32[]{:S(2)}, u32[]{:S(2)}) collective-permute-start(bf16[256,512]{1,0:T(8,128)(2,1)S(1)} %slice.4), channel_id=1, source_target_pairs={{0,2},{2,4},{4,6},{6,0},{1,3},{3,5},{5,7},{7,1},{8,10},{10,12},{12... | collective-permute-start | bytes 786440 | tf_op jit(solution)/shard_map/ppermute | solution.py:291
  85.7 16.5 %copy-start = (bf16[512,512]{1,0:T(8,128)(2,1)}, bf16[512,512]{1,0:T(8,128)(2,1)S(1)}, u32[]{:S(2)}) copy-start(bf16[512,512]{1,0:T(8,128)(2,1)S(1)} %collective-permute-done.3.block_ref.refs_4_) | copy-start | bytes 1572868
  85.7 16.5 %copy-start.1 = (bf16[512,512]{1,0:T(8,128)(2,1)}, bf16[512,512]{1,0:T(8,128)(2,1)S(1)}, u32[]{:S(2)}) copy-start(bf16[512,512]{1,0:T(8,128)(2,1)S(1)} %collective-permute-done.crossed_ref.refs_1_) | copy-start | bytes 1572868
  85.7 12.3 %collective-permute-start.6 = (bf16[256,512]{1,0:T(8,128)(2,1)S(1)}, bf16[256,512]{1,0:T(8,128)(2,1)S(1)}, u32[]{:S(2)}, u32[]{:S(2)}) collective-permute-start(bf16[256,512]{1,0:T(8,128)(2,1)S(1)} %shard_map.78), channel_id=1, source_target_pairs={{0,6},{2,0},{4,2},{6,4},{1,7},{3,1},{5,3},{7,5},{8,14},{10,8},{12,... | collective-permute-start | bytes 786440 | tf_op jit(solution)/shard_map/ppermute | solution.py:292
  90.3 10.2 %collective-permute-start.4 = (bf16[512,512]{1,0:T(8,128)(2,1)S(1)}, bf16[512,512]{1,0:T(8,128)(2,1)S(1)}, u32[]{:S(2)}, u32[]{:S(2)}) collective-permute-start(bf16[512,512]{1,0:T(8,128)(2,1)S(1)} %collective-permute-done.3.block_ref.refs_4_), channel_id=1, source_target_pairs={{0,1},{1,0},{2,3},{3,2},{4,5},{5,4},{6,7},{7,6},{8,9},{9,8},{10,11... | collective-permute-start | bytes 1572872 | tf_op jit(solution)/shard_map/ppermute | solution.py:293
  96.1 4.5 %collective-permute-start.2 = (bf16[512,512]{1,0:T(8,128)(2,1)S(1)}, bf16[512,512]{1,0:T(8,128)(2,1)S(1)}, u32[]{:S(2)}, u32[]{:S(2)}) collective-permute-start(bf16[512,512]{1,0:T(8,128)(2,1)S(1)} %collective-permute-done.1.refs_2_), channel_id=1, source_target_pairs={{0,1},{1,0},{2,3},{3,2},{4,5},{5,4},{6,7},{7,6},{8,9},{9,8},{10,11... | collective-permute-start | bytes 1572872 | tf_op jit(solution)/shard_map/ppermute | solution.py:293
  98.1 4.1 %copy-start.10 = (bf16[512,512]{1,0:T(8,128)(2,1)}, bf16[512,512]{1,0:T(8,128)(2,1)S(1)}, u32[]{:S(2)}) copy-start(bf16[512,512]{1,0:T(8,128)(2,1)S(1)} %constant_dynamic-update-slice_fusion.refs_6_) | copy-start | bytes 1572868
  98.1 4.1 %collective-permute-start.7 = (bf16[512,512]{1,0:T(8,128)(2,1)S(1)}, bf16[512,512]{1,0:T(8,128)(2,1)}, u32[]{:S(2)}, u32[]{:S(2)}) collective-permute-start(bf16[512,512]{1,0:T(8,128)(2,1)S(1)} %constant_dynamic-update-slice_fusion.refs_6_), channel_id=1, source_target_pairs={{0,1},{1,0},{2,3},{3,2},{4,5},{5,4},{6,7},{7,6},{8,9},{9,8},{10,11... | collective-permute-start | bytes 1572872 | tf_op jit(solution)/shard_map/ppermute | solution.py:293
  100.5 0.8 copy-start.11
  101.3 0.8 copy-start.12
Sparse Core Ops, SparseCore 0:
  41.3 55.9 all-gather.2
